TPU v7x, 32 devices: a whole 2x2x4 slice. The times are simulated.
32 devices in a mesh: dp: 8 (over z, y), tensor: 4 (over x, core).
Axes of the slice: x: 2, y: 2, z: 4, core: 2. Of those that a mesh axis runs over, the one named last changes fastest.
Arguments:
- hidden_in: bfloat16 [8192, 1536], P(('dp', 'tensor')), may hold values from -6 to 6
- context: bfloat16 [8, 512, 1536], P('dp', 'tensor'), may hold values from -6 to 6
- time_emb: float32 [8, 6, 1536], P('dp'), may hold values from -3 to 3
- text_lengths: int32 [8], P('dp'), may hold values from 385 to 512, as said below
- positions: int32 [3, 8192], P(None, 'dp'), may hold values from 0 to 31
- modulation: float32 [6, 1536], P(None, 'dp'), may hold values from -3 to 3
- self_query: float32 [1536, 1536], P('dp', 'tensor'), may hold values from -0.15625 to 0.15625
- self_key: float32 [1536, 1536], P('dp', 'tensor'), may hold values from -0.15625 to 0.15625
- self_value: float32 [1536, 1536], P('dp', 'tensor'), may hold values from -0.15625 to 0.15625
- self_output: float32 [1536, 1536], P('tensor', 'dp'), may hold values from -0.625 to 0.625
- self_query_gain: float32 [12, 128], P('tensor', 'dp'), may hold values from 1.3 to 1.7
- self_key_gain: float32 [12, 128], P('tensor', 'dp'), may hold values from 1.3 to 1.7
- cross_query: float32 [1536, 1536], P('dp', 'tensor'), may hold values from -0.15625 to 0.15625
- cross_key: float32 [1536, 1536], P('dp', 'tensor'), may hold values from -0.15625 to 0.15625
- cross_value: float32 [1536, 1536], P('dp', 'tensor'), may hold values from -0.15625 to 0.15625
- cross_output: float32 [1536, 1536], P('tensor', 'dp'), may hold values from -2 to 2
- cross_query_gain: float32 [12, 128], P('tensor', 'dp'), may hold values from 0.25 to 1.75
- cross_key_gain: float32 [12, 128], P('tensor', 'dp'), may hold values from 0.25 to 1.75
- norm_weight: float32 [1536], P('dp'), may hold values from 0.25 to 1.75
- norm_bias: float32 [1536], P('dp'), may hold values from -3 to 3
- ffn_up: float32 [1536, 8960], P('dp', 'tensor'), may hold values from -0.15625 to 0.15625
- ffn_down: float32 [8960, 1536], P('tensor', 'dp'), may hold values from -0.1875 to 0.1875
- out_cotangent: bfloat16 [8192, 1536], P(('dp', 'tensor')), may hold values from -6 to 6
Outputs:
- block_out: bfloat16 [8192, 1536], P(('dp', 'tensor'))
- hidden_grad: bfloat16 [8192, 1536], P(('dp', 'tensor'))
- context_grad: bfloat16 [8, 512, 1536], P('dp', 'tensor')
- time_grad: float32 [8, 6, 1536], P('dp')
- modulation_grad: float32 [6, 1536], P(None, 'dp')
- self_query_grad: float32 [1536, 1536], P('dp', 'tensor')
- self_key_grad: float32 [1536, 1536], P('dp', 'tensor')
- self_value_grad: float32 [1536, 1536], P('dp', 'tensor')
- self_output_grad: float32 [1536, 1536], P('tensor', 'dp')
- self_query_gain_grad: float32 [12, 128], P('tensor', 'dp')
- self_key_gain_grad: float32 [12, 128], P('tensor', 'dp')
- cross_query_grad: float32 [1536, 1536], P('dp', 'tensor')
- cross_key_grad: float32 [1536, 1536], P('dp', 'tensor')
- cross_value_grad: float32 [1536, 1536], P('dp', 'tensor')
- cross_output_grad: float32 [1536, 1536], P('tensor', 'dp')
- cross_query_gain_grad: float32 [12, 128], P('tensor', 'dp')
- cross_key_gain_grad: float32 [12, 128], P('tensor', 'dp')
- norm_weight_grad: float32 [1536], P('dp')
- norm_bias_grad: float32 [1536], P('dp')
- ffn_up_grad: float32 [1536, 8960], P('dp', 'tensor')
- ffn_down_grad: float32 [8960, 1536], P('tensor', 'dp')
Inputs may be any that keep to these rules, and one draw needn't show every extreme that they name: text_lengths[c] counts the live text rows of clip c; the rows from that index on are padding. Some clip uses all 512 rows.
All inputs are finite; a program needn't handle non-finite values.
Results may differ from a plain program's by a relative error of at most 0.03.
Values may be sent and summed in bfloat16 or wider, within the bound.
A program may use at most 192 MiB of HBM per device.

v0:
```python
from functools import reduce
import math

import jax
import jax.numpy as jnp
from jax import lax
from jax.sharding import PartitionSpec as P

D = 1536
HEAD = 128


epsilon = 1e-06


def layer_norm(values):
    center = values - jnp.mean(values, axis=-1, keepdims=True)
    return center * lax.rsqrt(jnp.mean(center * center, axis=-1, keepdims=True) + epsilon)


def modulated(values, shift_row, scale_row):
    return layer_norm(values) * (1.0 + scale_row) + shift_row


def affine_norm(values, weight_row, bias_row):
    return layer_norm(values) * weight_row + bias_row


def gelu_tanh(values):
    return jax.nn.gelu(values, approximate=True)


def rotary_tables(positions, head_dim):
    pair_count = head_dim // 2
    side_pairs = pair_count // 3
    frame_pairs = pair_count - 2 * side_pairs
    pair_index = jnp.arange(pair_count)
    frame_mask = pair_index < frame_pairs
    height_mask = (pair_index >= frame_pairs) & (pair_index < frame_pairs + side_pairs)
    within = jnp.where(
        frame_mask,
        pair_index,
        jnp.where(height_mask, pair_index - frame_pairs, pair_index - frame_pairs - side_pairs),
    )
    extent = jnp.where(frame_mask, frame_pairs, side_pairs)
    frequency = jnp.power(10000.0, -within.astype(jnp.float32) / extent.astype(jnp.float32))
    coords = positions.astype(jnp.float32)
    coordinate = jnp.where(
        frame_mask[None, :],
        coords[0][:, None],
        jnp.where(height_mask[None, :], coords[1][:, None], coords[2][:, None]),
    )
    angles = jnp.repeat(coordinate * frequency[None, :], 2, axis=1)
    parity = jnp.arange(head_dim) % 2
    sign_pattern = jnp.where(parity == 0, -1.0, 1.0)
    return (jnp.cos(angles), jnp.sin(angles) * sign_pattern)


def rotate(values, cosine, sine_signed):
    next_lane = jnp.roll(values, -1, axis=-1)
    last_lane = jnp.roll(values, 1, axis=-1)
    parity = jnp.arange(values.shape[-1]) % 2
    partner = jnp.where(parity == 0, next_lane, last_lane)
    return values * cosine[:, None, :] + partner * sine_signed[:, None, :]


def fetch_self(
    modulation, self_query, self_key, self_value, self_output, self_query_gain, self_key_gain
):
    return (
        lax.all_gather(modulation.astype(jnp.bfloat16), "dp", axis=1, tiled=True),
        lax.all_gather(self_query.astype(jnp.bfloat16), "dp", axis=0, tiled=True),
        lax.all_gather(self_key.astype(jnp.bfloat16), "dp", axis=0, tiled=True),
        lax.all_gather(self_value.astype(jnp.bfloat16), "dp", axis=0, tiled=True),
        lax.all_gather(self_output.astype(jnp.bfloat16), "dp", axis=1, tiled=True),
        lax.all_gather(self_query_gain.astype(jnp.bfloat16), "dp", axis=1, tiled=True),
        lax.all_gather(self_key_gain.astype(jnp.bfloat16), "dp", axis=1, tiled=True),
    )


def fetch_cross(
    cross_query,
    cross_key,
    cross_value,
    cross_output,
    cross_query_gain,
    cross_key_gain,
    norm_weight,
    norm_bias,
):
    return (
        lax.all_gather(cross_query.astype(jnp.bfloat16), "dp", axis=0, tiled=True),
        lax.all_gather(cross_key.astype(jnp.bfloat16), "dp", axis=0, tiled=True),
        lax.all_gather(cross_value.astype(jnp.bfloat16), "dp", axis=0, tiled=True),
        lax.all_gather(cross_output.astype(jnp.bfloat16), "dp", axis=1, tiled=True),
        lax.all_gather(cross_query_gain.astype(jnp.bfloat16), "dp", axis=1, tiled=True),
        lax.all_gather(cross_key_gain.astype(jnp.bfloat16), "dp", axis=1, tiled=True),
        lax.all_gather(norm_weight.astype(jnp.bfloat16), "dp", axis=0, tiled=True),
        lax.all_gather(norm_bias.astype(jnp.bfloat16), "dp", axis=0, tiled=True),
    )


def fetch_ffn(ffn_up, ffn_down):
    return (
        lax.all_gather(ffn_up.astype(jnp.bfloat16), "dp", axis=0, tiled=True),
        lax.all_gather(ffn_down.astype(jnp.bfloat16), "dp", axis=1, tiled=True),
    )


def gather_rows(values):
    return lax.all_gather(values, "tensor", axis=0, tiled=True)


def gather_grads(values):
    return lax.all_gather(values, "tensor", axis=0, tiled=True)


def branch_sum(left_side, right_side):
    return lax.psum_scatter(
        jnp.dot(left_side, right_side, preferred_element_type=jnp.float32).astype(jnp.bfloat16),
        "tensor",
        scatter_dimension=0,
        tiled=True,
    ).astype(jnp.float32)


def input_grad_sum(operand_pairs):
    products = [
        jnp.einsum("rf,cf->rc", left_side, right_side, preferred_element_type=jnp.float32)
        for left_side, right_side in operand_pairs
    ]
    return lax.psum_scatter(
        reduce(lambda first_part, second_part: first_part + second_part, products).astype(
            jnp.bfloat16
        ),
        "tensor",
        scatter_dimension=0,
        tiled=True,
    ).astype(jnp.float32)


def head_sums(first_raw, second_raw):
    return lax.psum(
        (jnp.sum(first_raw * first_raw, axis=1), jnp.sum(second_raw * second_raw, axis=1)), "tensor"
    )


def head_dots(first_dot, second_dot):
    return lax.psum((first_dot, second_dot), "tensor")


def root_scale(square_sum):
    return lax.rsqrt(square_sum / D + epsilon)


def root_back(raw_values, scale_rows, gain_row, grad_normed, dot_rows):
    grad_raw = (
        scale_rows[:, None] * gain_row * grad_normed
        - raw_values * (scale_rows * scale_rows * scale_rows)[:, None] * dot_rows[:, None] / D
    )
    grad_gain = jnp.sum(raw_values * scale_rows[:, None] * grad_normed, axis=0)
    return (grad_raw, grad_gain)


def attend_forward(query_low, key_low, value_low, key_bias, factor):
    query_rows, group_count, head_dim = query_low.shape
    block_size = min(512, query_rows)
    blocks = query_low.reshape(query_rows // block_size, block_size, group_count, head_dim)

    def one_block(query_block):
        scores = (
            jnp.einsum("qhd,khd->hqk", query_block, key_low, preferred_element_type=jnp.float32)
            * factor
            + key_bias
        )
        highest = jnp.max(scores, axis=-1, keepdims=True)
        exponent = jnp.exp(scores - highest)
        row_total = jnp.sum(exponent, axis=-1, keepdims=True)
        probability = (exponent / row_total).astype(jnp.bfloat16)
        attended = jnp.einsum(
            "hqk,khd->qhd", probability, value_low, preferred_element_type=jnp.float32
        )
        return (attended.astype(jnp.bfloat16), (highest + jnp.log(row_total))[..., 0])

    attended, logsum = lax.map(one_block, blocks)
    return (attended.reshape(query_rows, group_count * head_dim), logsum)


def attend_backward(query_low, key_low, value_low, key_bias, logsum, grad_low, factor):
    query_rows, group_count, head_dim = query_low.shape
    block_size = min(512, query_rows)
    block_count = query_rows // block_size
    query_blocks = query_low.reshape(block_count, block_size, group_count, head_dim)
    grad_blocks = grad_low.reshape(block_count, block_size, group_count, head_dim)

    def one_block(running, inputs):
        key_grad, value_grad = running
        query_block, grad_block, logsum_block = inputs
        scores = (
            jnp.einsum("qhd,khd->hqk", query_block, key_low, preferred_element_type=jnp.float32)
            * factor
            + key_bias
        )
        probability = jnp.exp(scores - logsum_block[..., None])
        grad_prob = jnp.einsum(
            "qhd,khd->hqk", grad_block, value_low, preferred_element_type=jnp.float32
        )
        center = jnp.sum(probability * grad_prob, axis=-1, keepdims=True)
        grad_scores = (probability * (grad_prob - center)).astype(jnp.bfloat16)
        query_grad = (
            jnp.einsum("hqk,khd->qhd", grad_scores, key_low, preferred_element_type=jnp.float32)
            * factor
        )
        key_grad = (
            key_grad
            + jnp.einsum(
                "hqk,qhd->khd", grad_scores, query_block, preferred_element_type=jnp.float32
            )
            * factor
        )
        value_grad = value_grad + jnp.einsum(
            "hqk,qhd->khd",
            probability.astype(jnp.bfloat16),
            grad_block,
            preferred_element_type=jnp.float32,
        )
        return ((key_grad, value_grad), query_grad)

    start_grads = (jnp.zeros(key_low.shape, jnp.float32), jnp.zeros(value_low.shape, jnp.float32))
    (key_grad, value_grad), query_grads = lax.scan(
        one_block, start_grads, (query_blocks, grad_blocks, logsum)
    )
    key_count = key_low.shape[0]
    return (
        query_grads.reshape(query_rows, group_count * head_dim),
        key_grad.reshape(key_count, group_count * head_dim),
        value_grad.reshape(key_count, group_count * head_dim),
    )


def on_device(
    hidden_in,
    context,
    time_emb,
    text_lengths,
    positions,
    modulation,
    self_query,
    self_key,
    self_value,
    self_output,
    self_query_gain,
    self_key_gain,
    cross_query,
    cross_key,
    cross_value,
    cross_output,
    cross_query_gain,
    cross_key_gain,
    norm_weight,
    norm_bias,
    ffn_up,
    ffn_down,
    out_cotangent,
):
    factor = 1.0 / math.sqrt(HEAD)
    group_count = self_query_gain.shape[0]
    clip_rows = positions.shape[1]
    residual = hidden_in.astype(jnp.float32)
    modulation_low, query_weight, key_weight, value_weight, output_weight, query_gain, key_gain = (
        fetch_self(
            modulation,
            self_query,
            self_key,
            self_value,
            self_output,
            self_query_gain,
            self_key_gain,
        )
    )
    shifts = modulation_low.astype(jnp.float32) + time_emb[0]
    cosine, sine_signed = rotary_tables(positions, HEAD)
    self_in = modulated(residual, shifts[0], shifts[1]).astype(jnp.bfloat16)
    self_rows = gather_rows(self_in)
    query_raw = jnp.dot(self_rows, query_weight, preferred_element_type=jnp.float32)
    key_raw = jnp.dot(self_rows, key_weight, preferred_element_type=jnp.float32)
    value_raw = jnp.dot(self_rows, value_weight, preferred_element_type=jnp.float32)
    query_sums, key_sums = head_sums(query_raw, key_raw)
    query_scale = root_scale(query_sums)
    key_scale = root_scale(key_sums)
    query_gain_row = query_gain.astype(jnp.float32).reshape(-1)
    key_gain_row = key_gain.astype(jnp.float32).reshape(-1)
    query_normed = query_raw * query_scale[:, None] * query_gain_row
    key_normed = key_raw * key_scale[:, None] * key_gain_row
    query_low = rotate(
        query_normed.reshape(clip_rows, group_count, HEAD), cosine, sine_signed
    ).astype(jnp.bfloat16)
    key_low = rotate(key_normed.reshape(clip_rows, group_count, HEAD), cosine, sine_signed).astype(
        jnp.bfloat16
    )
    value_low = value_raw.astype(jnp.bfloat16).reshape(clip_rows, group_count, HEAD)
    open_bias = jnp.zeros((clip_rows,), jnp.float32)
    self_attended, self_logsum = attend_forward(query_low, key_low, value_low, open_bias, factor)
    self_branch = branch_sum(self_attended, output_weight)
    after_self = residual + self_branch * shifts[2]
    (
        cross_query_weight,
        cross_key_weight,
        cross_value_weight,
        cross_output_weight,
        cross_query_gain_low,
        cross_key_gain_low,
        norm_weight_low,
        norm_bias_low,
    ) = fetch_cross(
        cross_query,
        cross_key,
        cross_value,
        cross_output,
        cross_query_gain,
        cross_key_gain,
        norm_weight,
        norm_bias,
    )
    norm_gain_row = norm_weight_low.astype(jnp.float32)
    norm_shift_row = norm_bias_low.astype(jnp.float32)
    cross_in = affine_norm(after_self, norm_gain_row, norm_shift_row).astype(jnp.bfloat16)
    cross_rows = gather_rows(cross_in)
    text_tokens = lax.all_gather(context, "tensor", axis=1, tiled=True)[0]
    text_count = text_tokens.shape[0]
    cross_query_raw = jnp.dot(cross_rows, cross_query_weight, preferred_element_type=jnp.float32)
    cross_key_raw = jnp.dot(text_tokens, cross_key_weight, preferred_element_type=jnp.float32)
    cross_value_raw = jnp.dot(text_tokens, cross_value_weight, preferred_element_type=jnp.float32)
    cross_query_sums, cross_key_sums = head_sums(cross_query_raw, cross_key_raw)
    cross_query_scale = root_scale(cross_query_sums)
    cross_key_scale = root_scale(cross_key_sums)
    cross_query_gain_row = cross_query_gain_low.astype(jnp.float32).reshape(-1)
    cross_key_gain_row = cross_key_gain_low.astype(jnp.float32).reshape(-1)
    cross_query_low = (
        (cross_query_raw * cross_query_scale[:, None] * cross_query_gain_row)
        .astype(jnp.bfloat16)
        .reshape(clip_rows, group_count, HEAD)
    )
    cross_key_low = (
        (cross_key_raw * cross_key_scale[:, None] * cross_key_gain_row)
        .astype(jnp.bfloat16)
        .reshape(text_count, group_count, HEAD)
    )
    cross_value_low = cross_value_raw.astype(jnp.bfloat16).reshape(text_count, group_count, HEAD)
    text_bias = jnp.where(jnp.arange(text_count) < text_lengths[0], 0.0, -1e30).astype(jnp.float32)
    cross_attended, cross_logsum = attend_forward(
        cross_query_low, cross_key_low, cross_value_low, text_bias, factor
    )
    cross_branch = branch_sum(cross_attended, cross_output_weight)
    after_cross = after_self + cross_branch
    up_weight, down_weight = fetch_ffn(ffn_up, ffn_down)
    ffn_in = modulated(after_cross, shifts[3], shifts[4]).astype(jnp.bfloat16)
    ffn_rows = gather_rows(ffn_in)
    hidden_pre = jnp.dot(ffn_rows, up_weight, preferred_element_type=jnp.float32)
    activated = gelu_tanh(hidden_pre).astype(jnp.bfloat16)
    ffn_branch = branch_sum(activated, down_weight)
    block_out = (after_cross + ffn_branch * shifts[5]).astype(jnp.bfloat16)
    grad_stream = out_cotangent.astype(jnp.float32)
    shift_five = jnp.sum(grad_stream * ffn_branch, axis=0)
    ffn_grad_rows = gather_grads((grad_stream * shifts[5]).astype(jnp.bfloat16))
    up_weight, down_weight = fetch_ffn(ffn_up, ffn_down)
    activated_grad = jnp.einsum(
        "rd,fd->rf", ffn_grad_rows, down_weight, preferred_element_type=jnp.float32
    )
    ffn_down_grad = jnp.einsum(
        "rf,rd->fd", activated, ffn_grad_rows, preferred_element_type=jnp.float32
    )
    ignored, gelu_back = jax.vjp(gelu_tanh, hidden_pre)
    hidden_pre_grad = gelu_back(activated_grad)[0].astype(jnp.bfloat16)
    ffn_up_grad = jnp.einsum(
        "rc,rf->cf", ffn_rows, hidden_pre_grad, preferred_element_type=jnp.float32
    )
    ffn_in_grad = input_grad_sum([(hidden_pre_grad, up_weight)])
    ignored, ffn_norm_back = jax.vjp(modulated, after_cross, shifts[3], shifts[4])
    stream_part, shift_three, shift_four = ffn_norm_back(ffn_in_grad)
    grad_stream = grad_stream + stream_part
    cross_grad_rows = gather_grads(grad_stream.astype(jnp.bfloat16))
    (
        cross_query_weight,
        cross_key_weight,
        cross_value_weight,
        cross_output_weight,
        cross_query_gain_low,
        cross_key_gain_low,
        norm_weight_low,
        norm_bias_low,
    ) = fetch_cross(
        cross_query,
        cross_key,
        cross_value,
        cross_output,
        cross_query_gain,
        cross_key_gain,
        norm_weight,
        norm_bias,
    )
    cross_attended_grad = jnp.einsum(
        "rd,ed->re", cross_grad_rows, cross_output_weight, preferred_element_type=jnp.float32
    ).astype(jnp.bfloat16)
    cross_output_grad = jnp.einsum(
        "re,rd->ed", cross_attended, cross_grad_rows, preferred_element_type=jnp.float32
    )
    cross_query_normed_grad, cross_key_normed_grad, cross_value_full_grad = attend_backward(
        cross_query_low,
        cross_key_low,
        cross_value_low,
        text_bias,
        cross_logsum,
        cross_attended_grad.reshape(clip_rows, group_count, HEAD),
        factor,
    )
    cross_query_dots, cross_key_dots = head_dots(
        jnp.sum(cross_query_raw * cross_query_gain_row * cross_query_normed_grad, axis=1),
        jnp.sum(cross_key_raw * cross_key_gain_row * cross_key_normed_grad, axis=1),
    )
    cross_query_pre_grad, cross_query_gain_grad = root_back(
        cross_query_raw,
        cross_query_scale,
        cross_query_gain_row,
        cross_query_normed_grad,
        cross_query_dots,
    )
    cross_key_pre_grad, cross_key_gain_grad = root_back(
        cross_key_raw, cross_key_scale, cross_key_gain_row, cross_key_normed_grad, cross_key_dots
    )
    cross_query_raw_grad = cross_query_pre_grad.astype(jnp.bfloat16)
    cross_key_raw_grad = cross_key_pre_grad.astype(jnp.bfloat16)
    cross_value_raw_grad = cross_value_full_grad.astype(jnp.bfloat16)
    cross_query_grad = jnp.einsum(
        "rc,re->ce", cross_rows, cross_query_raw_grad, preferred_element_type=jnp.float32
    )
    cross_key_grad = jnp.einsum(
        "rc,re->ce", text_tokens, cross_key_raw_grad, preferred_element_type=jnp.float32
    )
    cross_value_grad = jnp.einsum(
        "rc,re->ce", text_tokens, cross_value_raw_grad, preferred_element_type=jnp.float32
    )
    text_grad = lax.psum_scatter(
        (
            jnp.einsum(
                "re,ce->rc",
                cross_key_raw_grad,
                cross_key_weight,
                preferred_element_type=jnp.float32,
            )
            + jnp.einsum(
                "re,ce->rc",
                cross_value_raw_grad,
                cross_value_weight,
                preferred_element_type=jnp.float32,
            )
        ).astype(jnp.bfloat16),
        "tensor",
        scatter_dimension=0,
        tiled=True,
    )
    cross_in_grad = input_grad_sum([(cross_query_raw_grad, cross_query_weight)])
    ignored, cross_norm_back = jax.vjp(affine_norm, after_self, norm_gain_row, norm_shift_row)
    stream_part, norm_weight_part, norm_bias_part = cross_norm_back(cross_in_grad)
    grad_stream = grad_stream + stream_part
    shift_two = jnp.sum(grad_stream * self_branch, axis=0)
    self_grad_rows = gather_grads((grad_stream * shifts[2]).astype(jnp.bfloat16))
    modulation_low, query_weight, key_weight, value_weight, output_weight, query_gain, key_gain = (
        fetch_self(
            modulation,
            self_query,
            self_key,
            self_value,
            self_output,
            self_query_gain,
            self_key_gain,
        )
    )
    attended_grad = jnp.einsum(
        "rd,ed->re", self_grad_rows, output_weight, preferred_element_type=jnp.float32
    ).astype(jnp.bfloat16)
    self_output_grad = jnp.einsum(
        "re,rd->ed", self_attended, self_grad_rows, preferred_element_type=jnp.float32
    )
    query_rot_grad, key_rot_grad, value_full_grad = attend_backward(
        query_low,
        key_low,
        value_low,
        open_bias,
        self_logsum,
        attended_grad.reshape(clip_rows, group_count, HEAD),
        factor,
    )
    query_normed_grad = rotate(
        query_rot_grad.reshape(clip_rows, group_count, HEAD), cosine, -sine_signed
    ).reshape(clip_rows, -1)
    key_normed_grad = rotate(
        key_rot_grad.reshape(clip_rows, group_count, HEAD), cosine, -sine_signed
    ).reshape(clip_rows, -1)
    query_dots, key_dots = head_dots(
        jnp.sum(query_raw * query_gain_row * query_normed_grad, axis=1),
        jnp.sum(key_raw * key_gain_row * key_normed_grad, axis=1),
    )
    query_pre_grad, query_gain_grad = root_back(
        query_raw, query_scale, query_gain_row, query_normed_grad, query_dots
    )
    key_pre_grad, key_gain_grad = root_back(
        key_raw, key_scale, key_gain_row, key_normed_grad, key_dots
    )
    query_raw_grad = query_pre_grad.astype(jnp.bfloat16)
    key_raw_grad = key_pre_grad.astype(jnp.bfloat16)
    value_raw_grad = value_full_grad.astype(jnp.bfloat16)
    self_query_grad = jnp.einsum(
        "rc,re->ce", self_rows, query_raw_grad, preferred_element_type=jnp.float32
    )
    self_key_grad = jnp.einsum(
        "rc,re->ce", self_rows, key_raw_grad, preferred_element_type=jnp.float32
    )
    self_value_grad = jnp.einsum(
        "rc,re->ce", self_rows, value_raw_grad, preferred_element_type=jnp.float32
    )
    self_in_grad = input_grad_sum(
        [(query_raw_grad, query_weight), (key_raw_grad, key_weight), (value_raw_grad, value_weight)]
    )
    ignored, self_norm_back = jax.vjp(modulated, residual, shifts[0], shifts[1])
    stream_part, shift_zero, shift_one = self_norm_back(self_in_grad)
    hidden_grad = (grad_stream + stream_part).astype(jnp.bfloat16)
    shift_grads = jnp.stack([shift_zero, shift_one, shift_two, shift_three, shift_four, shift_five])
    time_total, norm_weight_total, norm_bias_total = (
        lax.psum(shift_grads.astype(jnp.bfloat16), "tensor").astype(jnp.float32),
        lax.psum(norm_weight_part.astype(jnp.bfloat16), "tensor").astype(jnp.float32),
        lax.psum(norm_bias_part.astype(jnp.bfloat16), "tensor").astype(jnp.float32),
    )
    summed_grads = (
        lax.psum_scatter(
            time_total.astype(jnp.bfloat16), "dp", scatter_dimension=1, tiled=True
        ).astype(jnp.float32),
        lax.psum_scatter(
            self_query_grad.astype(jnp.bfloat16), "dp", scatter_dimension=0, tiled=True
        ).astype(jnp.float32),
        lax.psum_scatter(
            self_key_grad.astype(jnp.bfloat16), "dp", scatter_dimension=0, tiled=True
        ).astype(jnp.float32),
        lax.psum_scatter(
            self_value_grad.astype(jnp.bfloat16), "dp", scatter_dimension=0, tiled=True
        ).astype(jnp.float32),
        lax.psum_scatter(
            self_output_grad.astype(jnp.bfloat16), "dp", scatter_dimension=1, tiled=True
        ).astype(jnp.float32),
        lax.psum_scatter(
            query_gain_grad.reshape(group_count, HEAD).astype(jnp.bfloat16),
            "dp",
            scatter_dimension=1,
            tiled=True,
        ).astype(jnp.float32),
        lax.psum_scatter(
            key_gain_grad.reshape(group_count, HEAD).astype(jnp.bfloat16),
            "dp",
            scatter_dimension=1,
            tiled=True,
        ).astype(jnp.float32),
        lax.psum_scatter(
            cross_query_grad.astype(jnp.bfloat16), "dp", scatter_dimension=0, tiled=True
        ).astype(jnp.float32),
        lax.psum_scatter(
            cross_key_grad.astype(jnp.bfloat16), "dp", scatter_dimension=0, tiled=True
        ).astype(jnp.float32),
        lax.psum_scatter(
            cross_value_grad.astype(jnp.bfloat16), "dp", scatter_dimension=0, tiled=True
        ).astype(jnp.float32),
        lax.psum_scatter(
            cross_output_grad.astype(jnp.bfloat16), "dp", scatter_dimension=1, tiled=True
        ).astype(jnp.float32),
        lax.psum_scatter(
            cross_query_gain_grad.reshape(group_count, HEAD).astype(jnp.bfloat16),
            "dp",
            scatter_dimension=1,
            tiled=True,
        ).astype(jnp.float32),
        lax.psum_scatter(
            cross_key_gain_grad.reshape(group_count, HEAD).astype(jnp.bfloat16),
            "dp",
            scatter_dimension=1,
            tiled=True,
        ).astype(jnp.float32),
        lax.psum_scatter(
            norm_weight_total.astype(jnp.bfloat16), "dp", scatter_dimension=0, tiled=True
        ).astype(jnp.float32),
        lax.psum_scatter(
            norm_bias_total.astype(jnp.bfloat16), "dp", scatter_dimension=0, tiled=True
        ).astype(jnp.float32),
        lax.psum_scatter(
            ffn_up_grad.astype(jnp.bfloat16), "dp", scatter_dimension=0, tiled=True
        ).astype(jnp.float32),
        lax.psum_scatter(
            ffn_down_grad.astype(jnp.bfloat16), "dp", scatter_dimension=1, tiled=True
        ).astype(jnp.float32),
    )
    return (
        block_out,
        hidden_grad,
        text_grad[None],
        time_total[None],
        summed_grads[0],
        summed_grads[1],
        summed_grads[2],
        summed_grads[3],
        summed_grads[4],
        summed_grads[5],
        summed_grads[6],
        summed_grads[7],
        summed_grads[8],
        summed_grads[9],
        summed_grads[10],
        summed_grads[11],
        summed_grads[12],
        summed_grads[13],
        summed_grads[14],
        summed_grads[15],
        summed_grads[16],
    )


def solution(mesh):
    placed = (
        P(("dp", "tensor"), None),
        P("dp", "tensor", None),
        P("dp", None, None),
        P("dp"),
        P(None, "dp"),
        P(None, "dp"),
        P("dp", "tensor"),
        P("dp", "tensor"),
        P("dp", "tensor"),
        P("tensor", "dp"),
        P("tensor", "dp"),
        P("tensor", "dp"),
        P("dp", "tensor"),
        P("dp", "tensor"),
        P("dp", "tensor"),
        P("tensor", "dp"),
        P("tensor", "dp"),
        P("tensor", "dp"),
        P("dp"),
        P("dp"),
        P("dp", "tensor"),
        P("tensor", "dp"),
        P(("dp", "tensor"), None),
    )
    return jax.shard_map(
        on_device,
        mesh=mesh,
        in_specs=placed,
        out_specs=(
            P(("dp", "tensor"), None),
            P(("dp", "tensor"), None),
            P("dp", "tensor", None),
            P("dp", None, None),
            P(None, "dp"),
            P("dp", "tensor"),
            P("dp", "tensor"),
            P("dp", "tensor"),
            P("tensor", "dp"),
            P("tensor", "dp"),
            P("tensor", "dp"),
            P("dp", "tensor"),
            P("dp", "tensor"),
            P("dp", "tensor"),
            P("tensor", "dp"),
            P("tensor", "dp"),
            P("tensor", "dp"),
            P("dp"),
            P("dp"),
            P("dp", "tensor"),
            P("tensor", "dp"),
        ),
        check_vma=False,
    )
```

profile of v0, /device:TPU:0, one launch (start us, length us, event | category | flops | bytes accessed | tf_op | source)
XLA Modules:
  0.0 2360.9 jit_solution(8531099906283934451)
XLA Ops:
  9.7 32.3 %all-gather = bf16[8,192,6]{1,2,0:T(8,128)(2,1)S(1)} all-gather(bf16[1,192,6]{1,2,0:T(8,128)(2,1)S(1)} %convert_bitcast_fusion), channel_id=1, replica_groups=mesh['dp'=8,'tensor'=4] {'dp'}, dimensions={0}, use_global_device_ids=true | all-gather | bytes 20736 | tf_op jit(solution)/shard_map/all_gather | solution.py:71
  51.9 20.5 all-gather.2
  72.5 16.3 all-gather.1
  97.2 30.7 %all-gather.27.cloned.1.call-done = bf16[1536,384]{1,0:T(8,128)(2,1)} async-done(((bf16[192,384]{1,0:T(8,128)(2,1)}), bf16[1536,384]{1,0:T(8,128)(2,1)}) %all-gather.27.cloned.1.call-update) | async-done | bytes 1179664 | tf_op jit(solution)/shard_map/all_gather | solution.py:73
  192.9 20.0 all-gather.31.cloned.1.call-done
  223.7 19.4 all-reduce.8
  259.1 20.5 all-gather.3
  280.3 16.5 all-gather.4
  298.9 20.1 all-gather.37.cloned.1.call-done
  322.6 40.5 %all-gather.39.cloned.1.call-done = bf16[1536,384]{1,0:T(8,128)(2,1)} async-done(((bf16[192,384]{1,0:T(8,128)(2,1)}), bf16[1536,384]{1,0:T(8,128)(2,1)}) %all-gather.39.cloned.1.call-update) | async-done | bytes 1179664 | tf_op jit(solution)/shard_map/all_gather | solution.py:93
  366.1 39.7 %all-gather.35.cloned.1.call-done = bf16[1536,384]{1,0:T(8,128)(2,1)} async-done(((bf16[192,384]{1,0:T(8,128)(2,1)}), bf16[1536,384]{1,0:T(8,128)(2,1)}) %all-gather.35.cloned.1.call-update) | async-done | bytes 1179664 | tf_op jit(solution)/shard_map/all_gather | solution.py:92
  405.8 29.5 %all-gather.33.cloned.1.call-done = bf16[1024,1536]{1,0:T(8,128)(2,1)} async-done(((bf16[256,1536]{1,0:T(8,128)(2,1)}), bf16[1024,1536]{1,0:T(8,128)(2,1)}) %all-gather.33.cloned.1.call-update) | async-done | bytes 3145744 | tf_op jit(solution)/shard_map/all_gather | solution.py:111
  491.5 29.5 %reduce-scatter.39.cloned.1.call-done = bf16[256,1536]{1,0:T(8,128)(2,1)} async-done(((bf16[1024,1536]{1,0:T(8,128)(2,1)}), bf16[256,1536]{1,0:T(8,128)(2,1)}) %reduce-scatter.39.cloned.1.call-update) | async-done | bytes 786448 | tf_op jit(solution)/shard_map/reduce_scatter | solution.py:119
  525.1 26.6 %all-gather.51.cloned.1.call-done = bf16[1024,1536]{1,0:T(8,128)(2,1)} async-done(((bf16[256,1536]{1,0:T(8,128)(2,1)}), bf16[1024,1536]{1,0:T(8,128)(2,1)}) %all-gather.51.cloned.1.call-update) | async-done | bytes 3145744 | tf_op jit(solution)/shard_map/all_gather | solution.py:115
  551.7 110.9 %all-gather.49.cloned.1.call-done = bf16[2240,1536]{0,1:T(8,128)(2,1)} async-done(((bf16[2240,192]{0,1:T(8,128)(2,1)}), bf16[2240,1536]{0,1:T(8,128)(2,1)}) %all-gather.49.cloned.1.call-update) | async-done | bytes 6881296 | tf_op jit(solution)/shard_map/all_gather | solution.py:106
  662.5 13.3 fusion.163
  675.8 95.8 %all-gather.47.cloned.1.call-done = bf16[1536,2240]{1,0:T(8,128)(2,1)} async-done(((bf16[192,2240]{1,0:T(8,128)(2,1)}), bf16[1536,2240]{1,0:T(8,128)(2,1)}) %all-gather.47.cloned.1.call-update) | async-done | bytes 6881296 | tf_op jit(solution)/shard_map/all_gather | solution.py:105
  771.6 28.7 %all-gather.45.cloned.1.call-done = bf16[1024,1536]{1,0:T(8,128)(2,1)} async-done(((bf16[256,1536]{1,0:T(8,128)(2,1)}), bf16[1024,1536]{1,0:T(8,128)(2,1)}) %all-gather.45.cloned.1.call-update) | async-done | bytes 3145744 | tf_op jit(solution)/shard_map/all_gather | solution.py:111
  800.3 20.9 fusion.81
  821.3 12.6 convolution_convert_fusion.3
  833.9 14.1 convolution_convert_fusion.4
  848.1 23.8 %reduce-scatter.43.cloned.1.call-done = bf16[256,1536]{1,0:T(8,128)(2,1)} async-done(((bf16[1024,1536]{1,0:T(8,128)(2,1)}), bf16[256,1536]{1,0:T(8,128)(2,1)}) %reduce-scatter.43.cloned.1.call-update) | async-done | bytes 786448 | tf_op jit(solution)/shard_map/reduce_scatter | solution.py:132
  875.7 37.0 %reduce-scatter.41.cloned.1.call-done = bf16[256,1536]{1,0:T(8,128)(2,1)} async-done(((bf16[1024,1536]{1,0:T(8,128)(2,1)}), bf16[256,1536]{1,0:T(8,128)(2,1)}) %reduce-scatter.41.cloned.1.call-update) | async-done | bytes 786448 | tf_op jit(solution)/shard_map/reduce_scatter | solution.py:119
  918.6 28.6 %all-gather.53.cloned.1.call-done = bf16[1024,1536]{1,0:T(8,128)(2,1)} async-done(((bf16[256,1536]{1,0:T(8,128)(2,1)}), bf16[1024,1536]{1,0:T(8,128)(2,1)}) %all-gather.53.cloned.1.call-update) | async-done | bytes 3145744 | tf_op jit(solution)/shard_map/all_gather | solution.py:115
  952.4 64.9 %while.57 = (s32[]{:T(128)}, f32[512,3,128]{0,2,1:T(8,128)}, f32[512,3,128]{0,2,1:T(8,128)}, f32[2,512,3,128]{1,0,3,2:T(2,128)}, bf16[2,512,3,128]{3,1,2,0:T(8,1...) while((s32[]{:T(128)}, f32[512,3,128]{0,2,1:T(8,128)}, ...), condition=%wide.region_30.31_spmd.clone, body=%wide.region_28.30_spmd.clone.sunk | while | flops 1014889984 | bytes 39751844 | solution.py:230
  964.0 15.0 dynamic_update_slice.40
  996.3 15.0 dynamic_update_slice.40
  1030.4 39.1 %reduce-scatter.45.cloned.1.call-done = bf16[256,1536]{1,0:T(8,128)(2,1)} async-done(((bf16[1024,1536]{1,0:T(8,128)(2,1)}), bf16[256,1536]{1,0:T(8,128)(2,1)}) %reduce-scatter.45.cloned.1.call-update) | async-done | bytes 786448 | tf_op jit(solution)/shard_map/reduce_scatter | solution.py:132
  1077.7 27.8 %all-gather.55.cloned.1.call-done = bf16[1024,1536]{1,0:T(8,128)(2,1)} async-done(((bf16[256,1536]{1,0:T(8,128)(2,1)}), bf16[1024,1536]{1,0:T(8,128)(2,1)}) %all-gather.55.cloned.1.call-update) | async-done | bytes 3145744 | tf_op jit(solution)/shard_map/all_gather | solution.py:115
  1110.6 34.2 %while.58 = (s32[]{:T(128)}, f32[1024,3,128]{0,2,1:T(8,128)}, f32[1024,3,128]{0,2,1:T(8,128)}, f32[2,512,3,128]{3,1,2,0:T(8,128)}, bf16[2,512,3,128]{3,1,2,0:T(8...) while((s32[]{:T(128)}, f32[1024,3,128]{0,2,1:T(8,128)}, ...), condition=%wide.region_38.39_spmd.clone, body=%wide.region_36.38_spmd.clone.sunk | while | flops 2034301440 | bytes 133740424 | solution.py:230
  1214.9 12.7 convolution_convert_fusion.1
  1227.6 14.1 convolution_convert_fusion
  1273.2 21.9 all-reduce.7
  1321.1 30.1 %reduce-scatter.77.cloned.1.call-done = bf16[16,3]{1,0:T(8,128)(2,1)} async-done(((bf16[128,3]{1,0:T(8,128)(2,1)}), bf16[16,3]{1,0:T(8,128)(2,1)}) %reduce-scatter.77.cloned.1.call-update) | async-done | bytes 112
  1352.5 65.6 %reduce-scatter.75.cloned.1.call-done = bf16[192,384]{1,0:T(8,128)(2,1)} async-done(((bf16[1536,384]{1,0:T(8,128)(2,1)}), bf16[192,384]{1,0:T(8,128)(2,1)}) %reduce-scatter.75.cloned.1.call-update) | async-done | bytes 147472
  1420.0 64.4 %reduce-scatter.61.cloned.1.call-done = bf16[384,192]{0,1:T(8,128)(2,1)} async-done(((bf16[384,1536]{0,1:T(8,128)(2,1)}), bf16[384,192]{0,1:T(8,128)(2,1)}) %reduce-scatter.61.cloned.1.call-update) | async-done | bytes 147472 | tf_op jit(solution)/shard_map/reduce_scatter | solution.py:571
  1486.1 65.4 %reduce-scatter.59.cloned.1.call-done = bf16[192,384]{1,0:T(8,128)(2,1)} async-done(((bf16[1536,384]{1,0:T(8,128)(2,1)}), bf16[192,384]{1,0:T(8,128)(2,1)}) %reduce-scatter.59.cloned.1.call-update) | async-done | bytes 147472 | tf_op jit(solution)/shard_map/reduce_scatter | solution.py:562
  1553.1 130.1 %reduce-scatter.63.cloned.1.call-done = bf16[192,2240]{1,0:T(8,128)(2,1)} async-done(((bf16[1536,2240]{1,0:T(8,128)(2,1)}), bf16[192,2240]{1,0:T(8,128)(2,1)}) %reduce-scatter.63.cloned.1.call-update) | async-done | bytes 860176 | tf_op jit(solution)/shard_map/reduce_scatter | solution.py:592
  1685.6 129.6 %reduce-scatter.65.cloned.1.call-done = bf16[2240,192]{0,1:T(8,128)(2,1)} async-done(((bf16[2240,1536]{0,1:T(8,128)(2,1)}), bf16[2240,192]{0,1:T(8,128)(2,1)}) %reduce-scatter.65.cloned.1.call-update) | async-done | bytes 860176 | tf_op jit(solution)/shard_map/reduce_scatter | solution.py:595
  1817.7 53.8 %reduce-scatter.71.cloned.1.call-done = bf16[16,3]{1,0:T(8,128)(2,1)} async-done(((bf16[128,3]{1,0:T(8,128)(2,1)}), bf16[16,3]{1,0:T(8,128)(2,1)}) %reduce-scatter.71.cloned.1.call-update) | async-done | bytes 112
  1872.9 54.9 %reduce-scatter.69.cloned.1.call-done = bf16[16,3]{1,0:T(8,128)(2,1)} async-done(((bf16[128,3]{1,0:T(8,128)(2,1)}), bf16[16,3]{1,0:T(8,128)(2,1)}) %reduce-scatter.69.cloned.1.call-update) | async-done | bytes 112
  1929.1 65.0 %reduce-scatter.73.cloned.1.call-done = bf16[192,384]{1,0:T(8,128)(2,1)} async-done(((bf16[1536,384]{1,0:T(8,128)(2,1)}), bf16[192,384]{1,0:T(8,128)(2,1)}) %reduce-scatter.73.cloned.1.call-update) | async-done | bytes 147472
  1996.0 64.7 %reduce-scatter.57.cloned.1.call-done = bf16[384,192]{0,1:T(8,128)(2,1)} async-done(((bf16[384,1536]{0,1:T(8,128)(2,1)}), bf16[384,192]{0,1:T(8,128)(2,1)}) %reduce-scatter.57.cloned.1.call-update) | async-done | bytes 147472 | tf_op jit(solution)/shard_map/reduce_scatter | solution.py:547
  2062.3 64.7 %reduce-scatter.53.cloned.1.call-done = bf16[192,384]{1,0:T(8,128)(2,1)} async-done(((bf16[1536,384]{1,0:T(8,128)(2,1)}), bf16[192,384]{1,0:T(8,128)(2,1)}) %reduce-scatter.53.cloned.1.call-update) | async-done | bytes 147472 | tf_op jit(solution)/shard_map/reduce_scatter | solution.py:541
  2128.7 64.7 %reduce-scatter.51.cloned.1.call-done = bf16[192,384]{1,0:T(8,128)(2,1)} async-done(((bf16[1536,384]{1,0:T(8,128)(2,1)}), bf16[192,384]{1,0:T(8,128)(2,1)}) %reduce-scatter.51.cloned.1.call-update) | async-done | bytes 147472 | tf_op jit(solution)/shard_map/reduce_scatter | solution.py:538
  2195.0 64.6 %reduce-scatter.55.cloned.1.call-done = bf16[192,384]{1,0:T(8,128)(2,1)} async-done(((bf16[1536,384]{1,0:T(8,128)(2,1)}), bf16[192,384]{1,0:T(8,128)(2,1)}) %reduce-scatter.55.cloned.1.call-update) | async-done | bytes 147472 | tf_op jit(solution)/shard_map/reduce_scatter | solution.py:544
  2264.6 58.8 %reduce-scatter.67.cloned.1.call-done = bf16[192,6]{1,0:T(8,128)(2,1)} async-done(((bf16[1536,6]{1,0:T(8,128)(2,1)}), bf16[192,6]{1,0:T(8,128)(2,1)}) %reduce-scatter.67.cloned.1.call-update) | async-done | bytes 2320
  2324.9 28.7 %reduce-scatter.49.cloned.1.call-done = bf16[128,1536]{1,0:T(8,128)(2,1)} async-done(((bf16[512,1536]{1,0:T(8,128)(2,1)}), bf16[128,1536]{1,0:T(8,128)(2,1)}) %reduce-scatter.49.cloned.1.call-update) | async-done | bytes 393232 | tf_op jit(solution)/shard_map/reduce_scatter | solution.py:443
  (688 shorter events, 465.7 us)
Async XLA Ops:
  7.2 85.2 %all-gather.25.cloned.1.call-start = ((), (), s32[]{:S(2)}) async-start(), calls=%async_computation.23 | async-start | bytes 1327104 | tf_op jit(solution)/shard_map/all_gather | solution.py:72
  9.0 83.4 %all-gather.23.cloned.1.call-start = ((), (), s32[]{:S(2)}) async-start(), calls=%async_computation.22 | async-start | bytes 3932160 | tf_op jit(solution)/shard_map/all_gather | solution.py:111
  46.0 81.9 %all-gather.27.cloned.1.call-start = ((), (), s32[]{:S(2)}) async-start(), calls=%async_computation.24 | async-start | bytes 1327104 | tf_op jit(solution)/shard_map/all_gather | solution.py:73
  46.7 123.6 %all-gather.29.cloned.1.call-start = ((), (), s32[]{:S(2)}) async-start(), calls=%async_computation.25 | async-start | bytes 1327104 | tf_op jit(solution)/shard_map/all_gather | solution.py:74
  47.5 165.3 %all-gather.31.cloned.1.call-start = ((), (), s32[]{:S(2)}) async-start(), calls=%async_computation.26 | async-start | bytes 1327104 | tf_op jit(solution)/shard_map/all_gather | solution.py:75
  48.3 206.5 %reduce-scatter.37.cloned.1.call-start = ((), (), s32[]{:S(2)}) async-start(), calls=%async_computation.27 | async-start | bytes 3932160 | tf_op jit(solution)/shard_map/reduce_scatter | solution.py:119
  48.4 114.4 %copy-start.133 = (pred[128]{0:T(512)(128)(4,1)}, pred[128]{0:T(512)(128)(4,1)S(1)}, u32[]{:S(2)}) copy-start(pred[128]{0:T(512)(128)(4,1)S(1)} %fusion.147) | copy-start | bytes 388
  51.2 95.7 %copy-start.38 = (f32[1024,128]{0,1:T(8,128)}, f32[1024,128]{0,1:T(8,128)S(1)}, u32[]{:S(2)}) copy-start(f32[1024,128]{0,1:T(8,128)S(1)} %cos.18) | copy-start | bytes 1572868
  217.9 81.0 %all-gather.41.cloned.1.call-start = ((), (), s32[]{:S(2)}) async-start(), calls=%async_computation.32 | async-start | bytes 1327104 | tf_op jit(solution)/shard_map/all_gather | solution.py:94
  219.5 99.5 %all-gather.37.cloned.1.call-start = ((), (), s32[]{:S(2)}) async-start(), calls=%async_computation.30 | async-start | bytes 1966080 | tf_op jit(solution)/shard_map/all_gather | solution.py:329
  220.2 142.9 %all-gather.39.cloned.1.call-start = ((), (), s32[]{:S(2)}) async-start(), calls=%async_computation.31 | async-start | bytes 1327104 | tf_op jit(solution)/shard_map/all_gather | solution.py:93
  221.0 184.8 %all-gather.35.cloned.1.call-start = ((), (), s32[]{:S(2)}) async-start(), calls=%async_computation.29 | async-start | bytes 1327104 | tf_op jit(solution)/shard_map/all_gather | solution.py:92
  221.8 213.6 %all-gather.33.cloned.1.call-start = ((), (), s32[]{:S(2)}) async-start(), calls=%async_computation.28 | async-start | bytes 3932160 | tf_op jit(solution)/shard_map/all_gather | solution.py:111
  258.2 221.1 %all-gather.43.cloned.1.call-start = ((), (), s32[]{:S(2)}) async-start(), calls=%async_computation.33 | async-start | bytes 1327104 | tf_op jit(solution)/shard_map/all_gather | solution.py:95
  259.0 262.1 %reduce-scatter.39.cloned.1.call-start = ((), (), s32[]{:S(2)}) async-start(), calls=%async_computation.34 | async-start | bytes 3932160 | tf_op jit(solution)/shard_map/reduce_scatter | solution.py:119
  366.1 79.5 %copy-start.105 = (f32[128,3]{0,1:T(4,128)S(1)}, f32[128,3]{0,1:T(4,128)}, u32[]{:S(2)}) copy-start(f32[128,3]{0,1:T(4,128)} %reshape.407) | copy-start | bytes 4612
  484.2 67.4 %all-gather.51.cloned.1.call-start = ((), (), s32[]{:S(2)}) async-start(), calls=%async_computation.39 | async-start | bytes 3932160 | tf_op jit(solution)/shard_map/all_gather | solution.py:115
  486.4 176.2 %all-gather.49.cloned.1.call-start = ((), (), s32[]{:S(2)}) async-start(), calls=%async_computation.37 | async-start | bytes 7962624 | tf_op jit(solution)/shard_map/all_gather | solution.py:106
  488.9 282.7 %all-gather.47.cloned.1.call-start = ((), (), s32[]{:S(2)}) async-start(), calls=%async_computation.36 | async-start | bytes 7962624 | tf_op jit(solution)/shard_map/all_gather | solution.py:105
  491.5 308.8 %all-gather.45.cloned.1.call-start = ((), (), s32[]{:S(2)}) async-start(), calls=%async_computation.35 | async-start | bytes 3932160 | tf_op jit(solution)/shard_map/all_gather | solution.py:111
  524.6 347.4 %reduce-scatter.43.cloned.1.call-start = ((), (), s32[]{:S(2)}) async-start(), calls=%async_computation.40 | async-start | bytes 3932160 | tf_op jit(solution)/shard_map/reduce_scatter | solution.py:132
  833.9 78.8 %reduce-scatter.41.cloned.1.call-start = ((), (), s32[]{:S(2)}) async-start(), calls=%async_computation.38 | async-start | bytes 3932160 | tf_op jit(solution)/shard_map/reduce_scatter | solution.py:119
  848.1 99.1 %all-gather.53.cloned.1.call-start = ((), (), s32[]{:S(2)}) async-start(), calls=%async_computation.41 | async-start | bytes 3932160 | tf_op jit(solution)/shard_map/all_gather | solution.py:115
  918.5 151.0 %reduce-scatter.45.cloned.1.call-start = ((), (), s32[]{:S(2)}) async-start(), calls=%async_computation.42 | async-start | bytes 3932160 | tf_op jit(solution)/shard_map/reduce_scatter | solution.py:132
  1030.4 75.1 %all-gather.55.cloned.1.call-start = ((), (), s32[]{:S(2)}) async-start(), calls=%async_computation.43 | async-start | bytes 3932160 | tf_op jit(solution)/shard_map/all_gather | solution.py:115
  1076.8 222.8 %reduce-scatter.47.cloned.1.call-start = ((), (), s32[]{:S(2)}) async-start(), calls=%async_computation.44 | async-start | bytes 3932160 | tf_op jit(solution)/shard_map/reduce_scatter | solution.py:132
  1198.1 121.7 %reduce-scatter.79.cloned.1.call-start = ((), (), s32[]{:S(2)}) async-start(), calls=%async_computation.60 | async-start | bytes 36864
  1198.9 152.3 %reduce-scatter.77.cloned.1.call-start = ((), (), s32[]{:S(2)}) async-start(), calls=%async_computation.59 | async-start | bytes 36864
  1200.9 217.3 %reduce-scatter.75.cloned.1.call-start = ((), (), s32[]{:S(2)}) async-start(), calls=%async_computation.58 | async-start | bytes 1327104
  1204.6 279.9 %reduce-scatter.61.cloned.1.call-start = ((), (), s32[]{:S(2)}) async-start(), calls=%async_computation.51 | async-start | bytes 1327104 | tf_op jit(solution)/shard_map/reduce_scatter | solution.py:571
  1210.0 341.5 %reduce-scatter.59.cloned.1.call-start = ((), (), s32[]{:S(2)}) async-start(), calls=%async_computation.50 | async-start | bytes 1327104 | tf_op jit(solution)/shard_map/reduce_scatter | solution.py:562
  1214.8 468.3 %reduce-scatter.63.cloned.1.call-start = ((), (), s32[]{:S(2)}) async-start(), calls=%async_computation.52 | async-start | bytes 7962624 | tf_op jit(solution)/shard_map/reduce_scatter | solution.py:592
  1227.6 587.6 %reduce-scatter.65.cloned.1.call-start = ((), (), s32[]{:S(2)}) async-start(), calls=%async_computation.53 | async-start | bytes 7962624 | tf_op jit(solution)/shard_map/reduce_scatter | solution.py:595
  1241.7 629.8 %reduce-scatter.71.cloned.1.call-start = ((), (), s32[]{:S(2)}) async-start(), calls=%async_computation.56 | async-start | bytes 36864
  1243.1 684.7 %reduce-scatter.69.cloned.1.call-start = ((), (), s32[]{:S(2)}) async-start(), calls=%async_computation.55 | async-start | bytes 36864
  1246.3 747.8 %reduce-scatter.73.cloned.1.call-start = ((), (), s32[]{:S(2)}) async-start(), calls=%async_computation.57 | async-start | bytes 1327104
  1250.1 810.6 %reduce-scatter.57.cloned.1.call-start = ((), (), s32[]{:S(2)}) async-start(), calls=%async_computation.49 | async-start | bytes 1327104 | tf_op jit(solution)/shard_map/reduce_scatter | solution.py:547
  1255.2 871.8 %reduce-scatter.53.cloned.1.call-start = ((), (), s32[]{:S(2)}) async-start(), calls=%async_computation.47 | async-start | bytes 1327104 | tf_op jit(solution)/shard_map/reduce_scatter | solution.py:541
  1260.4 933.0 %reduce-scatter.51.cloned.1.call-start = ((), (), s32[]{:S(2)}) async-start(), calls=%async_computation.46 | async-start | bytes 1327104 | tf_op jit(solution)/shard_map/reduce_scatter | solution.py:538
  1265.2 994.4 %reduce-scatter.55.cloned.1.call-start = ((), (), s32[]{:S(2)}) async-start(), calls=%async_computation.48 | async-start | bytes 1327104 | tf_op jit(solution)/shard_map/reduce_scatter | solution.py:544
  1270.3 1053.1 %reduce-scatter.67.cloned.1.call-start = ((), (), s32[]{:S(2)}) async-start(), calls=%async_computation.54 | async-start | bytes 442368
  1315.2 1038.3 %reduce-scatter.49.cloned.1.call-start = ((), (), s32[]{:S(2)}) async-start(), calls=%async_computation.45 | async-start | bytes 1966080 | tf_op jit(solution)/shard_map/reduce_scatter | solution.py:443
  1817.7 443.6 %copy-start.82 = (bf16[6,1536]{1,0:T(8,128)(2,1)S(1)}, bf16[6,1536]{1,0:T(8,128)(2,1)}, u32[]{:S(2)}) copy-start(bf16[6,1536]{1,0:T(8,128)(2,1)} %copy-done.81) | copy-start | bytes 55300
  1817.7 444.3 %copy-start.151 = (bf16[192]{0:T(256)(128)(2,1)S(1)}, bf16[192]{0:T(256)(128)(2,1)}, u32[]{:S(2)}) copy-start(bf16[192]{0:T(256)(128)(2,1)} %get-tuple-element.598) | copy-start | bytes 1156
  1817.7 444.8 %copy-start.150 = (bf16[192]{0:T(256)(128)(2,1)S(1)}, bf16[192]{0:T(256)(128)(2,1)}, u32[]{:S(2)}) copy-start(bf16[192]{0:T(256)(128)(2,1)} %get-tuple-element.599) | copy-start | bytes 1156
  1817.7 445.4 %copy-start.136 = (f32[256]{0:T(256)S(1)}, f32[256]{0:T(256)}, u32[]{:S(2)}) copy-start(f32[256]{0:T(256)} %get-tuple-element.511) | copy-start | bytes 3076
  1817.7 445.4 %copy-start.26 = (f32[256,1536]{1,0:T(8,128)S(1)}, f32[256,1536]{1,0:T(8,128)}, u32[]{:S(2)}) copy-start(f32[256,1536]{1,0:T(8,128)} %copy-done.25) | copy-start | bytes 4718596
  1817.7 445.4 %copy-start.126 = (f32[256]{0:T(256)S(1)}, f32[256]{0:T(256)}, u32[]{:S(2)}) copy-start(f32[256]{0:T(256)} %copy-done.125) | copy-start | bytes 3076
  (152 other events, 1156.3 us)
Sparse Core Ops, SparseCore 0:
  10.8 43.7 all-gather.24
  56.7 27.3 all-gather.22
  86.8 41.0 all-gather.26
  130.5 39.8 all-gather.28
  173.0 39.8 all-gather.30
  218.0 36.7 reduce-scatter.36
  257.8 41.1 all-gather.40
  300.6 18.4 all-gather.36
  322.0 41.0 all-gather.38
  366.0 39.8 all-gather.34
  408.0 27.2 all-gather.32
  438.2 41.0 all-gather.42
  484.3 36.7 reduce-scatter.38
  523.1 28.5 all-gather.50
  553.7 108.7 all-gather.48
  664.6 106.9 all-gather.46
  773.6 26.7 all-gather.44
  834.0 37.9 reduce-scatter.42
  874.7 37.9 reduce-scatter.40
  918.6 28.5 all-gather.52
  1030.5 38.9 reduce-scatter.44
  1076.9 28.5 all-gather.54
  1198.2 39.5 reduce-scatter.46
  1241.4 53.5 reduce-scatter.78
  1298.6 52.5 reduce-scatter.76
  1355.0 63.1 reduce-scatter.74
  1421.4 62.9 reduce-scatter.60
  1488.4 62.9 reduce-scatter.58
  1555.1 127.9 reduce-scatter.62
  1687.1 128.0 reduce-scatter.64
  1818.9 52.5 reduce-scatter.70
  1875.2 52.5 reduce-scatter.68
  1931.0 63.0 reduce-scatter.72
  1997.5 63.1 reduce-scatter.56
  2064.0 62.9 reduce-scatter.52
  2130.3 63.0 reduce-scatter.50
  2196.6 62.9 reduce-scatter.54
  2262.9 60.4 reduce-scatter.66
  2326.3 27.1 reduce-scatter.48
where the time goes:
time: 2370 us; the launch traced here: 2360 us
  waiting for transfers between devices  1660 us (70%)
  matrix products  243 us (10%)
  blocking collectives  187 us (8%)
  local copies, waits for them, and re-layouts  138 us (6%)
  other arithmetic  109 us (5%)
    unnamed x46, waiting for transfers between devices  330 us
    reduce_scatter x1, waiting for transfers between devices, on_device(): lax.psum_scatter(ffn_up_grad.astype(jnp.bfloat16), 'dp', scatter_dimensio...  130 us
    reduce_scatter x1, waiting for transfers between devices, on_device(): lax.psum_scatter(ffn_down_grad.astype(jnp.bfloat16), 'dp', scatter_dimens...  130 us
    all_gather x1, waiting for transfers between devices, fetch_ffn(): lax.all_gather(ffn_down.astype(jnp.bfloat16), 'dp', axis=1, tiled=True)  111 us
    all_gather x1, waiting for transfers between devices, fetch_ffn(): lax.all_gather(ffn_up.astype(jnp.bfloat16), 'dp', axis=0, tiled=True)  95.8 us
    all_gather x3, waiting for transfers between devices, gather_grads(): return lax.all_gather(values, 'tensor', axis=0, tiled=True)  83 us
    reduce_scatter x3, waiting for transfers between devices, branch_sum(): lax.psum_scatter(jnp.dot(left_side, right_side, preferred_element_type=jn...  78.1 us
    reduce_scatter x1, waiting for transfers between devices, on_device(): lax.psum_scatter(cross_query_grad.astype(jnp.bfloat16), 'dp', scatter_dim...  65.4 us
  transfers between devices with their start and end apart: 39, of which 35 were waited for; matrix products, arithmetic and copies ran while one was open for 11% of the time, Pallas kernels for 0%

commit v1 on v0

v1 whole, which is shorter than its diff:
```python
import math

import jax
import jax.numpy as jnp
from jax import lax
from jax.sharding import PartitionSpec as P

D = 1536
HEAD = 128
EPS = 1e-6
BF = jnp.bfloat16
F32 = jnp.float32


def dot(a, b):
    return jnp.dot(a, b, preferred_element_type=F32)


def dot_nt(a, b):
    return lax.dot_general(a, b, (((1,), (1,)), ((), ())), preferred_element_type=F32)


def dot_tn(a, b):
    return lax.dot_general(a, b, (((0,), (0,)), ((), ())), preferred_element_type=F32)


def rotary_tables(positions, head_dim):
    pair_count = head_dim // 2
    side_pairs = pair_count // 3
    frame_pairs = pair_count - 2 * side_pairs
    pair_index = jnp.arange(pair_count)
    frame_mask = pair_index < frame_pairs
    height_mask = (pair_index >= frame_pairs) & (pair_index < frame_pairs + side_pairs)
    within = jnp.where(
        frame_mask,
        pair_index,
        jnp.where(height_mask, pair_index - frame_pairs, pair_index - frame_pairs - side_pairs),
    )
    extent = jnp.where(frame_mask, frame_pairs, side_pairs)
    frequency = jnp.power(10000.0, -within.astype(F32) / extent.astype(F32))
    coords = positions.astype(F32)
    coordinate = jnp.where(
        frame_mask[None, :],
        coords[0][:, None],
        jnp.where(height_mask[None, :], coords[1][:, None], coords[2][:, None]),
    )
    angles = jnp.repeat(coordinate * frequency[None, :], 2, axis=1)
    parity = jnp.arange(head_dim) % 2
    sign_pattern = jnp.where(parity == 0, -1.0, 1.0)
    return (jnp.cos(angles), jnp.sin(angles) * sign_pattern)


def rotate(values, cosine, sine_signed):
    next_lane = jnp.roll(values, -1, axis=-1)
    last_lane = jnp.roll(values, 1, axis=-1)
    parity = jnp.arange(values.shape[-1]) % 2
    partner = jnp.where(parity == 0, next_lane, last_lane)
    return values * cosine[:, None, :] + partner * sine_signed[:, None, :]


def norm_stats(v):
    center = v - jnp.mean(v, axis=-1, keepdims=True)
    r = lax.rsqrt(jnp.mean(center * center, axis=-1, keepdims=True) + EPS)
    return center * r, r


def norm_back(n, r, da, m):
    dn = da * m
    return r * (
        dn - jnp.mean(dn, axis=-1, keepdims=True) - n * jnp.mean(dn * n, axis=-1, keepdims=True)
    )


def attend_forward(q, k, v, bias, factor):
    s = jnp.einsum("qhd,khd->hqk", q, k, preferred_element_type=F32) * factor + bias
    top = jnp.max(s, axis=-1, keepdims=True)
    e = jnp.exp(s - top)
    total = jnp.sum(e, axis=-1, keepdims=True)
    p = (e / total).astype(BF)
    o = jnp.einsum("hqk,khd->qhd", p, v, preferred_element_type=F32)
    return o.astype(BF).reshape(q.shape[0], -1), top + jnp.log(total)


def attend_backward(q, k, v, bias, lse, do, factor):
    s = jnp.einsum("qhd,khd->hqk", q, k, preferred_element_type=F32) * factor + bias
    p = jnp.exp(s - lse)
    dp = jnp.einsum("qhd,khd->hqk", do, v, preferred_element_type=F32)
    ds = (p * (dp - jnp.sum(p * dp, axis=-1, keepdims=True))).astype(BF)
    dq = jnp.einsum("hqk,khd->qhd", ds, k, preferred_element_type=F32) * factor
    dk = jnp.einsum("hqk,qhd->khd", ds, q, preferred_element_type=F32) * factor
    dv = jnp.einsum("hqk,qhd->khd", p.astype(BF), do, preferred_element_type=F32)
    return (
        dq.reshape(q.shape[0], -1),
        dk.reshape(k.shape[0], -1),
        dv.reshape(k.shape[0], -1),
    )


def solution(mesh):
    n_dp = mesh.shape["dp"]
    n_major = n_dp // 2
    pair_perm = [(i, i ^ 1) for i in range(n_dp)]
    ring_perm = {
        t: [((((i // 2) + t) % n_major) * 2 + i % 2, i) for i in range(n_dp)]
        for t in range(1, n_major)
    }
    back_perm = {t: [(b, a) for a, b in ring_perm[t]] for t in ring_perm}
    core_perm = [(i, i ^ 1) for i in range(4)]
    x_perm = [(i, i ^ 2) for i in range(4)]

    def core_swap(v):
        return lax.ppermute(v, "tensor", core_perm)

    def x_swap(v):
        return lax.ppermute(v, "tensor", x_perm)

    def gather_dp(block):
        d = lax.axis_index("dp")
        major, minor = d // 2, d % 2
        out = jnp.zeros((n_dp,) + block.shape, block.dtype)
        for t in range(n_major):
            piece = block if t == 0 else lax.ppermute(block, "dp", ring_perm[t])
            other = lax.ppermute(piece, "dp", pair_perm)
            origin = 2 * ((major + t) % n_major)
            out = lax.dynamic_update_slice(out, piece[None], (origin + minor, 0, 0))
            out = lax.dynamic_update_slice(out, other[None], (origin + 1 - minor, 0, 0))
        return out

    def scatter_dp(full):
        d = lax.axis_index("dp")
        major, minor = d // 2, d % 2
        r, c = full.shape[1:]
        low = full.astype(BF).reshape(n_major, 2, r, c)
        theirs = lax.dynamic_slice_in_dim(low, 1 - minor, 1, axis=1)[:, 0]
        mine = lax.dynamic_slice_in_dim(low, minor, 1, axis=1)[:, 0]
        got = lax.ppermute(theirs, "dp", pair_perm)
        pair = (mine.astype(F32) + got.astype(F32)).astype(BF)
        total = lax.dynamic_slice_in_dim(pair, major, 1, axis=0)[0].astype(F32)
        for t in range(1, n_major):
            send = lax.dynamic_slice_in_dim(pair, (major + t) % n_major, 1, axis=0)[0]
            total = total + lax.ppermute(send, "dp", back_perm[t]).astype(F32)
        return total

    def sum_rows(theirs, mine):
        chip = (mine + core_swap(theirs.astype(BF)).astype(F32)).astype(BF)
        h = chip.shape[0] // 2
        r0 = x_swap(chip[h:])
        r1 = x_swap(chip[:h])
        return chip.astype(F32) + jnp.concatenate([r0, r1]).astype(F32)

    def sum_quarter(theirs, mine):
        chip = (mine + core_swap(theirs.astype(BF)).astype(F32)).astype(BF)
        h = chip.shape[0] // 2
        return chip[:h].astype(F32) + x_swap(chip[h:]).astype(F32)

    def sum_all(v):
        v = v + core_swap(v)
        return v + x_swap(v)

    def sum_vectors(v):
        h = v.shape[-1] // 2
        other = core_swap(v)
        v = v + jnp.concatenate([other[..., h:], other[..., :h]], -1)
        split = v.shape[:-1] + (2, 2, h // 2)
        return v + x_swap(v).reshape(split)[..., ::-1, :].reshape(v.shape)

    def rows_all(mine):
        return jnp.concatenate([mine, core_swap(mine)])

    def quarters(values, axis):
        t = lax.axis_index("tensor")
        step = values.shape[axis] // 4
        return jnp.concatenate(
            [
                lax.dynamic_slice_in_dim(values, (t ^ flip) * step, step, axis)
                for flip in (0, 2, 1, 3)
            ],
            axis,
        )

    def on_device(
        hidden_in, context, time_emb, text_lengths, positions, modulation,
        self_query, self_key, self_value, self_output, self_query_gain, self_key_gain,
        cross_query, cross_key, cross_value, cross_output, cross_query_gain, cross_key_gain,
        norm_weight, norm_bias, ffn_up, ffn_down, out_cotangent,
    ):
        factor = 1.0 / math.sqrt(HEAD)
        heads = self_query_gain.shape[0]
        clip_rows = positions.shape[1]
        half = clip_rows // 2
        quarter = clip_rows // 4
        wide = heads * HEAD
        r_dp = self_query.shape[0]
        hid = ffn_up.shape[1]

        gains = [self_query_gain, self_key_gain, cross_query_gain, cross_key_gain]
        small = jnp.concatenate(
            [modulation.reshape(-1), norm_weight, norm_bias] + [g.reshape(-1) for g in gains]
        ).astype(BF)
        pad = -small.shape[0] % 1024
        small_all = gather_dp(jnp.pad(small, (0, pad)).reshape(8, -1)).reshape(n_dp, -1).astype(F32)
        mods = small_all[:, : 6 * r_dp].reshape(n_dp, 6, r_dp).transpose(1, 0, 2).reshape(6, D)
        at = 6 * r_dp
        norm_gain = small_all[:, at : at + r_dp].reshape(D)
        norm_shift = small_all[:, at + r_dp : at + 2 * r_dp].reshape(D)
        at += 2 * r_dp
        g_cols = self_query_gain.shape[1]
        g_rows = []
        for i in range(4):
            g = small_all[:, at + i * heads * g_cols : at + (i + 1) * heads * g_cols]
            g_rows.append(g.reshape(n_dp, heads, g_cols).transpose(1, 0, 2).reshape(wide))
        sq_gain, sk_gain, cq_gain, ck_gain = g_rows
        shifts = mods + time_emb[0]

        w_qkv = gather_dp(
            jnp.concatenate([self_query, self_key, self_value], axis=1).astype(BF)
        ).reshape(D, 3 * wide)
        w_oT = gather_dp(self_output.T.astype(BF)).reshape(D, wide)
        w_cross = gather_dp(
            jnp.concatenate([cross_query, cross_key, cross_value, cross_output.T], axis=1).astype(BF)
        ).reshape(D, 4 * wide)
        w_cq, w_ckv, w_coT = w_cross[:, :wide], w_cross[:, wide : 3 * wide], w_cross[:, 3 * wide :]
        w_downT = gather_dp(ffn_down.T.astype(BF)).reshape(D, hid)
        w_up = gather_dp(ffn_up.astype(BF)).reshape(D, hid)

        res = jnp.concatenate([hidden_in, x_swap(hidden_in)]).astype(F32)
        g = jnp.concatenate([out_cotangent, x_swap(out_cotangent)]).astype(F32)
        ctx = context[0]
        ctx = rows_all(jnp.concatenate([ctx, x_swap(ctx)]))
        texts = ctx.shape[0]
        cosine, sine = rotary_tables(quarters(positions, 1), HEAD)
        text_bias = jnp.where(quarters(jnp.arange(texts), 0) < text_lengths[0], 0.0, -1e30)
        open_bias = jnp.zeros((clip_rows,), F32)

        def heads_of(v):
            return v.reshape(v.shape[0], heads, HEAD)

        n_self, r_self = norm_stats(res)
        self_rows = rows_all((n_self * (1.0 + shifts[1]) + shifts[0]).astype(BF))
        qkv = dot(self_rows, w_qkv)
        q_raw, k_raw, v_raw = qkv[:, :wide], qkv[:, wide : 2 * wide], qkv[:, 2 * wide :]
        sums = sum_vectors(jnp.stack([jnp.sum(q_raw * q_raw, 1), jnp.sum(k_raw * k_raw, 1)]))
        scales = lax.rsqrt(sums / D + EPS)
        q_s, k_s = scales[0][:, None], scales[1][:, None]
        q = rotate(heads_of(q_raw * q_s * sq_gain), cosine, sine).astype(BF)
        k = rotate(heads_of(k_raw * k_s * sk_gain), cosine, sine).astype(BF)
        v = heads_of(v_raw.astype(BF))
        attn, lse = attend_forward(q, k, v, open_bias, factor)
        branch = dot_nt(attn, w_oT)
        self_branch = sum_rows(branch[half:], branch[:half])
        after_self = res + self_branch * shifts[2]

        ckv = dot(ctx, w_ckv)
        ck_raw, cv_raw = ckv[:, :wide], ckv[:, wide:]
        n_cross, r_cross = norm_stats(after_self)
        cross_rows = rows_all((n_cross * norm_gain + norm_shift).astype(BF))
        cq_raw = dot(cross_rows, w_cq)
        ck_s = lax.rsqrt(sum_vectors(jnp.sum(ck_raw * ck_raw, 1)) / D + EPS)[:, None]
        cq_s = lax.rsqrt(sum_vectors(jnp.sum(cq_raw * cq_raw, 1)) / D + EPS)[:, None]
        cq = heads_of((cq_raw * cq_s * cq_gain).astype(BF))
        ck = heads_of((ck_raw * ck_s * ck_gain).astype(BF))
        cv = heads_of(cv_raw.astype(BF))
        cattn, clse = attend_forward(cq, ck, cv, text_bias, factor)
        cbranch = dot_nt(cattn, w_coT)
        after_cross = after_self + sum_rows(cbranch[half:], cbranch[:half])

        dffn = rows_all((g * shifts[5]).astype(BF))
        dact = dot(dffn, w_downT)
        n_ffn, r_ffn = norm_stats(after_cross)
        ffn_rows = rows_all((n_ffn * (1.0 + shifts[4]) + shifts[3]).astype(BF))
        pre = dot(ffn_rows, w_up)
        c0 = math.sqrt(2.0 / math.pi)
        th = jnp.tanh(c0 * (pre + 0.044715 * pre * pre * pre))
        act = (0.5 * pre * (1.0 + th)).astype(BF)
        slope = 0.5 * (1.0 + th) + 0.5 * pre * (1.0 - th * th) * c0 * (1.0 + 3 * 0.044715 * pre * pre)
        dpre = (dact * slope).astype(BF)
        dffn_part = dot_nt(dpre, w_up)
        dffn_in = sum_rows(dffn_part[half:], dffn_part[:half])
        g_c = g + norm_back(n_ffn, r_ffn, dffn_in, 1.0 + shifts[4])
        ffn_part = dot_nt(act, w_downT)
        ffn_branch = sum_quarter(ffn_part[half:], ffn_part[:half])
        block_out = (after_cross[:quarter] + ffn_branch * shifts[5]).astype(BF)
        downT_grad = scatter_dp(dot_tn(dffn, act).reshape(n_dp, r_dp, hid))
        up_grad = scatter_dp(dot_tn(ffn_rows, dpre).reshape(n_dp, r_dp, hid))

        dcross = rows_all(g_c.astype(BF))
        dcattn = dot(dcross, w_coT).astype(BF)
        dcq, dck, dcv = attend_backward(cq, ck, cv, text_bias, clse, heads_of(dcattn), factor)
        dots_q = sum_vectors(jnp.sum(cq_raw * cq_gain * dcq, 1))[:, None]
        dots_k = sum_vectors(jnp.sum(ck_raw * ck_gain * dck, 1))[:, None]
        dcq_raw = (cq_s * cq_gain * dcq - cq_raw * (cq_s**3 * dots_q / D)).astype(BF)
        dck_raw = (ck_s * ck_gain * dck - ck_raw * (ck_s**3 * dots_k / D)).astype(BF)
        cq_gain_grad = jnp.sum(cq_raw * cq_s * dcq, 0)
        ck_gain_grad = jnp.sum(ck_raw * ck_s * dck, 0)
        dckv = jnp.concatenate([dck_raw, dcv.astype(BF)], axis=1)
        dcross_part = dot_nt(dcq_raw, w_cq)
        dcross_in = sum_rows(dcross_part[half:], dcross_part[:half])
        g_s = g_c + norm_back(n_cross, r_cross, dcross_in, norm_gain)
        dctx = dot_nt(dckv, w_ckv)
        th2 = texts // 2
        context_grad = sum_quarter(dctx[th2:], dctx[:th2]).astype(BF)
        cross_grad = scatter_dp(
            jnp.concatenate(
                [dot_tn(cross_rows, dcq_raw), dot_tn(ctx, dckv), dot_tn(dcross, cattn)], axis=1
            ).reshape(n_dp, r_dp, 4 * wide)
        )

        dself = rows_all((g_s * shifts[2]).astype(BF))
        dattn = dot(dself, w_oT).astype(BF)
        oT_grad = scatter_dp(dot_tn(dself, attn).reshape(n_dp, r_dp, wide))
        dq, dk, dv = attend_backward(q, k, v, open_bias, lse, heads_of(dattn), factor)
        dq = rotate(heads_of(dq), cosine, -sine).reshape(clip_rows, wide)
        dk = rotate(heads_of(dk), cosine, -sine).reshape(clip_rows, wide)
        dots = sum_vectors(
            jnp.stack([jnp.sum(q_raw * sq_gain * dq, 1), jnp.sum(k_raw * sk_gain * dk, 1)])
        )
        dq_raw = (q_s * sq_gain * dq - q_raw * (q_s**3 * dots[0][:, None] / D)).astype(BF)
        dk_raw = (k_s * sk_gain * dk - k_raw * (k_s**3 * dots[1][:, None] / D)).astype(BF)
        sq_gain_grad = jnp.sum(q_raw * q_s * dq, 0)
        sk_gain_grad = jnp.sum(k_raw * k_s * dk, 0)
        dqkv = jnp.concatenate([dq_raw, dk_raw, dv.astype(BF)], axis=1)
        dself_part = dot_nt(dqkv, w_qkv)
        qkv_grad = scatter_dp(dot_tn(self_rows, dqkv).reshape(n_dp, r_dp, 3 * wide))
        dself_in = sum_quarter(dself_part[half:], dself_part[:half])
        n_q, r_q = n_self[:quarter], r_self[:quarter]
        hidden_grad = (
            g_s[:quarter] + norm_back(n_q, r_q, dself_in, 1.0 + shifts[1])
        ).astype(BF)

        da3, da2 = dffn_in[:quarter], dcross_in[:quarter]
        sums_own = jnp.stack(
            [
                jnp.sum(dself_in, 0),
                jnp.sum(dself_in * n_q, 0),
                jnp.sum(g_s[:quarter] * self_branch[:quarter], 0),
                jnp.sum(da3, 0),
                jnp.sum(da3 * n_ffn[:quarter], 0),
                jnp.sum(g[:quarter] * ffn_branch, 0),
                jnp.sum(da2 * n_cross[:quarter], 0),
                jnp.sum(da2, 0),
            ]
        )
        sums_clip = sum_all(sums_own)
        time_grad = sums_clip[:6]
        low_sums = sums_clip.reshape(8, n_dp, r_dp).transpose(1, 0, 2).reshape(n_dp, -1)
        gain_grads = jnp.stack([sq_gain_grad, sk_gain_grad, cq_gain_grad, ck_gain_grad])
        low_gains = gain_grads.reshape(4 * heads, n_dp, g_cols).transpose(1, 0, 2).reshape(n_dp, -1)
        packed = jnp.concatenate([low_sums, low_gains], axis=1)
        packed = jnp.pad(packed, ((0, 0), (0, pad))).reshape(n_dp, 8, -1)
        tiny = scatter_dp(packed).reshape(-1)
        eight = tiny[: 8 * r_dp].reshape(8, r_dp)
        gains_out = tiny[8 * r_dp : 8 * r_dp + 4 * heads * g_cols].reshape(4, heads, g_cols)

        return (
            block_out,
            hidden_grad,
            context_grad[None],
            time_grad[None],
            eight[:6],
            qkv_grad[:, :wide],
            qkv_grad[:, wide : 2 * wide],
            qkv_grad[:, 2 * wide :],
            oT_grad.T,
            gains_out[0],
            gains_out[1],
            cross_grad[:, :wide],
            cross_grad[:, wide : 2 * wide],
            cross_grad[:, 2 * wide : 3 * wide],
            cross_grad[:, 3 * wide :].T,
            gains_out[2],
            gains_out[3],
            eight[6],
            eight[7],
            up_grad,
            downT_grad.T,
        )

    rows = P(("dp", "tensor"), None)
    col = P("dp", "tensor")
    row = P("tensor", "dp")
    text = P("dp", "tensor", None)
    time = P("dp", None, None)
    one = P("dp")
    ins = (
        rows, text, time, one, P(None, "dp"), P(None, "dp"),
        col, col, col, row, row, row,
        col, col, col, row, row, row,
        one, one, col, row, rows,
    )
    outs = (
        rows, rows, text, time, P(None, "dp"),
        col, col, col, row, row, row,
        col, col, col, row, row, row,
        one, one, col, row,
    )
    return jax.shard_map(on_device, mesh=mesh, in_specs=ins, out_specs=outs, check_vma=False)
```

time: 2370 us -> 1080 us (0.46)
  waiting for transfers between devices: 1660 us -> 461 us
  blocking collectives: 187 us -> 0 us
  starting transfers between devices: 2.58 us -> 128 us
  matrix products: 243 us -> 172 us
  local copies, waits for them, and re-layouts: 138 us -> 170 us
  other arithmetic: 109 us -> 138 us
    reduce_scatter x15 -> x0, waiting for transfers between devices: 818 us -> none  [the longest x1 130 us: on_device(): lax.psum_scatter(ffn_up_grad.astype(jnp.bfloat16), 'dp', scatter_dimensio...]
    all_gather x17 -> x0, waiting for transfers between devices: 514 us -> none  [the longest x1 111 us: fetch_ffn(): lax.all_gather(ffn_down.astype(jnp.bfloat16), 'dp', axis=1, tiled=True)]
    ppermute x0 -> x108, waiting for transfers between devices: none -> 461 us  [the longest x18 113 us: scatter_dp(): total = total + lax.ppermute(send, 'dp', back_perm[t]).astype(F32)]
    unnamed x46 -> x0, waiting for transfers between devices: 330 us -> none
    ppermute x0 -> x108, starting transfers between devices: none -> 128 us  [the longest x18 47.5 us: gather_dp(): piece = block if t == 0 else lax.ppermute(block, 'dp', ring_perm[t])]
    all_gather x5 -> x0, blocking collectives: 106 us -> none  [the longest x1 32.3 us: fetch_self(): lax.all_gather(modulation.astype(jnp.bfloat16), 'dp', axis=1, tiled=True)]
    dot_general x58 -> x33, matrix products: 243 us -> 172 us  [the longest x7 50.7 us: dot(): return jnp.dot(a, b, preferred_element_type=F32)]
    unnamed x2 -> x0, blocking collectives: 41.4 us -> none
  transfers between devices with their start and end apart: 39 -> 108, of which waited for: 35 -> 40; matrix products, arithmetic and copies ran while one was open for 11% -> 38% of each run, Pallas kernels for 0% -> 0%
where the time goes in v1:
time: 1080 us; the launch traced here: 1070 us
  waiting for transfers between devices  461 us (43%)
  matrix products  172 us (16%)
  local copies, waits for them, and re-layouts  170 us (16%)
  other arithmetic  138 us (13%)
  starting transfers between devices  128 us (12%)
    ppermute x18, waiting for transfers between devices, scatter_dp(): total = total + lax.ppermute(send, 'dp', back_perm[t]).astype(F32)  113 us
    ppermute x24, waiting for transfers between devices, gather_dp(): other = lax.ppermute(piece, 'dp', pair_perm)  104 us
    ppermute x6, waiting for transfers between devices, scatter_dp(): got = lax.ppermute(theirs, 'dp', pair_perm)  101 us
    ppermute x21, waiting for transfers between devices, x_swap(): return lax.ppermute(v, 'tensor', x_perm)  94.5 us
    dot_general x7, matrix products, dot(): return jnp.dot(a, b, preferred_element_type=F32)  50.7 us
    ppermute x18, starting transfers between devices, gather_dp(): piece = block if t == 0 else lax.ppermute(block, 'dp', ring_perm[t])  47.5 us
    ppermute x18, waiting for transfers between devices, gather_dp(): piece = block if t == 0 else lax.ppermute(block, 'dp', ring_perm[t])  46.3 us
    dot_general x7, matrix products, dot_nt(): lax.dot_general(a, b, (((1,), (1,)), ((), ())), preferred_element_type=F32)  46.3 us
  transfers between devices with their start and end apart: 108, of which 40 were waited for; matrix products, arithmetic and copies ran while one was open for 38% of the time, Pallas kernels for 0%

profile of v1, /device:TPU:0, one launch (start us, length us, event | category | flops | bytes accessed | tf_op | source)
XLA Modules:
  0.0 1072.8 jit_solution(1239098729352570321)
XLA Ops:
  78.2 5.4 collective-permute-done.20
  90.0 6.2 collective-permute-done.24
  98.2 11.1 %collective-permute-done.9 = bf16[192,1152]{1,0:T(8,128)(2,1)S(1)} collective-permute-done((bf16[192,1152]{1,0:T(8,128)(2,1)}, bf16[192,1152]{1,0:T(8,128)(2,1)S(1)}, u32[]{:S(2)}, u32[]{:S(2)}) %collective-permute-start.9) | collective-permute-done | bytes 442400 | tf_op jit(solution)/shard_map/ppermute | solution.py:123
  111.9 7.2 collective-permute-done.30
  121.5 14.0 %collective-permute-done.31 = bf16[192,1536]{1,0:T(8,128)(2,1)S(1)} collective-permute-done((bf16[192,1536]{1,0:T(8,128)(2,1)S(1)}, bf16[192,1536]{1,0:T(8,128)(2,1)S(1)}, u32[]{:S(2)}, u32[]{:S(2)}) %collective-permute-start.31) | collective-permute-done | bytes 589856 | tf_op jit(solution)/shard_map/ppermute | solution.py:122
  142.7 11.8 %collective-permute-done.62 = bf16[256,1536]{1,0:T(8,128)(2,1)S(1)} collective-permute-done((bf16[256,1536]{1,0:T(8,128)(2,1)S(1)}, bf16[256,1536]{1,0:T(8,128)(2,1)S(1)}, u32[]{:S(2)}, u32[]{:S(2)}) %collective-permute-start.62) | collective-permute-done | bytes 786464 | tf_op jit(solution)/shard_map/ppermute | solution.py:115
  154.5 15.0 %collective-permute-start.54 = (bf16[192,2240]{1,0:T(8,128)(2,1)}, bf16[192,2240]{1,0:T(8,128)(2,1)}, u32[]{:S(2)}, u32[]{:S(2)}) collective-permute-start(bf16[192,2240]{1,0:T(8,128)(2,1)} %convert_bitcast_fusion), channel_id=1, source_target_pairs={{8,0},{12,4},{16,8},{20,12},{24,16},{28,20},{0,24},{4,28},{9,1},{1... | collective-permute-start | bytes 2580488 | tf_op jit(solution)/shard_map/ppermute | solution.py:122
  176.8 13.2 %collective-permute-done.54 = bf16[192,2240]{1,0:T(8,128)(2,1)} collective-permute-done((bf16[192,2240]{1,0:T(8,128)(2,1)}, bf16[192,2240]{1,0:T(8,128)(2,1)}, u32[]{:S(2)}, u32[]{:S(2)}) %collective-permute-start.54) | collective-permute-done | bytes 860192 | tf_op jit(solution)/shard_map/ppermute | solution.py:122
  195.4 13.6 %collective-permute-start.56 = (bf16[192,2240]{1,0:T(8,128)(2,1)}, bf16[192,2240]{1,0:T(8,128)(2,1)}, u32[]{:S(2)}, u32[]{:S(2)}) collective-permute-start(bf16[192,2240]{1,0:T(8,128)(2,1)} %convert_bitcast_fusion), channel_id=1, source_target_pairs={{16,0},{20,4},{24,8},{28,12},{0,16},{4,20},{8,24},{12,28},{17,1},{... | collective-permute-start | bytes 2580488 | tf_op jit(solution)/shard_map/ppermute | solution.py:122
  212.2 9.2 collective-permute-done.15
  225.6 6.2 fusion.42
  232.3 4.8 collective-permute-done.32
  238.4 16.4 %collective-permute-done.33 = bf16[192,1536]{1,0:T(8,128)(2,1)} collective-permute-done((bf16[192,1536]{1,0:T(8,128)(2,1)S(1)}, bf16[192,1536]{1,0:T(8,128)(2,1)}, u32[]{:S(2)}, u32[]{:S(2)}) %collective-permute-start.33) | collective-permute-done | bytes 589856 | tf_op jit(solution)/shard_map/ppermute | solution.py:122
  299.9 13.6 %collective-permute-done.46 = bf16[192,2240]{1,0:T(8,128)(2,1)S(1)} collective-permute-done((bf16[192,2240]{1,0:T(8,128)(2,1)S(1)}, bf16[192,2240]{1,0:T(8,128)(2,1)S(1)}, u32[]{:S(2)}, u32[]{:S(2)}) %collective-permute-start.46) | collective-permute-done | bytes 860192 | tf_op jit(solution)/shard_map/ppermute | solution.py:123
  320.2 16.0 %collective-permute-done.27 = bf16[256,1536]{1,0:T(8,128)(2,1)S(1)} collective-permute-done((bf16[256,1536]{1,0:T(8,128)(2,1)S(1)}, bf16[256,1536]{1,0:T(8,128)(2,1)S(1)}, u32[]{:S(2)}, u32[]{:S(2)}) %collective-permute-start.27) | collective-permute-done | bytes 786464 | tf_op jit(solution)/shard_map/ppermute | solution.py:115
  340.1 4.2 add_convert_fusion.1
  355.6 4.8 multiply_reduce_fusion.15
  363.0 12.2 %collective-permute-done.57 = bf16[192,2240]{1,0:T(8,128)(2,1)S(1)} collective-permute-done((bf16[192,2240]{1,0:T(8,128)(2,1)}, bf16[192,2240]{1,0:T(8,128)(2,1)S(1)}, u32[]{:S(2)}, u32[]{:S(2)}) %collective-permute-start.57) | collective-permute-done | bytes 860192 | tf_op jit(solution)/shard_map/ppermute | solution.py:123
  409.8 31.6 %collective-permute-done.50 = bf16[192,2240]{1,0:T(8,128)(2,1)S(1)} collective-permute-done((bf16[192,2240]{1,0:T(8,128)(2,1)}, bf16[192,2240]{1,0:T(8,128)(2,1)S(1)}, u32[]{:S(2)}, u32[]{:S(2)}) %collective-permute-start.50) | collective-permute-done | bytes 860192 | tf_op jit(solution)/shard_map/ppermute | solution.py:123
  446.0 13.2 %collective-permute-done.44 = bf16[256,1536]{1,0:T(8,128)(2,1)S(1)} collective-permute-done((bf16[256,1536]{1,0:T(8,128)(2,1)S(1)}, bf16[256,1536]{1,0:T(8,128)(2,1)S(1)}, u32[]{:S(2)}, u32[]{:S(2)}) %collective-permute-start.44) | collective-permute-done | bytes 786464 | tf_op jit(solution)/shard_map/ppermute | solution.py:115
  465.7 10.7 fusion.40
  476.5 16.6 %fusion.143 = f32[1024,1536]{1,0:T(8,128)} fusion(bf16[1536,2240]{1,0:T(8,128)(2,1)} %bitcast.87, f32[1024,2240]{0,1:T(8,128)S(1)} %fusion.40), kind=kOutput, calls=%fused_computation.398 | convolution fusion | flops 7067074560 | bytes 22347776 | tf_op jit(solution)/shard_map/dot_general | solution.py:20
  493.1 19.5 %fusion.7 = bf16[1024,2240]{0,1:T(8,128)(2,1)} fusion(f32[1024,2240]{0,1:T(8,128)} %copy-done.156, bf16[1536,2240]{1,0:T(8,128)(2,1)} %bitcast.87, bf16[512,1536]{1,0:T(8,128)(2,1)} %collective-permute-done.63, bf16[512,1536]{1,0:T(8,128)(2,1)} %multiply_convert_fusion.4), kind=kOutput, calls=%fused_computation.17 | convolution fusion | flops 7096303616 | bytes 23789568 | tf_op jit(solution)/shard_map/dot_general | solution.py:16
  512.6 11.4 %fusion.176 = f32[1024,1536]{1,0:T(8,128)S(1)} fusion(bf16[1024,2240]{0,1:T(8,128)(2,1)} %fusion.7, bf16[1536,2240]{1,0:T(8,128)(2,1)} %bitcast.77), kind=kOutput, calls=%fused_computation.431 | convolution fusion | flops 7046430720 | bytes 17760256 | tf_op jit(solution)/shard_map/dot_general | solution.py:20
  532.0 12.3 %convolution_convert_fusion = bf16[1536,2240]{0,1:T(8,128)(2,1)} fusion(bf16[512,1536]{1,0:T(8,128)(2,1)} %collective-permute-done.63, bf16[512,1536]{1,0:T(8,128)(2,1)} %multiply_convert_fusion.4, f32[1024,2240]{0,1:T(8,128)S(1)} %copy-done.157), kind=kOutput, calls=%fused_computation.7 | convolution fusion | flops 7076806656 | bytes 19202048 | tf_op jit(solution)/shard_map/dot_general | solution.py:24
  544.3 9.5 convolution_convert_fusion.1
  553.8 9.7 copy.191
  563.5 9.8 copy.192
  586.9 14.0 %collective-permute-done.61 = bf16[256,1536]{1,0:T(8,128)(2,1)} collective-permute-done((bf16[256,1536]{1,0:T(8,128)(2,1)S(1)}, bf16[256,1536]{1,0:T(8,128)(2,1)}, u32[]{:S(2)}, u32[]{:S(2)}) %collective-permute-start.61) | collective-permute-done | bytes 786464 | tf_op jit(solution)/shard_map/ppermute | solution.py:115
  604.1 13.6 %collective-permute-done.65 = bf16[256,1536]{1,0:T(8,128)(2,1)S(1)} collective-permute-done((bf16[256,1536]{1,0:T(8,128)(2,1)S(1)}, bf16[256,1536]{1,0:T(8,128)(2,1)S(1)}, u32[]{:S(2)}, u32[]{:S(2)}) %collective-permute-start.65) | collective-permute-done | bytes 786464 | tf_op jit(solution)/shard_map/ppermute | solution.py:115
  617.7 15.7 %collective-permute-done.66 = bf16[256,1536]{1,0:T(8,128)(2,1)S(1)} collective-permute-done((bf16[256,1536]{1,0:T(8,128)(2,1)S(1)}, bf16[256,1536]{1,0:T(8,128)(2,1)S(1)}, u32[]{:S(2)}, u32[]{:S(2)}) %collective-permute-start.66) | collective-permute-done | bytes 786464 | tf_op jit(solution)/shard_map/ppermute | solution.py:115
  636.0 5.1 fusion.147
  641.1 14.0 %collective-permute-done.100 = bf16[4,192,2240]{2,1,0:T(8,128)(2,1)S(1)} collective-permute-done((bf16[4,192,2240]{2,1,0:T(8,128)(2,1)S(1)}, bf16[4,192,2240]{2,1,0:T(8,128)(2,1)S(1)}, u32[]{:S(2)}, u32[]{:S(2)}) %collective-permute-start.100) | collective-permute-done | bytes 3440672 | tf_op jit(solution)/shard_map/ppermute | solution.py:136
  661.5 68.8 %collective-permute-done.104 = bf16[4,192,2240]{2,1,0:T(8,128)(2,1)} collective-permute-done((bf16[4,192,2240]{2,1,0:T(8,128)(2,1)S(1)}, bf16[4,192,2240]{2,1,0:T(8,128)(2,1)}, u32[]{:S(2)}, u32[]{:S(2)}) %collective-permute-start.104) | collective-permute-done | bytes 3440672 | tf_op jit(solution)/shard_map/ppermute | solution.py:136
  752.6 4.6 convolution_convert_fusion.4
  767.4 5.2 convolution_convert_fusion.3
  787.3 6.8 copy.190
  807.0 11.9 %collective-permute-done.107 = bf16[192,2240]{1,0:T(8,128)(2,1)S(1)} collective-permute-done((bf16[192,2240]{1,0:T(8,128)(2,1)S(1)}, bf16[192,2240]{1,0:T(8,128)(2,1)S(1)}, u32[]{:S(2)}, u32[]{:S(2)}) %collective-permute-start.107) | collective-permute-done | bytes 860192 | tf_op jit(solution)/shard_map/ppermute | solution.py:141
  819.4 37.3 %collective-permute-done.106 = bf16[192,2240]{1,0:T(8,128)(2,1)S(1)} collective-permute-done((bf16[192,2240]{1,0:T(8,128)(2,1)S(1)}, bf16[192,2240]{1,0:T(8,128)(2,1)S(1)}, u32[]{:S(2)}, u32[]{:S(2)}) %collective-permute-start.106) | collective-permute-done | bytes 860192 | tf_op jit(solution)/shard_map/ppermute | solution.py:141
  882.7 5.2 multiply_reduce_fusion
  905.4 24.3 %collective-permute-done.98 = bf16[192,1536]{1,0:T(8,128)(2,1)} collective-permute-done((bf16[192,1536]{1,0:T(8,128)(2,1)}, bf16[192,1536]{1,0:T(8,128)(2,1)}, u32[]{:S(2)}, u32[]{:S(2)}) %collective-permute-start.98) | collective-permute-done | bytes 589856 | tf_op jit(solution)/shard_map/ppermute | solution.py:141
  933.2 7.9 fusion.71
  946.3 6.8 fusion.90
  966.3 4.6 convolution_convert_fusion.2
  990.8 5.1 collective-permute-done.94
  1003.7 14.3 %collective-permute-done.88 = bf16[4,192,1152]{2,1,0:T(8,128)(2,1)} collective-permute-done((bf16[4,192,1152]{2,1,0:T(8,128)(2,1)}, bf16[4,192,1152]{2,1,0:T(8,128)(2,1)}, u32[]{:S(2)}, u32[]{:S(2)}) %collective-permute-start.88) | collective-permute-done | bytes 1769504 | tf_op jit(solution)/shard_map/ppermute | solution.py:136
  1038.0 7.4 collective-permute-done.91
  1045.4 16.2 %collective-permute-done.90 = bf16[192,1152]{1,0:T(8,128)(2,1)} collective-permute-done((bf16[192,1152]{1,0:T(8,128)(2,1)S(1)}, bf16[192,1152]{1,0:T(8,128)(2,1)}, u32[]{:S(2)}, u32[]{:S(2)}) %collective-permute-start.90) | collective-permute-done | bytes 442400 | tf_op jit(solution)/shard_map/ppermute | solution.py:141
  (896 shorter events, 450.2 us)
Async XLA Ops:
  6.7 50.9 %collective-permute-start.6 = (bf16[8,256]{1,0:T(8,128)(2,1)}, bf16[8,256]{1,0:T(8,128)(2,1)S(1)}, u32[]{:S(2)}, u32[]{:S(2)}) collective-permute-start(bf16[8,256]{1,0:T(8,128)(2,1)} %reshape.783), channel_id=1, source_target_pairs={{24,0},{28,4},{0,8},{4,12},{8,16},{12,20},{16,24},{20,28},{25,1},{... | collective-permute-start | bytes 12296 | tf_op jit(solution)/shard_map/ppermute | solution.py:122
  9.8 48.3 %collective-permute-start.4 = (bf16[8,256]{1,0:T(8,128)(2,1)}, bf16[8,256]{1,0:T(8,128)(2,1)S(1)}, u32[]{:S(2)}, u32[]{:S(2)}) collective-permute-start(bf16[8,256]{1,0:T(8,128)(2,1)} %reshape.783), channel_id=1, source_target_pairs={{16,0},{20,4},{24,8},{28,12},{0,16},{4,20},{8,24},{12,28},{17,1},{... | collective-permute-start | bytes 12296 | tf_op jit(solution)/shard_map/ppermute | solution.py:122
  12.3 47.4 %collective-permute-start.2 = (bf16[8,256]{1,0:T(8,128)(2,1)}, bf16[8,256]{1,0:T(8,128)(2,1)S(1)}, u32[]{:S(2)}, u32[]{:S(2)}) collective-permute-start(bf16[8,256]{1,0:T(8,128)(2,1)} %reshape.783), channel_id=1, source_target_pairs={{8,0},{12,4},{16,8},{20,12},{24,16},{28,20},{0,24},{4,28},{9,1},{1... | collective-permute-start | bytes 12296 | tf_op jit(solution)/shard_map/ppermute | solution.py:122
  13.7 46.5 %collective-permute-start.1 = (bf16[8,256]{1,0:T(8,128)(2,1)}, bf16[8,256]{1,0:T(8,128)(2,1)}, u32[]{:S(2)}, u32[]{:S(2)}) collective-permute-start(bf16[8,256]{1,0:T(8,128)(2,1)} %reshape.783), channel_id=1, source_target_pairs={{0,4},{4,0},{8,12},{12,8},{16,20},{20,16},{24,28},{28,24},{1,5},{5... | collective-permute-start | bytes 12296 | tf_op jit(solution)/shard_map/ppermute | solution.py:123
  16.8 60.9 %collective-permute-start.21 = (bf16[192,384]{1,0:T(8,128)(2,1)}, bf16[192,384]{1,0:T(8,128)(2,1)}, u32[]{:S(2)}, u32[]{:S(2)}) collective-permute-start(bf16[192,384]{1,0:T(8,128)(2,1)} %convert_bitcast_fusion.3), channel_id=1, source_target_pairs={{16,0},{20,4},{24,8},{28,12},{0,16},{4,20},{8,24},{12,28},{17,1},{... | collective-permute-start | bytes 442376 | tf_op jit(solution)/shard_map/ppermute | solution.py:122
  65.5 129.8 %collective-permute-start.14 = (bf16[192,1152]{1,0:T(8,128)(2,1)}, bf16[192,1152]{1,0:T(8,128)(2,1)}, u32[]{:S(2)}, u32[]{:S(2)}) collective-permute-start(bf16[192,1152]{1,0:T(8,128)(2,1)} %pad_maximum_fusion.34), channel_id=1, source_target_pairs={{24,0},{28,4},{0,8},{4,12},{8,16},{12,20},{16,24},{20,28},{25,1},{... | collective-permute-start | bytes 1327112 | tf_op jit(solution)/shard_map/ppermute | solution.py:122
  73.2 102.1 %collective-permute-start.12 = (bf16[192,1152]{1,0:T(8,128)(2,1)}, bf16[192,1152]{1,0:T(8,128)(2,1)S(1)}, u32[]{:S(2)}, u32[]{:S(2)}) collective-permute-start(bf16[192,1152]{1,0:T(8,128)(2,1)} %pad_maximum_fusion.34), channel_id=1, source_target_pairs={{16,0},{20,4},{24,8},{28,12},{0,16},{4,20},{8,24},{12,28},{17,1},{... | collective-permute-start | bytes 1327112 | tf_op jit(solution)/shard_map/ppermute | solution.py:122
  77.7 32.9 %collective-permute-start.10 = (bf16[192,1152]{1,0:T(8,128)(2,1)}, bf16[192,1152]{1,0:T(8,128)(2,1)S(1)}, u32[]{:S(2)}, u32[]{:S(2)}) collective-permute-start(bf16[192,1152]{1,0:T(8,128)(2,1)} %pad_maximum_fusion.34), channel_id=1, source_target_pairs={{8,0},{12,4},{16,8},{20,12},{24,16},{28,20},{0,24},{4,28},{9,1},{1... | collective-permute-start | bytes 1327112 | tf_op jit(solution)/shard_map/ppermute | solution.py:122
  96.8 162.7 %collective-permute-start.35 = (bf16[192,1536]{1,0:T(8,128)(2,1)S(1)}, bf16[192,1536]{1,0:T(8,128)(2,1)}, u32[]{:S(2)}, u32[]{:S(2)}) collective-permute-start(bf16[192,1536]{1,0:T(8,128)(2,1)S(1)} %pad_maximum_fusion.31), channel_id=1, source_target_pairs={{24,0},{28,4},{0,8},{4,12},{8,16},{12,20},{16,24},{20,28},{25,1},{... | collective-permute-start | bytes 1769480 | tf_op jit(solution)/shard_map/ppermute | solution.py:122
  138.0 35.0 %collective-permute-start.53 = (bf16[192,2240]{1,0:T(8,128)(2,1)}, bf16[192,2240]{1,0:T(8,128)(2,1)S(1)}, u32[]{:S(2)}, u32[]{:S(2)}) collective-permute-start(bf16[192,2240]{1,0:T(8,128)(2,1)} %convert_bitcast_fusion), channel_id=1, source_target_pairs={{0,4},{4,0},{8,12},{12,8},{16,20},{20,16},{24,28},{28,24},{1,5},{5... | collective-permute-start | bytes 2580488 | tf_op jit(solution)/shard_map/ppermute | solution.py:123
  154.5 35.5 %collective-permute-start.54 = (bf16[192,2240]{1,0:T(8,128)(2,1)}, bf16[192,2240]{1,0:T(8,128)(2,1)}, u32[]{:S(2)}, u32[]{:S(2)}) collective-permute-start(bf16[192,2240]{1,0:T(8,128)(2,1)} %convert_bitcast_fusion), channel_id=1, source_target_pairs={{8,0},{12,4},{16,8},{20,12},{24,16},{28,20},{0,24},{4,28},{9,1},{1... | collective-permute-start | bytes 2580488 | tf_op jit(solution)/shard_map/ppermute | solution.py:122
  173.0 81.8 %collective-permute-start.33 = (bf16[192,1536]{1,0:T(8,128)(2,1)S(1)}, bf16[192,1536]{1,0:T(8,128)(2,1)}, u32[]{:S(2)}, u32[]{:S(2)}) collective-permute-start(bf16[192,1536]{1,0:T(8,128)(2,1)S(1)} %pad_maximum_fusion.31), channel_id=1, source_target_pairs={{16,0},{20,4},{24,8},{28,12},{0,16},{4,20},{8,24},{12,28},{17,1},{... | collective-permute-start | bytes 1769480 | tf_op jit(solution)/shard_map/ppermute | solution.py:122
  193.7 30.1 %collective-permute-start.8 = (bf16[512,1536]{1,0:T(8,128)(2,1)S(1)}, bf16[512,1536]{1,0:T(8,128)(2,1)S(1)}, u32[]{:S(2)}, u32[]{:S(2)}) collective-permute-start(bf16[512,1536]{1,0:T(8,128)(2,1)S(1)} %get-tuple-element.92), channel_id=1, source_target_pairs={{0,1},{1,0},{2,3},{3,2},{4,5},{5,4},{6,7},{7,6},{8,9},{9,8},{10,11... | collective-permute-start | bytes 4718600 | tf_op jit(solution)/shard_map/ppermute | solution.py:112
  195.4 157.5 %collective-permute-start.56 = (bf16[192,2240]{1,0:T(8,128)(2,1)}, bf16[192,2240]{1,0:T(8,128)(2,1)}, u32[]{:S(2)}, u32[]{:S(2)}) collective-permute-start(bf16[192,2240]{1,0:T(8,128)(2,1)} %convert_bitcast_fusion), channel_id=1, source_target_pairs={{16,0},{20,4},{24,8},{28,12},{0,16},{4,20},{8,24},{12,28},{17,1},{... | collective-permute-start | bytes 2580488 | tf_op jit(solution)/shard_map/ppermute | solution.py:122
  221.5 173.3 %collective-permute-start.58 = (bf16[192,2240]{1,0:T(8,128)(2,1)}, bf16[192,2240]{1,0:T(8,128)(2,1)}, u32[]{:S(2)}, u32[]{:S(2)}) collective-permute-start(bf16[192,2240]{1,0:T(8,128)(2,1)} %convert_bitcast_fusion), channel_id=1, source_target_pairs={{24,0},{28,4},{0,8},{4,12},{8,16},{12,20},{16,24},{20,28},{25,1},{... | collective-permute-start | bytes 2580488 | tf_op jit(solution)/shard_map/ppermute | solution.py:122
  238.2 56.9 %collective-permute-start.29 = (bf16[256,1536]{1,0:T(8,128)(2,1)}, bf16[256,1536]{1,0:T(8,128)(2,1)}, u32[]{:S(2)}, u32[]{:S(2)}) collective-permute-start(bf16[256,1536]{1,0:T(8,128)(2,1)} %pad_maximum_fusion.27), channel_id=1, source_target_pairs={{0,1},{1,0},{2,3},{3,2},{4,5},{5,4},{6,7},{7,6},{8,9},{9,8},{10,11... | collective-permute-start | bytes 2359304 | tf_op jit(solution)/shard_map/ppermute | solution.py:112
  261.0 30.6 %collective-permute-start.36 = (bf16[192,1536]{1,0:T(8,128)(2,1)}, bf16[192,1536]{1,0:T(8,128)(2,1)}, u32[]{:S(2)}, u32[]{:S(2)}) collective-permute-start(bf16[192,1536]{1,0:T(8,128)(2,1)} %collective-permute-done.35), channel_id=1, source_target_pairs={{0,4},{4,0},{8,12},{12,8},{16,20},{20,16},{24,28},{28,24},{1,5},{5... | collective-permute-start | bytes 1769480 | tf_op jit(solution)/shard_map/ppermute | solution.py:123
  315.0 29.3 %collective-permute-start.47 = (bf16[192,2240]{1,0:T(8,128)(2,1)S(1)}, bf16[192,2240]{1,0:T(8,128)(2,1)}, u32[]{:S(2)}, u32[]{:S(2)}) collective-permute-start(bf16[192,2240]{1,0:T(8,128)(2,1)S(1)} %copy-done.75), channel_id=1, source_target_pairs={{8,0},{12,4},{16,8},{20,12},{24,16},{28,20},{0,24},{4,28},{9,1},{1... | collective-permute-start | bytes 2580488 | tf_op jit(solution)/shard_map/ppermute | solution.py:122
  319.7 33.2 %collective-permute-start.55 = (bf16[192,2240]{1,0:T(8,128)(2,1)}, bf16[192,2240]{1,0:T(8,128)(2,1)}, u32[]{:S(2)}, u32[]{:S(2)}) collective-permute-start(bf16[192,2240]{1,0:T(8,128)(2,1)} %collective-permute-done.54), channel_id=1, source_target_pairs={{0,4},{4,0},{8,12},{12,8},{16,20},{20,16},{24,28},{28,24},{1,5},{5... | collective-permute-start | bytes 2580488 | tf_op jit(solution)/shard_map/ppermute | solution.py:123
  347.7 52.1 %collective-permute-start.49 = (bf16[192,2240]{1,0:T(8,128)(2,1)}, bf16[192,2240]{1,0:T(8,128)(2,1)}, u32[]{:S(2)}, u32[]{:S(2)}) collective-permute-start(bf16[192,2240]{1,0:T(8,128)(2,1)} %get-tuple-element.64), channel_id=1, source_target_pairs={{16,0},{20,4},{24,8},{28,12},{0,16},{4,20},{8,24},{12,28},{17,1},{... | collective-permute-start | bytes 2580488 | tf_op jit(solution)/shard_map/ppermute | solution.py:122
  352.9 48.5 %collective-permute-start.51 = (bf16[192,2240]{1,0:T(8,128)(2,1)}, bf16[192,2240]{1,0:T(8,128)(2,1)}, u32[]{:S(2)}, u32[]{:S(2)}) collective-permute-start(bf16[192,2240]{1,0:T(8,128)(2,1)} %get-tuple-element.64), channel_id=1, source_target_pairs={{24,0},{28,4},{0,8},{4,12},{8,16},{12,20},{16,24},{20,28},{25,1},{... | collective-permute-start | bytes 2580488 | tf_op jit(solution)/shard_map/ppermute | solution.py:122
  362.7 130.4 %collective-permute-start.63 = (bf16[512,1536]{1,0:T(8,128)(2,1)}, bf16[512,1536]{1,0:T(8,128)(2,1)}, u32[]{:S(2)}, u32[]{:S(2)}) collective-permute-start(bf16[512,1536]{1,0:T(8,128)(2,1)} %multiply_convert_fusion.4), channel_id=1, source_target_pairs={{0,1},{1,0},{2,3},{3,2},{4,5},{5,4},{6,7},{7,6},{8,9},{9,8},{10,11... | collective-permute-start | bytes 4718600 | tf_op jit(solution)/shard_map/ppermute | solution.py:112
  399.8 62.5 %collective-permute-start.59 = (bf16[192,2240]{1,0:T(8,128)(2,1)}, bf16[192,2240]{1,0:T(8,128)(2,1)S(1)}, u32[]{:S(2)}, u32[]{:S(2)}) collective-permute-start(bf16[192,2240]{1,0:T(8,128)(2,1)} %collective-permute-done.58), channel_id=1, source_target_pairs={{0,4},{4,0},{8,12},{12,8},{16,20},{20,16},{24,28},{28,24},{1,5},{5... | collective-permute-start | bytes 2580488 | tf_op jit(solution)/shard_map/ppermute | solution.py:123
  401.3 40.1 %collective-permute-start.50 = (bf16[192,2240]{1,0:T(8,128)(2,1)}, bf16[192,2240]{1,0:T(8,128)(2,1)S(1)}, u32[]{:S(2)}, u32[]{:S(2)}) collective-permute-start(bf16[192,2240]{1,0:T(8,128)(2,1)} %collective-permute-done.49), channel_id=1, source_target_pairs={{0,4},{4,0},{8,12},{12,8},{16,20},{20,16},{24,28},{28,24},{1,5},{5... | collective-permute-start | bytes 2580488 | tf_op jit(solution)/shard_map/ppermute | solution.py:123
  401.8 61.5 %collective-permute-start.52 = (bf16[192,2240]{1,0:T(8,128)(2,1)}, bf16[192,2240]{1,0:T(8,128)(2,1)S(1)}, u32[]{:S(2)}, u32[]{:S(2)}) collective-permute-start(bf16[192,2240]{1,0:T(8,128)(2,1)} %collective-permute-done.51), channel_id=1, source_target_pairs={{0,4},{4,0},{8,12},{12,8},{16,20},{20,16},{24,28},{28,24},{1,5},{5... | collective-permute-start | bytes 2580488 | tf_op jit(solution)/shard_map/ppermute | solution.py:123
  408.3 37.8 %collective-permute-start.43 = (bf16[256,1536]{1,0:T(8,128)(2,1)S(1)}, bf16[256,1536]{1,0:T(8,128)(2,1)S(1)}, u32[]{:S(2)}, u32[]{:S(2)}) collective-permute-start(bf16[256,1536]{1,0:T(8,128)(2,1)S(1)} %get-tuple-element.105), channel_id=1, source_target_pairs={{0,2},{1,3},{2,0},{3,1},{4,6},{5,7},{6,4},{7,5},{8,10},{9,11},{10,... | collective-permute-start | bytes 2359304 | tf_op jit(solution)/shard_map/ppermute | solution.py:115
  531.4 45.8 %collective-permute-start.60 = (bf16[512,1536]{1,0:T(8,128)(2,1)}, bf16[512,1536]{1,0:T(8,128)(2,1)}, u32[]{:S(2)}, u32[]{:S(2)}) collective-permute-start(bf16[512,1536]{1,0:T(8,128)(2,1)} %slice.681), channel_id=1, source_target_pairs={{0,1},{1,0},{2,3},{3,2},{4,5},{5,4},{6,7},{7,6},{8,9},{9,8},{10,11... | collective-permute-start | bytes 4718600 | tf_op jit(solution)/shard_map/ppermute | solution.py:112
  531.6 50.3 %collective-permute-start.64 = (bf16[512,1536]{1,0:T(8,128)(2,1)}, bf16[512,1536]{1,0:T(8,128)(2,1)}, u32[]{:S(2)}, u32[]{:S(2)}) collective-permute-start(bf16[512,1536]{1,0:T(8,128)(2,1)} %slice.680), channel_id=1, source_target_pairs={{0,1},{1,0},{2,3},{3,2},{4,5},{5,4},{6,7},{7,6},{8,9},{9,8},{10,11... | collective-permute-start | bytes 4718600 | tf_op jit(solution)/shard_map/ppermute | solution.py:112
  575.7 79.4 %collective-permute-start.100 = (bf16[4,192,2240]{2,1,0:T(8,128)(2,1)S(1)}, bf16[4,192,2240]{2,1,0:T(8,128)(2,1)S(1)}, u32[]{:S(2)}, u32[]{:S(2)}) collective-permute-start(bf16[4,192,2240]{2,1,0:T(8,128)(2,1)S(1)} %dynamic-slice_bitcast_fusion.1), channel_id=1, source_target_pairs={{0,4},{4,0},{8,12},{12,8},{16,20},{20,16},{24,28},{28,24},{1,5},{5... | collective-permute-start | bytes 10321928 | tf_op jit(solution)/shard_map/ppermute | solution.py:136
  584.0 33.7 %collective-permute-start.65 = (bf16[256,1536]{1,0:T(8,128)(2,1)S(1)}, bf16[256,1536]{1,0:T(8,128)(2,1)S(1)}, u32[]{:S(2)}, u32[]{:S(2)}) collective-permute-start(bf16[256,1536]{1,0:T(8,128)(2,1)S(1)} %get-tuple-element.103), channel_id=1, source_target_pairs={{0,2},{1,3},{2,0},{3,1},{4,6},{5,7},{6,4},{7,5},{8,10},{9,11},{10,... | collective-permute-start | bytes 2359304 | tf_op jit(solution)/shard_map/ppermute | solution.py:115
  584.8 48.6 %collective-permute-start.66 = (bf16[256,1536]{1,0:T(8,128)(2,1)S(1)}, bf16[256,1536]{1,0:T(8,128)(2,1)S(1)}, u32[]{:S(2)}, u32[]{:S(2)}) collective-permute-start(bf16[256,1536]{1,0:T(8,128)(2,1)S(1)} %get-tuple-element.104), channel_id=1, source_target_pairs={{0,2},{1,3},{2,0},{3,1},{4,6},{5,7},{6,4},{7,5},{8,10},{9,11},{10,... | collective-permute-start | bytes 2359304 | tf_op jit(solution)/shard_map/ppermute | solution.py:115
  586.4 143.9 %collective-permute-start.104 = (bf16[4,192,2240]{2,1,0:T(8,128)(2,1)S(1)}, bf16[4,192,2240]{2,1,0:T(8,128)(2,1)}, u32[]{:S(2)}, u32[]{:S(2)}) collective-permute-start(bf16[4,192,2240]{2,1,0:T(8,128)(2,1)S(1)} %dynamic-slice_bitcast_fusion), channel_id=1, source_target_pairs={{0,4},{4,0},{8,12},{12,8},{16,20},{20,16},{24,28},{28,24},{1,5},{5... | collective-permute-start | bytes 10321928 | tf_op jit(solution)/shard_map/ppermute | solution.py:136
  641.1 96.6 %collective-permute-start.67 = (bf16[512,1536]{1,0:T(8,128)(2,1)}, bf16[512,1536]{1,0:T(8,128)(2,1)S(1)}, u32[]{:S(2)}, u32[]{:S(2)}) collective-permute-start(bf16[512,1536]{1,0:T(8,128)(2,1)} %get-tuple-element.57), channel_id=1, source_target_pairs={{0,1},{1,0},{2,3},{3,2},{4,5},{5,4},{6,7},{7,6},{8,9},{9,8},{10,11... | collective-permute-start | bytes 4718600 | tf_op jit(solution)/shard_map/ppermute | solution.py:112
  657.6 138.4 %collective-permute-start.101 = (bf16[192,2240]{1,0:T(8,128)(2,1)}, bf16[192,2240]{1,0:T(8,128)(2,1)}, u32[]{:S(2)}, u32[]{:S(2)}) collective-permute-start(bf16[192,2240]{1,0:T(8,128)(2,1)} %get-tuple-element.74), channel_id=1, source_target_pairs={{0,8},{4,12},{8,16},{12,20},{16,24},{20,28},{24,0},{28,4},{1,9},{5... | collective-permute-start | bytes 2580488 | tf_op jit(solution)/shard_map/ppermute | solution.py:141
  658.7 140.2 %collective-permute-start.103 = (bf16[192,2240]{1,0:T(8,128)(2,1)}, bf16[192,2240]{1,0:T(8,128)(2,1)}, u32[]{:S(2)}, u32[]{:S(2)}) collective-permute-start(bf16[192,2240]{1,0:T(8,128)(2,1)} %get-tuple-element.75), channel_id=1, source_target_pairs={{0,24},{4,28},{8,0},{12,4},{16,8},{20,12},{24,16},{28,20},{1,25},{... | collective-permute-start | bytes 2580488 | tf_op jit(solution)/shard_map/ppermute | solution.py:141
  661.5 137.4 %collective-permute-start.102 = (bf16[192,2240]{1,0:T(8,128)(2,1)}, bf16[192,2240]{1,0:T(8,128)(2,1)}, u32[]{:S(2)}, u32[]{:S(2)}) collective-permute-start(bf16[192,2240]{1,0:T(8,128)(2,1)} %get-tuple-element.76), channel_id=1, source_target_pairs={{0,16},{4,20},{8,24},{12,28},{16,0},{20,4},{24,8},{28,12},{1,17},{... | collective-permute-start | bytes 2580488 | tf_op jit(solution)/shard_map/ppermute | solution.py:141
  736.4 70.0 %collective-permute-start.105 = (bf16[192,2240]{1,0:T(8,128)(2,1)}, bf16[192,2240]{1,0:T(8,128)(2,1)}, u32[]{:S(2)}, u32[]{:S(2)}) collective-permute-start(bf16[192,2240]{1,0:T(8,128)(2,1)} %get-tuple-element.71), channel_id=1, source_target_pairs={{0,8},{4,12},{8,16},{12,20},{16,24},{20,28},{24,0},{28,4},{1,9},{5... | collective-permute-start | bytes 2580488 | tf_op jit(solution)/shard_map/ppermute | solution.py:141
  798.8 57.9 %collective-permute-start.106 = (bf16[192,2240]{1,0:T(8,128)(2,1)S(1)}, bf16[192,2240]{1,0:T(8,128)(2,1)S(1)}, u32[]{:S(2)}, u32[]{:S(2)}) collective-permute-start(bf16[192,2240]{1,0:T(8,128)(2,1)S(1)} %copy-done.76), channel_id=1, source_target_pairs={{0,16},{4,20},{8,24},{12,28},{16,0},{20,4},{24,8},{28,12},{1,17},{... | collective-permute-start | bytes 2580488 | tf_op jit(solution)/shard_map/ppermute | solution.py:141
  798.9 60.9 %collective-permute-start.80 = (bf16[256,1536]{1,0:T(8,128)(2,1)S(1)}, bf16[256,1536]{1,0:T(8,128)(2,1)S(1)}, u32[]{:S(2)}, u32[]{:S(2)}) collective-permute-start(bf16[256,1536]{1,0:T(8,128)(2,1)S(1)} %copy-done.83), channel_id=1, source_target_pairs={{0,1},{1,0},{2,3},{3,2},{4,5},{5,4},{6,7},{7,6},{8,9},{9,8},{10,11... | collective-permute-start | bytes 2359304 | tf_op jit(solution)/shard_map/ppermute | solution.py:112
  802.9 68.8 %collective-permute-start.96 = (bf16[4,192,1536]{2,1,0:T(8,128)(2,1)S(1)}, bf16[4,192,1536]{2,1,0:T(8,128)(2,1)}, u32[]{:S(2)}, u32[]{:S(2)}) collective-permute-start(bf16[4,192,1536]{2,1,0:T(8,128)(2,1)S(1)} %dynamic-slice_bitcast_fusion.2), channel_id=1, source_target_pairs={{0,4},{4,0},{8,12},{12,8},{16,20},{20,16},{24,28},{28,24},{1,5},{5... | collective-permute-start | bytes 7077896 | tf_op jit(solution)/shard_map/ppermute | solution.py:136
  806.5 54.2 %collective-permute-start.71 = (bf16[256,1536]{1,0:T(8,128)(2,1)S(1)}, bf16[256,1536]{1,0:T(8,128)(2,1)S(1)}, u32[]{:S(2)}, u32[]{:S(2)}) collective-permute-start(bf16[256,1536]{1,0:T(8,128)(2,1)S(1)} %get-tuple-element.101), channel_id=1, source_target_pairs={{0,2},{1,3},{2,0},{3,1},{4,6},{5,7},{6,4},{7,5},{8,10},{9,11},{10,... | collective-permute-start | bytes 2359304 | tf_op jit(solution)/shard_map/ppermute | solution.py:115
  818.9 41.7 %collective-permute-start.72 = (bf16[256,1536]{1,0:T(8,128)(2,1)S(1)}, bf16[256,1536]{1,0:T(8,128)(2,1)S(1)}, u32[]{:S(2)}, u32[]{:S(2)}) collective-permute-start(bf16[256,1536]{1,0:T(8,128)(2,1)S(1)} %get-tuple-element.102), channel_id=1, source_target_pairs={{0,2},{1,3},{2,0},{3,1},{4,6},{5,7},{6,4},{7,5},{8,10},{9,11},{10,... | collective-permute-start | bytes 2359304 | tf_op jit(solution)/shard_map/ppermute | solution.py:115
  875.5 29.8 %collective-permute-start.97 = (bf16[192,1536]{1,0:T(8,128)(2,1)}, bf16[192,1536]{1,0:T(8,128)(2,1)}, u32[]{:S(2)}, u32[]{:S(2)}) collective-permute-start(bf16[192,1536]{1,0:T(8,128)(2,1)} %get-tuple-element.83), channel_id=1, source_target_pairs={{0,8},{4,12},{8,16},{12,20},{16,24},{20,28},{24,0},{28,4},{1,9},{5... | collective-permute-start | bytes 1769480 | tf_op jit(solution)/shard_map/ppermute | solution.py:141
  875.9 29.4 %collective-permute-start.99 = (bf16[192,1536]{1,0:T(8,128)(2,1)}, bf16[192,1536]{1,0:T(8,128)(2,1)}, u32[]{:S(2)}, u32[]{:S(2)}) collective-permute-start(bf16[192,1536]{1,0:T(8,128)(2,1)} %get-tuple-element.84), channel_id=1, source_target_pairs={{0,24},{4,28},{8,0},{12,4},{16,8},{20,12},{24,16},{28,20},{1,25},{... | collective-permute-start | bytes 1769480 | tf_op jit(solution)/shard_map/ppermute | solution.py:141
  879.3 50.4 %collective-permute-start.98 = (bf16[192,1536]{1,0:T(8,128)(2,1)}, bf16[192,1536]{1,0:T(8,128)(2,1)}, u32[]{:S(2)}, u32[]{:S(2)}) collective-permute-start(bf16[192,1536]{1,0:T(8,128)(2,1)} %get-tuple-element.85), channel_id=1, source_target_pairs={{0,16},{4,20},{8,24},{12,28},{16,0},{20,4},{24,8},{28,12},{1,17},{... | collective-permute-start | bytes 1769480 | tf_op jit(solution)/shard_map/ppermute | solution.py:141
  972.4 45.6 %collective-permute-start.88 = (bf16[4,192,1152]{2,1,0:T(8,128)(2,1)}, bf16[4,192,1152]{2,1,0:T(8,128)(2,1)}, u32[]{:S(2)}, u32[]{:S(2)}) collective-permute-start(bf16[4,192,1152]{2,1,0:T(8,128)(2,1)} %dynamic-slice_bitcast_fusion.3), channel_id=1, source_target_pairs={{0,4},{4,0},{8,12},{12,8},{16,20},{20,16},{24,28},{28,24},{1,5},{5... | collective-permute-start | bytes 5308424 | tf_op jit(solution)/shard_map/ppermute | solution.py:136
  1026.7 35.0 %collective-permute-start.90 = (bf16[192,1152]{1,0:T(8,128)(2,1)S(1)}, bf16[192,1152]{1,0:T(8,128)(2,1)}, u32[]{:S(2)}, u32[]{:S(2)}) collective-permute-start(bf16[192,1152]{1,0:T(8,128)(2,1)S(1)} %get-tuple-element.90), channel_id=1, source_target_pairs={{0,16},{4,20},{8,24},{12,28},{16,0},{20,4},{24,8},{28,12},{1,17},{... | collective-permute-start | bytes 1327112 | tf_op jit(solution)/shard_map/ppermute | solution.py:141
  1032.4 30.5 %collective-permute-start.84 = (bf16[4,8,256]{2,1,0:T(8,128)(2,1)S(1)}, bf16[4,8,256]{2,1,0:T(8,128)(2,1)S(1)}, u32[]{:S(2)}, u32[]{:S(2)}) collective-permute-start(bf16[4,8,256]{2,1,0:T(8,128)(2,1)S(1)} %fusion.104), channel_id=1, source_target_pairs={{0,4},{4,0},{8,12},{12,8},{16,20},{20,16},{24,28},{28,24},{1,5},{5... | collective-permute-start | bytes 49160 | tf_op jit(solution)/shard_map/ppermute | solution.py:136
  (238 other events, 3277.5 us)

commit v2 on v1

v2 whole, which is shorter than its diff:
```python
import math

import jax
import jax.numpy as jnp
from jax import lax
from jax.experimental import pallas as pl
from jax.experimental.pallas import tpu as pltpu
from jax.sharding import PartitionSpec as P

D = 1536
HEAD = 128
EPS = 1e-6
BF = jnp.bfloat16
F32 = jnp.float32
FACTOR = 1.0 / math.sqrt(HEAD)
GELU = math.sqrt(2.0 / math.pi)
CUBE = 0.044715
MESH = pl.DeviceIdType.MESH


def dot_nn(a, b):
    return lax.dot_general(a, b, (((1,), (0,)), ((), ())), preferred_element_type=F32)


def dot_nt(a, b):
    return lax.dot_general(a, b, (((1,), (1,)), ((), ())), preferred_element_type=F32)


def dot_tn(a, b):
    return lax.dot_general(a, b, (((0,), (0,)), ((), ())), preferred_element_type=F32)


def shape(dims, dtype):
    return jax.ShapeDtypeStruct(dims, dtype)


def run(kernel, outs, blocks, far=(), scratch=(), flops=0, exps=0, limit=60):
    moved = sum(math.prod(v.shape) * v.dtype.itemsize for v in (*blocks, *far, *outs))
    return pl.pallas_call(
        kernel,
        out_shape=tuple(outs),
        in_specs=[pl.BlockSpec(memory_space=pltpu.VMEM)] * len(blocks)
        + [pl.BlockSpec(memory_space=pl.ANY)] * len(far),
        out_specs=tuple(pl.BlockSpec(memory_space=pltpu.VMEM) for _ in outs),
        scratch_shapes=list(scratch),
        compiler_params=pltpu.CompilerParams(vmem_limit_bytes=limit * 2**20),
        cost_estimate=pl.CostEstimate(flops=int(flops), bytes_accessed=moved, transcendentals=int(exps)),
    )(*blocks, *far)


def load(pieces, w, sems, first=0):
    n = len(pieces)
    r, c = w.shape[0] // n, w.shape[1]
    if n == 1:
        copy = pltpu.make_async_copy(pieces[0].at[:, pl.ds(first, c)], w, sems.at[0])
        copy.start()
        return [copy]
    d = lax.axis_index("dp")
    major, minor = d // 2, d % 2
    copies = []
    for i, piece in enumerate(pieces):
        t, flip = i // 2, i % 2
        block = 2 * lax.rem(major + t, n // 2) + (1 - minor if flip else minor)
        rows = pl.ds(pl.multiple_of(block * r, 16), r)
        copy = pltpu.make_async_copy(piece.at[:, pl.ds(first, c)], w.at[rows], sems.at[i])
        copy.start()
        copies.append(copy)
    return copies


def wait(copies):
    for copy in copies:
        copy.wait()


def weight(n, c):
    return [pltpu.VMEM((D, c), BF), pltpu.SemaphoreType.DMA((n,))]


def to_rows(columns, count):
    lane = lax.broadcasted_iota(jnp.int32, (count, 128), 1)
    out = jnp.zeros((count, 128), F32)
    for i, column in enumerate(columns):
        out = jnp.where(lane == i, column, out)
    return jnp.transpose(out)[:8]


def to_columns(rows):
    return jnp.transpose(jnp.concatenate([rows] * 16, axis=0))


def turn(values, cosine, sine):
    even = lax.broadcasted_iota(jnp.int32, values.shape, 1) % 2 == 0
    partner = jnp.where(even, pltpu.roll(values, HEAD - 1, 1), pltpu.roll(values, 1, 1))
    return values * cosine + partner * sine


def norm_of(v):
    center = v - jnp.mean(v, axis=-1, keepdims=True)
    r = lax.rsqrt(jnp.mean(center * center, axis=-1, keepdims=True) + EPS)
    return center * r, r


STEP = 32


def over_rows(count, body):
    def one(i, carry):
        body(pl.ds(pl.multiple_of(i * STEP, STEP), STEP))
        return carry

    lax.fori_loop(0, count // STEP, one, 0)


def norm_first(v, m, t):
    def kernel(v_ref, m_ref, t_ref, rows_ref):
        def body(s):
            n, _ = norm_of(v_ref[s].astype(F32))
            rows_ref[s] = (n * m_ref[...] + t_ref[...]).astype(BF)

        over_rows(v_ref.shape[0], body)

    return run(kernel, [shape(v.shape, BF)], [v, m, t], flops=1e9)[0]


def norm_forward(v, chip, far_chip, s, m, t):
    def kernel(v_ref, a_ref, b_ref, s_ref, m_ref, t_ref, out_ref, rows_ref):
        def body(i):
            branch = a_ref[i].astype(F32) + b_ref[i].astype(F32)
            out = v_ref[i].astype(F32) + branch * s_ref[...]
            out_ref[i] = out
            n, _ = norm_of(out)
            rows_ref[i] = (n * m_ref[...] + t_ref[...]).astype(BF)

        over_rows(v_ref.shape[0], body)

    return run(
        kernel, [shape(v.shape, F32), shape(v.shape, BF)], [v, chip, far_chip, s, m, t], flops=1e9
    )


def norm_backward(g, v, chip, far_chip, m, s):
    def kernel(g_ref, v_ref, a_ref, b_ref, m_ref, s_ref, out_ref, rows_ref, sum_ref):
        sum_ref[...] = jnp.zeros_like(sum_ref)

        def body(i):
            da = a_ref[i].astype(F32) + b_ref[i].astype(F32)
            n, r = norm_of(v_ref[i].astype(F32))
            dn = da * m_ref[...]
            mean = jnp.mean(dn, axis=-1, keepdims=True)
            along = jnp.mean(dn * n, axis=-1, keepdims=True)
            out = g_ref[i].astype(F32) + r * (dn - mean - n * along)
            out_ref[i] = out
            rows_ref[i] = (out * s_ref[...]).astype(BF)
            dan = da * n
            for k in range(STEP // 8):
                sum_ref[:8] += da[k * 8 : k * 8 + 8]
                sum_ref[8:] += dan[k * 8 : k * 8 + 8]

        over_rows(g_ref.shape[0], body)

    return run(
        kernel,
        [shape(g.shape, F32), shape(g.shape, BF), shape((16, D), F32)],
        [g, v, chip, far_chip, m, s],
        flops=1e9,
    )


def hold(v, after):
    def kernel(v_ref, *refs):
        refs[-1][...] = v_ref[...]

    return run(kernel, [shape(v.shape, v.dtype)], [v], after)[0]


def project(xs, pieces, first, squares, lows, wide):
    total = sum(x.shape[0] for x in xs)
    cols = (squares + lows) * wide
    n = len(pieces)
    outs = [shape((total, squares * wide), F32)] * (squares > 0)
    outs += [shape((total, lows * wide), BF)] * (lows > 0)
    outs += [shape((8, total), F32)] * (squares > 0)

    def kernel(*refs):
        x_refs, refs = refs[: len(xs)], refs[len(xs) :]
        piece_refs, refs = refs[:n], refs[n:]
        out_refs, (w, sems) = list(refs[:-2]), refs[-2:]
        wait(load(piece_refs, w, sems, first))
        at = 0
        for x_ref in x_refs:
            m = x_ref.shape[0]
            value = dot_nn(x_ref[...], w[...])
            columns = []
            for i in range(squares):
                part = value[:, i * wide : (i + 1) * wide]
                columns.append(jnp.sum(part * part, axis=1, keepdims=True))
            if squares:
                out_refs[0][at : at + m] = value[:, : squares * wide]
                out_refs[-1][:, at : at + m] = to_rows(columns, m)
            if lows:
                out_refs[1 if squares else 0][at : at + m] = value[:, squares * wide :].astype(BF)
            at += m

    return run(kernel, outs, xs, pieces, weight(n, cols), flops=2 * total * D * cols)


def normalize(raws, stats, gains, tables, wide):
    count = len(gains)
    parts = len(raws)
    outs = [shape((r.shape[0], wide), BF) for r in raws for _ in range(count)]

    def kernel(*refs):
        raw_refs, refs = refs[:parts], refs[parts:]
        stat_refs, refs = refs[:parts], refs[parts:]
        gain_refs, refs = refs[:count], refs[count:]
        if tables:
            cos_refs, sin_refs, refs = refs[:parts], refs[parts : 2 * parts], refs[2 * parts :]
        for p in range(parts):
            scale = lax.rsqrt(to_columns(stat_refs[p][...]) / D + EPS)
            for i in range(count):
                for h in range(wide // HEAD):
                    lanes = slice(i * wide + h * HEAD, i * wide + (h + 1) * HEAD)
                    own = slice(h * HEAD, (h + 1) * HEAD)
                    value = raw_refs[p][:, lanes] * scale[:, i : i + 1] * gain_refs[i][:, own]
                    if tables:
                        value = turn(value, cos_refs[p][...], sin_refs[p][...])
                    refs[p * count + i][:, own] = value.astype(BF)

    args = [*raws, *stats, *gains]
    if tables:
        args += [*tables[0], *tables[1]]
    return run(kernel, outs, args, flops=1e9)


QB = 256


def attend(q, ks, vs, bias, pieces, first):
    rows, wide = q.shape
    heads = wide // HEAD
    nk = sum(k.shape[0] for k in ks)
    n = len(pieces)
    parts = len(ks)
    half = rows // 2
    biases = [] if bias is None else [bias]

    def kernel(*refs):
        q_ref, k_refs, v_refs = refs[0], refs[1 : 1 + parts], refs[1 + parts : 1 + 2 * parts]
        refs = refs[1 + 2 * parts :]
        b_refs, refs = refs[: len(biases)], refs[len(biases) :]
        piece_refs, (out_ref, lse_ref, mine_ref, theirs_ref, w, sems) = refs[:n], refs[n:]
        copies = load(piece_refs, w, sems, first)
        lse_ref[...] = jnp.zeros_like(lse_ref)
        for h in range(heads):
            lanes = slice(h * HEAD, (h + 1) * HEAD)
            k = jnp.concatenate([r[:, lanes] for r in k_refs]) if parts > 1 else k_refs[0][:, lanes]
            v = jnp.concatenate([r[:, lanes] for r in v_refs]) if parts > 1 else v_refs[0][:, lanes]
            for b in range(rows // QB):
                block = slice(b * QB, (b + 1) * QB)
                s = dot_nt(k, q_ref[block, lanes]) * FACTOR
                if biases:
                    s = s + b_refs[0][...]
                top = jnp.max(s, axis=0, keepdims=True)
                e = jnp.exp(s - top)
                total = jnp.sum(e, axis=0, keepdims=True)
                lse_ref[h : h + 1, block] = top + jnp.log(total)
                o = dot_tn(v, e.astype(BF)) * (1.0 / total)
                out_ref[block, lanes] = jnp.transpose(o).astype(BF)
        wait(copies)
        mine_ref[...] = dot_nt(out_ref[:half], w[...])
        theirs_ref[...] = dot_nt(out_ref[half:], w[...]).astype(BF)

    return run(
        kernel,
        [shape((rows, wide), BF), shape((8, rows), F32), shape((half, D), F32), shape((half, D), BF)],
        [q, *ks, *vs, *biases],
        pieces,
        weight(n, wide),
        flops=2 * rows * wide * (2 * nk + D),
        exps=rows * nk * heads,
    )


def attend_back(xs, pieces, first, q, ks, vs, bias, lse, sofar):
    rows, wide = q.shape
    heads = wide // HEAD
    nk = sum(k.shape[0] for k in ks)
    n = len(pieces)
    parts = len(ks)
    biases = [] if bias is None else [bias]

    def kernel(*refs):
        x_refs, q_ref, refs = refs[:2], refs[2], refs[3:]
        k_refs, v_refs, lse_ref, refs = refs[:parts], refs[parts : 2 * parts], refs[2 * parts], refs[2 * parts + 1 :]
        b_refs, refs = refs[: len(biases)], refs[len(biases) :]
        old_refs, refs = refs[: len(sofar)], refs[len(sofar) :]
        piece_refs, (dq_ref, dk_ref, dv_ref, w, sems, do_ref) = refs[:n], refs[n:]
        wait(load(piece_refs, w, sems, first))
        for i in range(2):
            m = x_refs[i].shape[0]
            do_ref[i * m : (i + 1) * m] = dot_nn(x_refs[i][...], w[...]).astype(BF)
        for h in range(heads):
            lanes = slice(h * HEAD, (h + 1) * HEAD)
            k = jnp.concatenate([r[:, lanes] for r in k_refs]) if parts > 1 else k_refs[0][:, lanes]
            v = jnp.concatenate([r[:, lanes] for r in v_refs]) if parts > 1 else v_refs[0][:, lanes]
            for b in range(rows // QB):
                block = slice(b * QB, (b + 1) * QB)
                qb = q_ref[block, lanes]
                do = do_ref[block, lanes]
                s = dot_nt(k, qb) * FACTOR
                if biases:
                    s = s + b_refs[0][...]
                p = jnp.exp(s - lse_ref[h : h + 1, block])
                dp = dot_nt(v, do)
                center = jnp.sum(p * dp, axis=0, keepdims=True)
                ds = (p * (dp - center)).astype(BF)
                dq_ref[block, lanes] = dot_tn(ds, k) * FACTOR
                dk = dot_nn(ds, qb) * FACTOR
                dv = dot_nn(p.astype(BF), do)
                if b == 0 and not sofar:
                    dk_ref[:, lanes] = dk
                    dv_ref[:, lanes] = dv
                elif b == 0:
                    dk_ref[:, lanes] = old_refs[0][:, lanes] + dk
                    dv_ref[:, lanes] = old_refs[1][:, lanes] + dv
                else:
                    dk_ref[:, lanes] += dk
                    dv_ref[:, lanes] += dv

    return run(
        kernel,
        [shape((rows, wide), F32), shape((nk, wide), F32), shape((nk, wide), F32)],
        [*xs, q, *ks, *vs, lse, *biases, *sofar],
        pieces,
        weight(n, wide) + [pltpu.VMEM((rows, wide), BF)],
        flops=2 * rows * wide * (5 * nk + D),
        exps=rows * nk * heads,
    )


def root_dots(dys, raws, stats, gains, tables, wide):
    count = len(gains)
    outs = [shape(dy.shape, F32) for dy in dys] if tables else []
    outs += [shape((8, dy.shape[0]), F32) for dy in dys]
    outs += [shape((8, wide), F32)]

    def kernel(*refs):
        dy_refs, refs = refs[:count], refs[count:]
        raw_refs, refs = refs[:count], refs[count:]
        stat_refs, refs = refs[:count], refs[count:]
        gain_refs, refs = refs[:count], refs[count:]
        if tables:
            cos_ref, sin_ref, refs = refs[0], refs[1], refs[2:]
            turned, refs = refs[:count], refs[count:]
        dot_refs, grad_ref = refs[:count], refs[count]
        grad_ref[...] = jnp.zeros_like(grad_ref)
        for i in range(count):
            row = raws[i][2]
            m = dy_refs[i].shape[0]
            scale = lax.rsqrt(to_columns(stat_refs[i][...]) / D + EPS)[:, row : row + 1]
            dots = jnp.zeros((m, 1), F32)
            for h in range(wide // HEAD):
                own = slice(h * HEAD, (h + 1) * HEAD)
                dy = dy_refs[i][:, own]
                if tables:
                    dy = turn(dy, cos_ref[...], -sin_ref[...])
                    turned[i][:, own] = dy
                c = raws[i][1] + h * HEAD
                both = raw_refs[i][:, c : c + HEAD] * dy
                dots = dots + jnp.sum(both * gain_refs[i][:, own], axis=1, keepdims=True)
                grad_ref[i : i + 1, own] = jnp.sum(both * scale, axis=0, keepdims=True)
            dot_refs[i][...] = to_rows([dots], m)

    args = [*dys, *(r[0] for r in raws), *stats, *gains]
    if tables:
        args += [*tables]
    return run(kernel, outs, args, flops=1e9)


def root_back(dys, raws, stats, dots, gains, dv, pieces, first, wide, halves):
    count = len(gains)
    extra = 0 if dv is None else 1
    rows = dys[0].shape[0]
    cols = (count + extra) * wide
    n = len(pieces)
    part = rows // (2 * halves)
    vs = [] if dv is None else [dv]

    def kernel(*refs):
        dy_refs, refs = refs[:count], refs[count:]
        raw_refs, refs = refs[:count], refs[count:]
        stat_refs, refs = refs[:count], refs[count:]
        dot_refs, refs = refs[:count], refs[count:]
        gain_refs, refs = refs[:count], refs[count:]
        v_refs, refs = refs[:extra], refs[extra:]
        piece_refs, refs = refs[:n], refs[n:]
        low_ref, refs = refs[0], refs[1:]
        mine_refs, their_refs, (w, sems) = refs[:halves], refs[halves : 2 * halves], refs[2 * halves :]
        copies = load(piece_refs, w, sems, first)
        for i in range(count):
            row = raws[i][2]
            scale = lax.rsqrt(to_columns(stat_refs[i][...]) / D + EPS)[:, row : row + 1]
            along = scale * scale * scale * to_columns(dot_refs[i][...])[:, 0:1] / D
            for h in range(wide // HEAD):
                own = slice(h * HEAD, (h + 1) * HEAD)
                c = raws[i][1] + h * HEAD
                dx = scale * gain_refs[i][:, own] * dy_refs[i][:, own] - raw_refs[i][:, c : c + HEAD] * along
                low_ref[:, i * wide + h * HEAD : i * wide + (h + 1) * HEAD] = dx.astype(BF)
        if extra:
            low_ref[:, count * wide :] = v_refs[0][...].astype(BF)
        wait(copies)
        for j in range(halves):
            at = 2 * part * j
            mine_refs[j][...] = dot_nt(low_ref[at : at + part], w[...])
            their_refs[j][...] = dot_nt(low_ref[at + part : at + 2 * part], w[...]).astype(BF)

    return run(
        kernel,
        [shape((rows, cols), BF)]
        + [shape((part, D), F32)] * halves
        + [shape((part, D), BF)] * halves,
        [*dys, *(r[0] for r in raws), *stats, *dots, *gains, *vs],
        pieces,
        weight(n, cols),
        flops=2 * rows * cols * D,
    )


HC = 768


def expand(xs, pieces, first, hid):
    rows = sum(x.shape[0] for x in xs)
    n = len(pieces)

    def kernel(*refs):
        x_refs, piece_refs, (out_ref, w, sems) = refs[: len(xs)], refs[len(xs) : len(xs) + n], refs[len(xs) + n :]
        chunks = [load(piece_refs[j : j + 1], w.at[j], sems.at[j], first) for j in range(hid // HC)]
        for j in range(hid // HC):
            wait(chunks[j])
            at = 0
            for x_ref in x_refs:
                m = x_ref.shape[0]
                out_ref[at : at + m, j * HC : (j + 1) * HC] = dot_nn(x_ref[...], w[j]).astype(BF)
                at += m

    return run(
        kernel,
        [shape((rows, hid), BF)],
        xs,
        pieces,
        [pltpu.VMEM((hid // HC, D, HC), BF), pltpu.SemaphoreType.DMA((hid // HC, 1))],
        flops=2 * rows * D * hid,
    )[0]


def feed(xs, dact, pieces, first):
    rows, hid = dact.shape
    n = len(pieces)
    m = rows // 2

    def kernel(*refs):
        x_refs, dact_ref, piece_refs = refs[:2], refs[2], refs[3 : 3 + n]
        act_ref, dpre_ref, mine_ref, theirs_ref, w, sems = refs[3 + n :]
        chunks = [load(piece_refs[j : j + 1], w.at[j], sems.at[j], first) for j in range(hid // HC)]
        for j in range(hid // HC):
            cols = slice(j * HC, (j + 1) * HC)
            wait(chunks[j])
            for i in range(2):
                own = slice(i * m, (i + 1) * m)
                u = dot_nn(x_refs[i][...], w[j])
                sq = u * u
                th = jnp.tanh(u * (GELU + GELU * CUBE * sq))
                near = 0.5 + 0.5 * th
                act_ref[own, cols] = (u * near).astype(BF)
                slope = near + u * near * (1.0 - th) * (GELU + 3 * GELU * CUBE * sq)
                dpre_ref[own, cols] = (dact_ref[own, cols].astype(F32) * slope).astype(BF)
        for i in range(2):
            own = slice(i * m, (i + 1) * m)
            total = dot_nt(dpre_ref[own, :HC], w[0])
            for j in range(1, hid // HC):
                total = total + dot_nt(dpre_ref[own, j * HC : (j + 1) * HC], w[j])
            if i == 0:
                mine_ref[...] = total
            else:
                theirs_ref[...] = total.astype(BF)

    return run(
        kernel,
        [shape((rows, hid), BF), shape((rows, hid), BF), shape((m, D), F32), shape((m, D), BF)],
        [*xs, dact],
        pieces,
        [pltpu.VMEM((hid // HC, D, HC), BF), pltpu.SemaphoreType.DMA((hid // HC, 1))],
        flops=4 * rows * D * hid,
        exps=rows * hid,
        limit=60,
    )


def contract(act, pieces, first):
    rows, hid = act.shape
    n = len(pieces)
    m = rows // 2

    def kernel(*refs):
        act_ref, piece_refs, (mine_ref, theirs_ref, w, sems) = refs[0], refs[1 : 1 + n], refs[1 + n :]
        chunks = [load(piece_refs[j : j + 1], w.at[j], sems.at[j], first) for j in range(hid // HC)]
        for chunk in chunks:
            wait(chunk)
        for i in range(2):
            own = slice(i * m, (i + 1) * m)
            total = dot_nt(act_ref[own, :HC], w[0])
            for j in range(1, hid // HC):
                total = total + dot_nt(act_ref[own, j * HC : (j + 1) * HC], w[j])
            if i == 0:
                mine_ref[...] = total
            else:
                theirs_ref[...] = total.astype(BF)

    return run(
        kernel,
        [shape((m, D), F32), shape((m, D), BF)],
        [act],
        pieces,
        [pltpu.VMEM((hid // HC, D, HC), BF), pltpu.SemaphoreType.DMA((hid // HC, 1))],
        flops=2 * rows * D * hid,
    )


GC = 384


def full_grads(xs, ys):
    cols = ys[0].shape[1]
    most = sum(x.shape[0] for x in xs)

    def kernel(*refs):
        x_refs, y_refs, (out_ref, turned) = refs[: len(xs)], refs[len(xs) : -2], refs[-2:]
        row = 0
        for x_ref in x_refs:
            m = x_ref.shape[0]
            turned[:, row : row + m] = jnp.transpose(x_ref[...])
            row += m
        for c in range(0, cols, HC):
            lanes = slice(c, c + HC)
            for k in range(0, D, 512):
                row = 0
                total = None
                for y_ref in y_refs:
                    m = y_ref.shape[0]
                    term = dot_nn(turned[k : k + 512, row : row + m], y_ref[:, lanes])
                    total = term if total is None else total + term
                    row += m
                out_ref[k : k + 512, lanes] = total.astype(BF)

    return run(
        kernel,
        [shape((D, cols), BF)],
        [*xs, *ys],
        (),
        [pltpu.VMEM((D, most), BF)],
        flops=2 * most * D * cols,
        limit=60,
    )[0]


def weight_grads(pairs, n, after=()):
    widths = [ys[0].shape[1] for _, ys in pairs]
    cols = sum(widths)
    r = D // n
    flat = [a for xs, ys in pairs for a in (*xs, *ys)]
    out = shape((n // 2, r, cols), BF)
    most = max(sum(x.shape[0] for x in xs) for xs, _ in pairs)

    def kernel(*refs):
        ins, refs = refs[: len(flat)], refs[len(flat) + len(after) :]
        theirs_ref, mine_ref, total_ref, turned, sems = refs
        minor = lax.axis_index("dp") % 2
        at = 0
        col = 0
        copies = []
        for p, (xs, ys) in enumerate(pairs):
            x_refs, y_refs = ins[at : at + len(xs)], ins[at + len(xs) : at + len(xs) + len(ys)]
            at += len(xs) + len(ys)
            row = 0
            for x_ref in x_refs:
                m = x_ref.shape[0]
                turned[:, row : row + m] = jnp.transpose(x_ref[...])
                row += m
            for c in range(0, widths[p], GC):
                lanes = slice(c, c + GC)
                for k in range(0, D, 512):
                    row = 0
                    total = None
                    for y_ref in y_refs:
                        m = y_ref.shape[0]
                        term = dot_nn(turned[k : k + 512, row : row + m], y_ref[:, lanes])
                        total = term if total is None else total + term
                        row += m
                    total_ref[k : k + 512, col + c : col + c + GC] = total.astype(BF)
                for j in range(n // 2):
                    for flip, ref in ((1, theirs_ref), (0, mine_ref)):
                        block = 2 * j + (1 - minor if flip else minor)
                        copy = pltpu.make_async_copy(
                            total_ref.at[
                                pl.ds(pl.multiple_of(block * r, 16), r), pl.ds(col + c, GC)
                            ],
                            ref.at[j, :, pl.ds(col + c, GC)],
                            sems.at[(col + c) // GC, 2 * j + flip],
                        )
                        copy.start()
                        copies.append(copy)
            col += widths[p]
        wait(copies)

    moved = sum(math.prod(v.shape) * 2 for v in flat) + 2 * D * cols
    return pl.pallas_call(
        kernel,
        out_shape=(out, out),
        in_specs=[pl.BlockSpec(memory_space=pltpu.VMEM)] * len(flat)
        + [pl.BlockSpec(memory_space=pl.ANY)] * len(after),
        out_specs=(pl.BlockSpec(memory_space=pl.ANY),) * 2,
        scratch_shapes=[
            pltpu.VMEM((D, cols), BF),
            pltpu.VMEM((D, most), BF),
            pltpu.SemaphoreType.DMA((cols // GC, n)),
        ],
        compiler_params=pltpu.CompilerParams(vmem_limit_bytes=60 * 2**20),
        cost_estimate=pl.CostEstimate(
            flops=int(2 * most * D * cols), bytes_accessed=moved, transcendentals=0
        ),
    )(*flat, *after)


def run_remote(kernel, outs, far_outs, blocks, far, scratch, cid, flops):
    moved = sum(math.prod(v.shape) * v.dtype.itemsize for v in (*blocks, *outs))
    vmem, hbm = pl.BlockSpec(memory_space=pltpu.VMEM), pl.BlockSpec(memory_space=pl.ANY)
    return pl.pallas_call(
        kernel,
        out_shape=(*outs, *far_outs),
        in_specs=[vmem] * len(blocks) + [hbm] * len(far),
        out_specs=(vmem,) * len(outs) + (hbm,) * len(far_outs),
        scratch_shapes=list(scratch),
        compiler_params=pltpu.CompilerParams(
            vmem_limit_bytes=60 * 2**20, collective_id=cid, has_side_effects=True
        ),
        cost_estimate=pl.CostEstimate(flops=int(flops), bytes_accessed=moved, transcendentals=0),
    )(*blocks, *far)


def tensor_peers():
    t = lax.axis_index("tensor")
    core = t + 1 - 2 * lax.rem(t, 2)
    across = lax.rem(t + 2, 4)
    return t, core, across, 3 - t


def greet(n_dp):
    d = lax.axis_index("dp")
    barrier = pltpu.get_barrier_semaphore()
    for k in range(1, n_dp):
        pl.semaphore_signal(
            barrier, inc=1, device_id={"dp": lax.rem(d + k, n_dp)}, device_id_type=MESH
        )
    for peer in tensor_peers()[1:]:
        pl.semaphore_signal(barrier, inc=1, device_id={"tensor": peer}, device_id_type=MESH)
    pl.semaphore_wait(barrier, n_dp + 2)


def remote(src, dst, send, recv, **place):
    return pltpu.make_async_remote_copy(
        src_ref=src, dst_ref=dst, send_sem=send, recv_sem=recv, device_id=place, device_id_type=MESH
    )


class Gather:
    def __init__(self, ref, sems, n):
        d = lax.axis_index("dp")
        self.z, self.y = d // 2, lax.rem(d, 2)
        self.ref, self.sems, self.n, self.r = ref, sems, n, ref.shape[0] // (2 * n)

    def block(self, o, y):
        return self.ref.at[pl.ds(pl.multiple_of((2 * o + y) * self.r, 16), self.r)]

    def copy(self, o, kind, index, z, y, own=True):
        block = self.block(o, self.y if own else 1 - self.y)
        sems = self.sems
        return remote(
            block, block, sems.at[2 * kind, index], sems.at[2 * kind + 1, index], dp=2 * z + y
        )

    def up(self, s):
        return self.copy(self.z - s, 0, s, self.z + 1, self.y)

    def down(self, s):
        return self.copy(self.z + s, 1, s, self.z - 1, self.y)

    def over(self, o):
        return self.copy(o, 2, o, self.z, 1 - self.y)

    def start(self, own, sem):
        copy = pltpu.make_async_copy(own, self.block(self.z, self.y), sem)
        copy.start()
        copy.wait()
        pl.when(self.z < self.n - 1)(lambda: self.up(0).start())
        pl.when(self.z > 0)(lambda: self.down(0).start())
        self.over(self.z).start()

    def step(self, s):
        z, n = self.z, self.n

        @pl.when(z - 1 - s >= 0)
        def _():
            self.copy(z - 1 - s, 0, s, z - 1, self.y).wait_recv()
            pl.when(z < n - 1)(lambda: self.up(s + 1).start())
            self.over(z - 1 - s).start()

        @pl.when(z + 1 + s <= n - 1)
        def _():
            self.copy(z + 1 + s, 1, s, z + 1, self.y).wait_recv()
            pl.when(z > 0)(lambda: self.down(s + 1).start())
            self.over(z + 1 + s).start()

    def finish(self):
        for o in range(self.n):
            self.copy(o, 2, o, self.z, 1 - self.y, own=False).wait_recv()

    def drain(self):
        z, n = self.z, self.n
        for s in range(n - 1):
            pl.when((z - s >= 0) & (z < n - 1))(lambda: self.up(s).wait_send())
            pl.when((z + s <= n - 1) & (z > 0))(lambda: self.down(s).wait_send())
        for o in range(n):
            self.over(o).wait_send()


class Swap:
    def __init__(self, sems):
        self.sems, self.used, self.sent = sems, 0, []

    def start(self, src, dst, peer):
        k = self.used
        self.used += 1
        copy = remote(src, dst, self.sems.at[0, k], self.sems.at[1, k], tensor=peer)
        copy.start()
        self.sent.append(copy)
        return copy

    def settle(self):
        for copy in self.sent:
            copy.wait_send()
        self.sent = []


class Sums:
    def __init__(self, landed, sems, peers):
        self.landed, self.peers, self.used = landed, peers, 0
        self.swap = Swap(sems)

    def start(self, ref):
        k, c = self.used, ref.shape[1]
        self.used += 1
        copies = [
            self.swap.start(ref, self.landed.at[k, p, :, pl.ds(0, c)], peer)
            for p, peer in enumerate(self.peers)
        ]

        def collect():
            for copy in copies:
                copy.wait()
            stat_sum(ref, [self.landed[k, p, :, :c] for p in range(3)])

        return collect


def project_body(x_refs, w, first, out_ref, low_ref, stat_ref, squares, lows, wide):
    at = 0
    for x_ref in x_refs:
        m = x_ref.shape[0]
        value = dot_nn(x_ref[...], w[:, first : first + (squares + lows) * wide])
        columns = []
        for i in range(squares):
            part = value[:, i * wide : (i + 1) * wide]
            columns.append(jnp.sum(part * part, axis=1, keepdims=True))
        out_ref[at : at + m] = value[:, : squares * wide]
        stat_ref[:, at : at + m] = to_rows(columns, m)
        if lows:
            low_ref[at : at + m] = value[:, squares * wide :].astype(BF)
        at += m


def normalize_body(raw_ref, stat_ref, gains, cos, sin, out_refs, wide):
    scale = lax.rsqrt(to_columns(stat_ref[...]) / D + EPS)
    for i, out_ref in enumerate(out_refs):
        for h in range(wide // HEAD):
            lanes = slice(i * wide + h * HEAD, i * wide + (h + 1) * HEAD)
            value = raw_ref[:, lanes] * scale[:, i : i + 1] * gains[i][h]
            if cos is not None:
                value = turn(value, cos, sin)
            out_ref[:, h * HEAD : (h + 1) * HEAD] = value.astype(BF)


def attend_body(q_ref, k_refs, v_refs, bias_ref, out_ref, lse_ref):
    rows, wide = q_ref.shape
    lse_ref[...] = jnp.zeros_like(lse_ref)
    for h in range(wide // HEAD):
        lanes = slice(h * HEAD, (h + 1) * HEAD)
        k = jnp.concatenate([r[:, lanes] for r in k_refs]) if len(k_refs) > 1 else k_refs[0][:, lanes]
        v = jnp.concatenate([r[:, lanes] for r in v_refs]) if len(v_refs) > 1 else v_refs[0][:, lanes]
        for b in range(rows // QB):
            block = slice(b * QB, (b + 1) * QB)
            s = dot_nt(k, q_ref[block, lanes]) * FACTOR
            if bias_ref is not None:
                s = s + bias_ref[...]
            top = jnp.max(s, axis=0, keepdims=True)
            e = jnp.exp(s - top)
            total = jnp.sum(e, axis=0, keepdims=True)
            lse_ref[h : h + 1, block] = top + jnp.log(total)
            o = dot_tn(v, e.astype(BF)) * (1.0 / total)
            out_ref[block, lanes] = jnp.transpose(o).astype(BF)


def stat_sum(stat_ref, landed):
    h = stat_ref.shape[1] // 2
    other = landed[0] + landed[2]
    total = stat_ref[...] + landed[1]
    stat_ref[:, :h] = total[:, :h] + other[:, h:]
    stat_ref[:, h:] = total[:, h:] + other[:, :h]


def join_body(mine, got, chip):
    def body(i):
        chip[i] = (mine[i] + got[i].astype(F32)).astype(BF)

    over_rows(mine.shape[0], body)


def stream_body(base, chip, far, s, m, t, out_ref, rows_ref):
    def body(i):
        out = base(i) + (chip[i].astype(F32) + far[i].astype(F32)) * s
        out_ref[i] = out
        n, _ = norm_of(out)
        rows_ref[i] = (n * m + t).astype(BF)

    over_rows(rows_ref.shape[0], body)


def self_forward(hidden, context, cotangent, time_rows, tables, small, own_self, own_cross, own_first, n_dp, heads):
    quarter, texts = hidden.shape[0], context.shape[0]
    half, wide = 2 * quarter, heads * HEAD
    n = n_dp // 2
    r = D // n_dp
    g_cols = HEAD // n_dp
    rows = shape((quarter, D), BF)
    outs = dict(
        w_self=shape((D, 4 * wide), BF), w_cross=shape((D, 4 * wide), BF), got=rows,
        c0=shape((texts, D), BF), c1=shape((texts, D), BF), c2=shape((texts, D), BF), c3=shape((texts, D), BF),
        shifts=shape((8, D), F32), gains=shape((16, HEAD), F32),
        x0=rows, x1=rows, x2=rows, x3=rows,
        qk0=shape((half, 2 * wide), F32), qk1=shape((half, 2 * wide), F32),
        v0=shape((half, wide), BF), v1=shape((half, wide), BF),
        stat0=shape((8, half), F32), stat1=shape((8, half), F32),
        q0=shape((half, wide), BF), q1=shape((half, wide), BF),
        k0=shape((half, wide), BF), k1=shape((half, wide), BF),
        attn0=shape((half, wide), BF), attn1=shape((half, wide), BF),
        lse0=shape((8, half), F32), lse1=shape((8, half), F32),
        chip0=rows, chip1=rows, far0=rows, far1=rows,
        after0=shape((quarter, D), F32), after1=shape((quarter, D), F32),
        y0=rows, y1=rows, y2=rows, y3=rows,
        ck_raw=shape((4 * texts, wide), F32), cv=shape((4 * texts, wide), BF),
        ck_stat=shape((8, 4 * texts), F32), ck=shape((4 * texts, wide), BF),
    )
    far_outs = dict(f0=shape((D, own_first.shape[1]), BF), g_got=rows)
    blocks = [hidden, context, time_rows, tables[0], tables[1], small]
    far = [own_self, own_cross, own_first, cotangent]
    names = [*outs, *far_outs]

    def kernel(*refs):
        hid, ctx, times, cos, sin, small_ref = refs[:6]
        own1, own2, own3, cot = refs[6:10]
        o = dict(zip(names, refs[10 : 10 + len(names)]))
        all_small, ctx_got, theirs, landed, mine, stats_in, ring, near, cross_x, near_sums, small_sems, local = refs[
            10 + len(names) :
        ]
        t, core, across, diagonal = tensor_peers()
        first = t < 2
        d = lax.axis_index("dp")
        cores, xs = Swap(near), Swap(cross_x)
        greet(n_dp)

        g1 = Gather(o["w_self"], ring.at[0], n)
        g2 = Gather(o["w_cross"], ring.at[1], n)
        g3 = Gather(o["f0"], ring.at[2], n)
        g1.start(own1, local.at[0])
        own_small = all_small.at[pl.ds(pl.multiple_of(d * r, 16), r)]
        own_small[...] = small_ref[...]
        small_copies = []
        for k in range(1, n_dp):
            copy = remote(
                own_small, own_small, small_sems.at[0, k], small_sems.at[1, k], dp=lax.rem(d + k, n_dp)
            )
            copy.start()
            small_copies.append(copy)
        hid_copy = xs.start(hid, o["got"], across)
        ctx_copy = xs.start(ctx, ctx_got, across)
        g_copy = xs.start(cot, o["g_got"], across)

        for k in range(1, n_dp):
            source = lax.rem(d - k + n_dp, n_dp)
            block = all_small.at[pl.ds(pl.multiple_of(source * r, 16), r)]
            remote(block, block, small_sems.at[0, k], small_sems.at[1, k], dp=source).wait_recv()
        turned = jnp.transpose(all_small[...].astype(F32))
        o["shifts"][:6] = turned[:6] + times[...]
        o["shifts"][6:] = turned[6:8]
        at = lax.broadcasted_iota(jnp.int32, (D, HEAD), 0)
        to = lax.broadcasted_iota(jnp.int32, (D, HEAD), 1)
        pick = (at == (to // g_cols) * r + lax.rem(to, g_cols)).astype(F32)
        o["gains"][...] = dot_nn(turned[8:24].astype(BF), pick.astype(BF))
        g1.step(0)

        hid_copy.wait_recv()
        m_row, t_row = 1.0 + o["shifts"][1:2], o["shifts"][0:1]
        slots = [o["x0"], o["x1"], o["x2"], o["x3"]]

        def base(j):
            def pick_rows(i):
                own, other = hid[i].astype(F32), o["got"][i].astype(F32)
                return jnp.where(first, own, other) if j == 0 else jnp.where(first, other, own)

            return pick_rows

        arrivals = []
        for j in range(2):

            def body(i, j=j):
                v, _ = norm_of(base(j)(i))
                slots[2 * j][i] = (v * m_row + t_row).astype(BF)

            over_rows(quarter, body)
            arrivals.append(cores.start(slots[2 * j], slots[2 * j + 1], core))
        g1.step(1)
        ctx_copy.wait_recv()
        c_slots = [o["c0"], o["c1"], o["c2"], o["c3"]]
        a, b = ctx[...].astype(F32), ctx_got[...].astype(F32)
        c_slots[0][...] = jnp.where(first, a, b).astype(BF)
        c_slots[2][...] = jnp.where(first, b, a).astype(BF)
        c_arrivals = [cores.start(c_slots[2 * j], c_slots[2 * j + 1], core) for j in range(2)]
        for s in range(2, n - 1):
            g1.step(s)
        g2.start(own2, local.at[0])
        g1.finish()
        g2.step(0)

        qk, v = [o["qk0"], o["qk1"]], [o["v0"], o["v1"]]
        stat = [o["stat0"], o["stat1"]]
        w_self, w_cross = o["w_self"], o["w_cross"]

        sums = Sums(stats_in, near_sums, (core, across, diagonal))
        shared = []
        for j in range(2):
            arrivals[j].wait_recv()
            project_body(slots[2 * j : 2 * j + 2], w_self, 0, qk[j], v[j], stat[j], 2, 1, wide)
            shared.append(sums.start(stat[j]))
            if j == 0 and n > 2:
                g2.step(1)
        q, k = [o["q0"], o["q1"]], [o["k0"], o["k1"]]
        gain = [[o["gains"][i * heads + h : i * heads + h + 1] for h in range(heads)] for i in range(4)]
        for s in range(2, n - 1):
            g2.step(s)
        g3.start(own3, local.at[0])
        for j in range(2):
            shared[j]()
            own = slice(j * half, (j + 1) * half)
            normalize_body(qk[j], stat[j], gain[:2], cos[own], sin[own], [q[j], k[j]], wide)

        attn, lse = [o["attn0"], o["attn1"]], [o["lse0"], o["lse1"]]
        sent = []
        for j in range(2):
            attend_body(q[j], k, v, None, attn[j], lse[j])
            w_out = w_self[:, 3 * wide :]
            theirs[j] = dot_nt(attn[j][quarter:], w_out).astype(BF)
            sent.append(cores.start(theirs.at[j], landed.at[j], core))
            mine[j] = dot_nt(attn[j][:quarter], w_out)
            if j == 0:
                g3.step(0)
        chip, far_refs = [o["chip0"], o["chip1"]], [o["far0"], o["far1"]]
        crossed = []
        for j in range(2):
            sent[j].wait_recv()
            join_body(mine.at[j], landed.at[j], chip[j])
            crossed.append(xs.start(chip[j], far_refs[j], across))
        if n > 2:
            g3.step(1)

        g2.finish()
        for copy in c_arrivals:
            copy.wait_recv()
        project_body(c_slots, w_cross, wide, o["ck_raw"], o["cv"], o["ck_stat"], 1, 1, wide)
        halves = 2 * texts
        for j in range(2):
            part = o["ck_stat"].at[:, pl.ds(j * halves, halves)]
            sums.start(part)()
        normalize_body(o["ck_raw"], o["ck_stat"], gain[3:], None, None, [o["ck"]], wide)

        after = [o["after0"], o["after1"]]
        y_slots = [o["y0"], o["y1"], o["y2"], o["y3"]]
        shifts = o["shifts"]
        passed = []
        for j in range(2):
            crossed[j].wait_recv()
            stream_body(
                base(j), chip[j], far_refs[j], shifts[2:3], shifts[6:7], shifts[7:8], after[j], y_slots[2 * j]
            )
            passed.append(cores.start(y_slots[2 * j], y_slots[2 * j + 1], core))
            if j == 0:
                for s in range(2, n - 1):
                    g3.step(s)
        for copy in passed:
            copy.wait_recv()
        g_copy.wait_recv()
        g3.finish()
        for g in (g1, g2, g3):
            g.drain()
        for copy in small_copies:
            copy.wait_send()
        cores.settle()
        xs.settle()

    scratch = [
        pltpu.VMEM((D, HEAD), BF),
        pltpu.VMEM((texts, D), BF),
        pltpu.VMEM((2, quarter, D), BF),
        pltpu.VMEM((2, quarter, D), BF),
        pltpu.VMEM((2, quarter, D), F32),
        pltpu.VMEM((4, 3, 8, half), F32),
        pltpu.SemaphoreType.DMA((3, 6, n)),
        pltpu.SemaphoreType.DMA((2, 8)),
        pltpu.SemaphoreType.DMA((2, 8)),
        pltpu.SemaphoreType.DMA((2, 12)),
        pltpu.SemaphoreType.DMA((2, n_dp)),
        pltpu.SemaphoreType.DMA((1,)),
    ]
    got = run_remote(
        kernel, list(outs.values()), list(far_outs.values()), blocks, far, scratch, 1, 2e10
    )
    return dict(zip(names, got))


def cross_forward(state, bias, own_second, own_third, n_dp, heads):
    quarter = state["y0"].shape[0]
    half, wide = 2 * quarter, heads * HEAD
    n = n_dp // 2
    rows = shape((quarter, D), BF)
    outs = dict(
        cq_raw0=shape((half, wide), F32), cq_raw1=shape((half, wide), F32),
        cq_stat0=shape((8, half), F32), cq_stat1=shape((8, half), F32),
        cq0=shape((half, wide), BF), cq1=shape((half, wide), BF),
        cattn0=shape((half, wide), BF), cattn1=shape((half, wide), BF),
        clse0=shape((8, half), F32), clse1=shape((8, half), F32),
        after_c0=shape((quarter, D), F32), after_c1=shape((quarter, D), F32),
        z0=rows, z1=rows, z2=rows, z3=rows,
    )
    far_outs = dict(f1=shape((D, own_second.shape[1]), BF), f2=shape((D, own_third.shape[1]), BF))
    given = ("w_cross", "after0", "after1", "y0", "y1", "y2", "y3", "ck", "cv", "shifts", "gains")
    blocks = [state[name] for name in given] + [bias]
    far = [own_second, own_third]
    names = [*outs, *far_outs]

    def kernel(*refs):
        i = dict(zip(given, refs))
        bias_ref, own1, own2 = refs[len(given) : len(given) + 3]
        refs = refs[len(given) + 3 :]
        o = dict(zip(names, refs))
        theirs, landed, mine, chips, fars, stats_in, ring, near, cross_x, near_sums, local = refs[len(names) :]
        t, core, across, diagonal = tensor_peers()
        cores, xs = Swap(near), Swap(cross_x)
        sums = Sums(stats_in, near_sums, (core, across, diagonal))
        greet(n_dp)
        g1 = Gather(o["f1"], ring.at[0], n)
        g2 = Gather(o["f2"], ring.at[1], n)
        g1.start(own1, local.at[0])
        w = i["w_cross"]
        slots = [i["y0"], i["y1"], i["y2"], i["y3"]]
        raw, stat = [o["cq_raw0"], o["cq_raw1"]], [o["cq_stat0"], o["cq_stat1"]]
        q = [o["cq0"], o["cq1"]]
        attn, lse = [o["cattn0"], o["cattn1"]], [o["clse0"], o["clse1"]]
        gain = [i["gains"][2 * heads + h : 2 * heads + h + 1] for h in range(heads)]
        shared = []
        for j in range(2):
            project_body(slots[2 * j : 2 * j + 2], w, 0, raw[j], None, stat[j], 1, 0, wide)
            shared.append(sums.start(stat[j]))
        sent = []
        for j in range(2):
            shared[j]()
            normalize_body(raw[j], stat[j], [gain], None, None, [q[j]], wide)
            attend_body(q[j], [i["ck"]], [i["cv"]], bias_ref, attn[j], lse[j])
            w_out = w[:, 3 * wide :]
            theirs[j] = dot_nt(attn[j][quarter:], w_out).astype(BF)
            sent.append(cores.start(theirs.at[j], landed.at[j], core))
            mine[j] = dot_nt(attn[j][:quarter], w_out)
            if j == 0:
                g1.step(0)
        crossed = []
        for j in range(2):
            sent[j].wait_recv()
            join_body(mine.at[j], landed.at[j], chips.at[j])
            crossed.append(xs.start(chips.at[j], fars.at[j], across))
        for s in range(1, n - 1):
            g1.step(s)
        g2.start(own2, local.at[0])
        base = [i["after0"], i["after1"]]
        after = [o["after_c0"], o["after_c1"]]
        z_slots = [o["z0"], o["z1"], o["z2"], o["z3"]]
        m_row, t_row = 1.0 + i["shifts"][4:5], i["shifts"][3:4]
        passed = []
        for j in range(2):
            crossed[j].wait_recv()
            stream_body(
                lambda rows, j=j: base[j][rows], chips.at[j], fars.at[j], 1.0, m_row, t_row, after[j], z_slots[2 * j]
            )
            passed.append(cores.start(z_slots[2 * j], z_slots[2 * j + 1], core))
        for s in range(n - 1):
            g2.step(s)
        for copy in passed:
            copy.wait_recv()
        for g in (g1, g2):
            g.finish()
        for g in (g1, g2):
            g.drain()
        cores.settle()
        xs.settle()

    scratch = [
        pltpu.VMEM((2, quarter, D), BF),
        pltpu.VMEM((2, quarter, D), BF),
        pltpu.VMEM((2, quarter, D), F32),
        pltpu.VMEM((2, quarter, D), BF),
        pltpu.VMEM((2, quarter, D), BF),
        pltpu.VMEM((2, 3, 8, half), F32),
        pltpu.SemaphoreType.DMA((2, 6, n)),
        pltpu.SemaphoreType.DMA((2, 8)),
        pltpu.SemaphoreType.DMA((2, 8)),
        pltpu.SemaphoreType.DMA((2, 6)),
        pltpu.SemaphoreType.DMA((1,)),
    ]
    got = run_remote(
        kernel, list(outs.values()), list(far_outs.values()), blocks, far, scratch, 2, 1e10
    )
    return dict(zip(names, got))


def rotary_tables(positions, head_dim):
    pair_count = head_dim // 2
    side_pairs = pair_count // 3
    frame_pairs = pair_count - 2 * side_pairs
    pair_index = jnp.arange(pair_count)
    frame_mask = pair_index < frame_pairs
    height_mask = (pair_index >= frame_pairs) & (pair_index < frame_pairs + side_pairs)
    within = jnp.where(
        frame_mask,
        pair_index,
        jnp.where(height_mask, pair_index - frame_pairs, pair_index - frame_pairs - side_pairs),
    )
    extent = jnp.where(frame_mask, frame_pairs, side_pairs)
    frequency = jnp.power(10000.0, -within.astype(F32) / extent.astype(F32))
    coords = positions.astype(F32)
    coordinate = jnp.where(
        frame_mask[None, :],
        coords[0][:, None],
        jnp.where(height_mask[None, :], coords[1][:, None], coords[2][:, None]),
    )
    angles = jnp.repeat(coordinate * frequency[None, :], 2, axis=1)
    parity = jnp.arange(head_dim) % 2
    sign_pattern = jnp.where(parity == 0, -1.0, 1.0)
    return (jnp.cos(angles), jnp.sin(angles) * sign_pattern)


def solution(mesh):
    n_dp = mesh.shape["dp"]
    n_major = n_dp // 2
    pair_perm = [(i, i ^ 1) for i in range(n_dp)]
    ring_perm = {
        t: [((((i // 2) + t) % n_major) * 2 + i % 2, i) for i in range(n_dp)]
        for t in range(1, n_major)
    }
    back_perm = {t: [(b, a) for a, b in ring_perm[t]] for t in ring_perm}
    core_perm = [(i, i ^ 1) for i in range(4)]
    x_perm = [(i, i ^ 2) for i in range(4)]

    def core_swap(v):
        return lax.ppermute(v, "tensor", core_perm)

    def x_swap(v):
        return lax.ppermute(v, "tensor", x_perm)

    def gather_dp(block):
        pieces = []
        for t in range(n_major):
            piece = block if t == 0 else lax.ppermute(block, "dp", ring_perm[t])
            pieces += [piece, lax.ppermute(piece, "dp", pair_perm)]
        return pieces

    def scatter_dp(theirs, mine):
        major = lax.axis_index("dp") // 2
        got = lax.ppermute(theirs, "dp", pair_perm)

        def block(t):
            at = (major + t) % n_major
            a = lax.dynamic_slice_in_dim(mine, at, 1, axis=0)[0].astype(F32)
            return a + lax.dynamic_slice_in_dim(got, at, 1, axis=0)[0].astype(F32)

        arrived = [
            lax.ppermute(block(t).astype(BF), "dp", back_perm[t]) for t in range(1, n_major)
        ]
        total = block(0)
        for piece in arrived:
            total = total + piece.astype(F32)
        return total

    def join(mine, theirs):
        return (mine + core_swap(theirs).astype(F32)).astype(BF)

    def own_half(pair):
        first = lax.axis_index("tensor") < 2
        return jnp.where(first, pair[0], pair[1])

    def other_half(pair):
        first = lax.axis_index("tensor") < 2
        return jnp.where(first, pair[1], pair[0])

    def two_halves(own):
        got = x_swap(own)
        first = lax.axis_index("tensor") < 2
        return jnp.where(first, own, got), jnp.where(first, got, own)

    def sum_all(v):
        v = v + core_swap(v)
        return v + x_swap(v)

    def sum_vectors(v):
        h = v.shape[-1] // 2
        other = core_swap(v)
        v = v + jnp.concatenate([other[..., h:], other[..., :h]], -1)
        return v + x_swap(v)

    def sum_halves(pair):
        both = sum_vectors(jnp.stack(pair))
        return both[0], both[1]

    def quarters(values, axis):
        core = lax.axis_index("tensor") % 2
        step = values.shape[axis] // 4
        return jnp.concatenate(
            [
                lax.dynamic_slice_in_dim(values, at * step, step, axis)
                for at in (core, 1 - core, 2 + core, 3 - core)
            ],
            axis,
        )

    def on_device(
        hidden_in, context, time_emb, text_lengths, positions, modulation,
        self_query, self_key, self_value, self_output, self_query_gain, self_key_gain,
        cross_query, cross_key, cross_value, cross_output, cross_query_gain, cross_key_gain,
        norm_weight, norm_bias, ffn_up, ffn_down, out_cotangent,
    ):
        heads = self_query_gain.shape[0]
        half = positions.shape[1] // 2
        wide = heads * HEAD
        r_dp = self_query.shape[0]
        hid = ffn_up.shape[1]
        spare = -hid % HC

        texts = context.shape[1]
        quarter = half // 2
        g_cols = self_query_gain.shape[1]
        gains = [self_query_gain, self_key_gain, cross_query_gain, cross_key_gain]
        flat = jnp.concatenate([modulation, norm_weight[None], norm_bias[None]])
        side = jnp.pad(jnp.concatenate(gains), ((0, 0), (0, r_dp - g_cols)))
        small = jnp.concatenate([flat, side])
        small = jnp.pad(small, ((0, HEAD - small.shape[0]), (0, 0))).T.astype(BF)
        own_self = jnp.concatenate([self_query, self_key, self_value, self_output.T], axis=1).astype(BF)
        own_cross = jnp.concatenate([cross_query, cross_key, cross_value, cross_output.T], axis=1).astype(BF)
        padded = [jnp.pad(w, ((0, 0), (0, spare))) for w in (ffn_up.astype(BF), ffn_down.T.astype(BF))]
        hid_low = hid + spare
        own_ffn = [
            jnp.concatenate([w[:, j * HC : (j + 1) * HC] for w in padded], axis=1) for j in range(hid_low // HC)
        ]
        tables = rotary_tables(quarters(positions, 1), HEAD)
        text_bias = jnp.where(quarters(jnp.arange(4 * texts), 0) < text_lengths[0], 0.0, -1e30)
        text_bias = text_bias.astype(F32)[:, None]

        st = self_forward(
            hidden_in, context[0], out_cotangent, time_emb[0], tables, small,
            own_self, own_cross, own_ffn[0], n_dp, heads,
        )
        st |= cross_forward(st, text_bias, own_ffn[1], own_ffn[2], n_dp, heads)
        d = lax.axis_index("dp")
        cosine, sine = ((t[:half], t[half:]) for t in tables)
        s0, s1, s2, s3, s4, s5, norm_gain, norm_shift = (st["shifts"][i : i + 1] for i in range(8))
        sq_gain, sk_gain, cq_gain, ck_gain = (
            st["gains"][i * heads : (i + 1) * heads].reshape(1, wide) for i in range(4)
        )
        ones = jnp.ones((1, D), F32)
        w_self, w_cross = [st["w_self"]], [st["w_cross"]]
        w_ffn = [st["f0"], st["f1"], st["f2"]]
        at_o, at_cq, at_ck, at_co = 3 * wide, 0, wide, 3 * wide

        def both(name):
            return [st[name + "0"], st[name + "1"]]

        def four(name):
            return [[st[name + "0"], st[name + "1"]], [st[name + "2"], st[name + "3"]]]

        first = lax.axis_index("tensor") < 2
        g = [jnp.where(first, out_cotangent, st["g_got"]), jnp.where(first, st["g_got"], out_cotangent)]
        ctx = [st[f"c{i}"] for i in range(4)]
        self_rows, cross_rows, ffn_rows = four("x"), four("y"), four("z")
        qk, v, stat, q, k, attn, lse = (both(name) for name in ("qk", "v", "stat", "q", "k", "attn", "lse"))
        self_chip, self_far, after_self = both("chip"), both("far"), both("after")
        ck_raw, cv, ck_stat, ck = st["ck_raw"], st["cv"], st["ck_stat"], st["ck"]
        cq_raw, cq_stat, cq, cattn, clse = (both(name) for name in ("cq_raw", "cq_stat", "cq", "cattn", "clse"))
        after_cross = both("after_c")

        def with_peer(rows):
            return [rows, core_swap(rows)]

        dffn = [with_peer((a.astype(F32) * s5).astype(BF)) for a in g]
        dact = [expand(a, w_ffn, HC, hid_low) for a in dffn]
        act, dpre, mine, theirs = zip(*(feed(ffn_rows[i], dact[i], w_ffn, 0) for i in range(2)))
        ffn_chip = [join(a, b) for a, b in zip(mine, theirs)]
        ffn_far = [x_swap(a) for a in ffn_chip]
        g_c, rows, sums_f = zip(
            *(norm_backward(g[i], after_cross[i], ffn_chip[i], ffn_far[i], 1.0 + s4, ones) for i in range(2))
        )
        down_grad = full_grads(dffn[0] + dffn[1], act)
        down_grad = lax.psum_scatter(down_grad, "dp", scatter_dimension=0, tiled=True).astype(F32)
        up_grad = full_grads(ffn_rows[0] + ffn_rows[1], dpre)
        up_grad = lax.psum_scatter(up_grad, "dp", scatter_dimension=0, tiled=True).astype(F32)

        dcross = [with_peer(a) for a in rows]
        sofar = ()
        dcq = []
        for i in range(2):
            a, *sofar = attend_back(dcross[i], w_cross, at_co, cq[i], [ck], [cv], text_bias, clse[i], sofar)
            dcq.append(a)
        dck, dcv = sofar
        dcq_low, mine, theirs, cq_gain_grad = [], [], [], 0.0
        for i in range(2):
            raws = [(cq_raw[i], 0, 0)]
            dots, grad = root_dots([dcq[i]], raws, [cq_stat[i]], [cq_gain], None, wide)
            cq_gain_grad = cq_gain_grad + grad[0]
            low, a, b = root_back(
                [dcq[i]], raws, [cq_stat[i]], [sum_vectors(dots)], [cq_gain], None, w_cross, at_cq, wide, 1
            )
            dcq_low.append(low)
            mine.append(a)
            theirs.append(b)
        cross_in_chip = [join(a, b) for a, b in zip(mine, theirs)]
        cross_in_far = [x_swap(a) for a in cross_in_chip]
        g_s, rows, sums_c = zip(
            *(norm_backward(g_c[i], after_self[i], cross_in_chip[i], cross_in_far[i], norm_gain, s2) for i in range(2))
        )
        raws = [(ck_raw, 0, 0)]
        dots, grad = root_dots([dck], raws, [ck_stat], [ck_gain], None, wide)
        ck_gain_grad = grad[0]
        dots = jnp.concatenate(sum_halves((dots[:, : 2 * texts], dots[:, 2 * texts :])), -1)
        dckv, mine0, mine1, theirs0, theirs1 = root_back(
            [dck], raws, [ck_stat], [dots], [ck_gain], dcv, w_cross, at_ck, wide, 2
        )
        chip = [join(mine0, theirs0), join(mine1, theirs1)]
        context_grad = (own_half(chip).astype(F32) + x_swap(other_half(chip)).astype(F32)).astype(BF)
        cross_grad = scatter_dp(
            *weight_grads(
                [(cross_rows[0] + cross_rows[1], dcq_low), (ctx, [dckv]), (dcross[0] + dcross[1], cattn)], n_dp
            )
        )

        dself = [with_peer(a) for a in rows]
        oT_grad = scatter_dp(*weight_grads([(dself[0] + dself[1], attn)], n_dp))
        sofar = ()
        dq = []
        for i in range(2):
            a, *sofar = attend_back(dself[i], w_self, at_o, q[i], k, v, None, lse[i], sofar)
            dq.append(a)
        dk, dv = sofar
        dk, dv = (dk[:half], dk[half:]), (dv[:half], dv[half:])
        dqkv, mine, theirs = [], [], []
        turned, dots, self_gain_grad = [], [], 0.0
        for i in range(2):
            raws = [(qk[i], 0, 0), (qk[i], wide, 1)]
            tq, tk, dot_q, dot_k, grad = root_dots(
                [dq[i], dk[i]], raws, [stat[i]] * 2, [sq_gain, sk_gain], (cosine[i], sine[i]), wide
            )
            self_gain_grad = self_gain_grad + grad[:2]
            turned.append((tq, tk))
            dots.append(jnp.stack([dot_q, dot_k]))
        dots = sum_halves(dots)
        for i in range(2):
            raws = [(qk[i], 0, 0), (qk[i], wide, 1)]
            low, a, b = root_back(
                list(turned[i]), raws, [stat[i]] * 2, [dots[i][0], dots[i][1]],
                [sq_gain, sk_gain], dv[i], w_self, 0, wide, 1,
            )
            dqkv.append(low)
            mine.append(a)
            theirs.append(b)
        qkv_grad = scatter_dp(*weight_grads([(self_rows[0] + self_rows[1], dqkv)], n_dp))
        chip = [join(a, b) for a, b in zip(mine, theirs)]
        ones_row = jnp.ones((1, D), F32)
        hidden_grad, _, sums_s = norm_backward(
            own_half(g_s), hidden_in, own_half(chip), x_swap(other_half(chip)), 1.0 + s1, ones_row
        )
        hidden_grad = hidden_grad.astype(BF)

        mine, theirs = zip(*(contract(a, w_ffn, HC) for a in act))
        chip = [join(a, b) for a, b in zip(mine, theirs)]
        ffn_branch = own_half(chip).astype(F32) + x_swap(other_half(chip)).astype(F32)
        block_out = (own_half(after_cross) + ffn_branch * s5).astype(BF)

        self_branch = own_half(self_chip).astype(F32) + own_half(self_far).astype(F32)
        sums_f = own_half(sums_f)
        sums_c = own_half(sums_c)
        sums_own = jnp.stack(
            [
                jnp.sum(sums_s[:8], 0),
                jnp.sum(sums_s[8:], 0),
                jnp.sum(own_half(g_s) * self_branch, 0),
                jnp.sum(sums_f[:8], 0),
                jnp.sum(sums_f[8:], 0),
                jnp.sum(out_cotangent.astype(F32) * ffn_branch, 0),
                jnp.sum(sums_c[8:], 0),
                jnp.sum(sums_c[:8], 0),
            ]
        )
        sums_clip = sum_all(sums_own)
        time_grad = sums_clip[:6]
        low_sums = sums_clip.reshape(8, n_dp, r_dp).transpose(1, 0, 2).reshape(n_dp, -1)
        gain_grads = jnp.stack([self_gain_grad[0], self_gain_grad[1], cq_gain_grad, ck_gain_grad])
        low_gains = gain_grads.reshape(4 * heads, n_dp, g_cols).transpose(1, 0, 2).reshape(n_dp, -1)
        packed = jnp.concatenate([low_sums, low_gains], axis=1).astype(BF)
        packed = jnp.pad(packed, ((0, 0), (0, -packed.shape[1] % 1024))).reshape(n_major, 2, 8, -1)
        minor = d % 2
        tiny = scatter_dp(
            lax.dynamic_slice_in_dim(packed, 1 - minor, 1, 1)[:, 0],
            lax.dynamic_slice_in_dim(packed, minor, 1, 1)[:, 0],
        ).reshape(-1)
        eight = tiny[: 8 * r_dp].reshape(8, r_dp)
        gains_out = tiny[8 * r_dp : 8 * r_dp + 4 * heads * g_cols].reshape(4, heads, g_cols)

        return (
            block_out,
            hidden_grad,
            context_grad[None],
            time_grad[None],
            eight[:6],
            qkv_grad[:, :wide],
            qkv_grad[:, wide : 2 * wide],
            qkv_grad[:, 2 * wide :],
            oT_grad.T,
            gains_out[0],
            gains_out[1],
            cross_grad[:, :wide],
            cross_grad[:, wide : 2 * wide],
            cross_grad[:, 2 * wide : 3 * wide],
            cross_grad[:, 3 * wide :].T,
            gains_out[2],
            gains_out[3],
            eight[6],
            eight[7],
            up_grad[:, :hid],
            down_grad[:, :hid].T,
        )

    rows = P(("dp", "tensor"), None)
    col = P("dp", "tensor")
    row = P("tensor", "dp")
    text = P("dp", "tensor", None)
    time = P("dp", None, None)
    one = P("dp")
    ins = (
        rows, text, time, one, P(None, "dp"), P(None, "dp"),
        col, col, col, row, row, row,
        col, col, col, row, row, row,
        one, one, col, row, rows,
    )
    outs = (
        rows, rows, text, time, P(None, "dp"),
        col, col, col, row, row, row,
        col, col, col, row, row, row,
        one, one, col, row,
    )
    return jax.shard_map(on_device, mesh=mesh, in_specs=ins, out_specs=outs, check_vma=False)
```

time: 1080 us -> 833 us (0.77)
  Pallas kernels: 0 us -> 578 us
  waiting for transfers between devices: 461 us -> 88.8 us
  matrix products: 172 us -> 0 us
  local copies, waits for them, and re-layouts: 170 us -> 32.4 us
  other arithmetic: 138 us -> 50.2 us
  starting transfers between devices: 128 us -> 62.1 us
  between operations: 4.41 us -> 16.4 us
    pallas_call x0 -> x32, Pallas kernels: none -> 578 us  [the longest x2 335 us: run_remote(): pl.pallas_call(kernel, out_shape=(*outs, *far_outs), in_specs=[vmem] * le...]
    ppermute x60 -> x12, waiting for transfers between devices: 263 us -> 50.3 us  [scatter_dp(): lax.ppermute(block(t).astype(BF), 'dp', back_perm[t])]
    dot_general x33 -> x0, matrix products: 172 us -> none  [the longest x7 50.7 us: dot(): return jnp.dot(a, b, preferred_element_type=F32)]
    ppermute x6 -> x4, waiting for transfers between devices: 101 us -> 1.69 us  [scatter_dp(): got = lax.ppermute(theirs, 'dp', pair_perm)]
    ppermute x21 -> x12, waiting for transfers between devices: 94.5 us -> 36.4 us  [x_swap(): return lax.ppermute(v, 'tensor', x_perm)]
    ppermute x60 -> x12, starting transfers between devices: 94 us -> 38.4 us  [scatter_dp(): lax.ppermute(block(t).astype(BF), 'dp', back_perm[t])]
    dynamic_update_slice x43 -> x0, local copies, waits for them, and re-layouts: 41.9 us -> none  [the longest x19 22.4 us: gather_dp(): out = lax.dynamic_update_slice(out, piece[None], (origin + minor, 0, 0))]
    convert_element_type x29 -> x12, other arithmetic: 52.1 us -> 14.4 us  [the longest x4 6.53 us: scatter_dp(): block(t).astype(BF)]
  transfers between devices with their start and end apart: 108 -> 51, of which waited for: 40 -> 15; matrix products, arithmetic and copies ran while one was open for 38% -> 7% of each run, Pallas kernels for 0% -> 42%
where the time goes in v2:
time: 833 us; the launch traced here: 828 us
  Pallas kernels  578 us (69%)
  waiting for transfers between devices  88.8 us (11%)
  starting transfers between devices  62.1 us (7%)
  other arithmetic  50.2 us (6%)
  local copies, waits for them, and re-layouts  32.4 us (4%)
  between operations  16.4 us (2%)
    pallas_call x2, Pallas kernels, run_remote(): pl.pallas_call(kernel, out_shape=(*outs, *far_outs), in_specs=[vmem] * le...  335 us
    pallas_call x27, Pallas kernels, run(): pl.pallas_call(kernel, out_shape=tuple(outs), in_specs=[pl.BlockSpec(memo...  218 us
    ppermute x12, waiting for transfers between devices, scatter_dp(): lax.ppermute(block(t).astype(BF), 'dp', back_perm[t])  50.3 us
    ppermute x12, starting transfers between devices, scatter_dp(): lax.ppermute(block(t).astype(BF), 'dp', back_perm[t])  38.4 us
    ppermute x12, waiting for transfers between devices, x_swap(): return lax.ppermute(v, 'tensor', x_perm)  36.4 us
    pallas_call x3, Pallas kernels, weight_grads(): pl.pallas_call(kernel, out_shape=(out, out), in_specs=[pl.BlockSpec(memor...  24.7 us
  transfers between devices with their start and end apart: 51, of which 15 were waited for; matrix products, arithmetic and copies ran while one was open for 7% of the time, Pallas kernels for 42%

profile of v2, /device:TPU:0, one launch (start us, length us, event | category | flops | bytes accessed | tf_op | source)
XLA Modules:
  0.0 827.5 jit_solution(17507893983530775522)
XLA Ops:
  20.3 190.7 %shard_map.382 = (bf16[1536,1536]{1,0:T(8,128)(2,1)}, bf16[1536,1536]{1,0:T(8,128)(2,1)}, bf16[256,1536]{1,0:T(8,128)(2,1)}, bf16[128,1536]{1,0:T(8,128)(2,1)}, ...) custom-call(bf16[256,1536]{1,0:T(8,128)(2,1)} %v_ref.1, ...), custom_call_target="tpu_custom_call" | custom-call | flops 20000000000 | bytes 34697216 | tf_op jit(solution)/shard_map/pallas_call | solution.py:639
  212.7 2.8 multiply_convert_fusion
  218.7 143.8 %shard_map.383 = (f32[512,384]{1,0:T(8,128)}, f32[512,384]{1,0:T(8,128)}, f32[8,512]{1,0:T(8,128)}, f32[8,512]{1,0:T(8,128)}, bf16[512,384]{1,0:T(8,128)(2,1)}, ...) custom-call(bf16[1536,1536]{1,0:T(8,128)(2,1)} %get-tuple-element.15, ...), custom_call_target="tpu_custom_call" | custom-call | flops 10000000000 | bytes 21358592 | tf_op jit(solution)/shard_map/pallas_call | solution.py:639
  362.5 8.6 %shard_map.384.refs_2_ = bf16[512,2304]{1,0:T(8,128)(2,1)} custom-call(bf16[256,1536]{1,0:T(8,128)(2,1)} %copy-done.3, bf16[256,1536]{1,0:T(8,128)(2,1)} %collective-permute-done.refs_1_, bf16[1536,1536]{1,0:T(8,128)(2,1)} %get-tuple-element.174.refs_2_.refs_3_.refs_1_, bf16[1536,1536]{1,0:T(8,128)(2,1)} %get-tuple-element.175.refs_3_.refs_4_.refs_2_, ...), custom_call_target="tpu_custom_call" | custom-call | flops 3623878656 | bytes 18087936 | tf_op jit(solution)/shard_map/pallas_call | solution.py:39
  371.2 14.1 %shard_map.385 = (bf16[512,2304]{1,0:T(8,128)(2,1)}, bf16[512,2304]{1,0:T(8,128)(2,1)}, f32[256,1536]{1,0:T(8,128)}, bf16[256,1536]{1,0:T(8,128)(2,1)}) custom-call(bf16[256,1536]{1,0:T(8,128)(2,1)} %get-tuple-element.171.refs_0_, bf16[256,1536]{1,0:T(8,128)(2,1)} %get-tuple-element.172.refs_1_, bf16[512,2304]{1,0:T(8,128)(2,1)} %shard_map.384.refs_2_, ...), custom_call_target="tpu_custom_call" | custom-call | flops 7247757312 | bytes 25165824 | tf_op jit(solution)/shard_map/pallas_call | solution.py:39
  385.3 9.0 %shard_map.387.refs_2_ = bf16[512,2304]{1,0:T(8,128)(2,1)} custom-call(bf16[256,1536]{1,0:T(8,128)(2,1)} %copy-done.2, bf16[256,1536]{1,0:T(8,128)(2,1)} %collective-permute-done.2.refs_1_.refs_3_, bf16[1536,1536]{1,0:T(8,128)(2,1)} %get-tuple-element.174.refs_2_.refs_3_.refs_1_, bf16[1536,1536]{1,0:T(8,128)(2,1)} %get-tuple-element.175.refs_3_.refs_4_.refs_2_, ...), custom_call_target="tpu_custom_call" | custom-call | flops 3623878656 | bytes 18087936 | tf_op jit(solution)/shard_map/pallas_call | solution.py:39
  394.3 14.1 %shard_map.388 = (bf16[512,2304]{1,0:T(8,128)(2,1)}, bf16[512,2304]{1,0:T(8,128)(2,1)}, f32[256,1536]{1,0:T(8,128)}, bf16[256,1536]{1,0:T(8,128)(2,1)}) custom-call(bf16[256,1536]{1,0:T(8,128)(2,1)} %get-tuple-element.180.refs_0_.refs_2_, bf16[256,1536]{1,0:T(8,128)(2,1)} %get-tuple-element.181.refs_1_.refs_3_, bf16[512,2304]{1,0:T(8,128)(2,1)} %shard_map.387.refs_2_, ...), custom_call_target="tpu_custom_call" | custom-call | flops 7247757312 | bytes 25165824 | tf_op jit(solution)/shard_map/pallas_call | solution.py:39
  408.4 14.0 %shard_map.412 = bf16[1536,2304]{1,0:T(8,128)(2,1)} custom-call(bf16[256,1536]{1,0:T(8,128)(2,1)} %get-tuple-element.171.refs_0_, bf16[256,1536]{1,0:T(8,128)(2,1)} %get-tuple-element.172.refs_1_, bf16[256,1536]{1,0:T(8,128)(2,1)} %get-tuple-element.180.refs_0_.refs_2_, bf16[256,1536]{1,0:T(8,128)(2,1)} %get-tuple-element.181.refs_1_.refs_3_, ...), custom_call_target="tpu_custom_call" | custom-call | flops 7247757312 | bytes 14942208 | tf_op jit(solution)/shard_map/pallas_call | solution.py:39
  428.9 9.5 %shard_map.386 = (f32[256,1536]{1,0:T(8,128)}, bf16[256,1536]{1,0:T(8,128)(2,1)}) custom-call(bf16[512,2304]{1,0:T(8,128)(2,1)} %get-tuple-element.177.refs_0_.refs_4_, bf16[1536,1536]{1,0:T(8,128)(2,1)} %get-tuple-element.174.refs_2_.refs_3_.refs_1_, bf16[1536,1536]{1,0:T(8,128)(2,1)} %get-tuple-element.175.refs_3_.refs_4_.refs_2_, ...), custom_call_target="tpu_custom_call" | custom-call | flops 3623878656 | bytes 18874368 | tf_op jit(solution)/shard_map/pallas_call | solution.py:39
  439.0 9.6 %shard_map.389 = (f32[256,1536]{1,0:T(8,128)}, bf16[256,1536]{1,0:T(8,128)(2,1)}) custom-call(bf16[512,2304]{1,0:T(8,128)(2,1)} %get-tuple-element.182.refs_0_.refs_5_, bf16[1536,1536]{1,0:T(8,128)(2,1)} %get-tuple-element.174.refs_2_.refs_3_.refs_1_, bf16[1536,1536]{1,0:T(8,128)(2,1)} %get-tuple-element.175.refs_3_.refs_4_.refs_2_, ...), custom_call_target="tpu_custom_call" | custom-call | flops 3623878656 | bytes 18874368 | tf_op jit(solution)/shard_map/pallas_call | solution.py:39
  459.2 14.4 %shard_map.413 = bf16[1536,2304]{1,0:T(8,128)(2,1)} custom-call(bf16[256,1536]{1,0:T(8,128)(2,1)} %copy-done.3, bf16[256,1536]{1,0:T(8,128)(2,1)} %collective-permute-done.refs_1_, bf16[256,1536]{1,0:T(8,128)(2,1)} %copy-done.2, bf16[256,1536]{1,0:T(8,128)(2,1)} %collective-permute-done.2.refs_1_.refs_3_, ...), custom_call_target="tpu_custom_call" | custom-call | flops 7247757312 | bytes 14942208 | tf_op jit(solution)/shard_map/pallas_call | solution.py:39
  474.2 6.2 shard_map.390
  480.3 9.0 %collective-permute-done.13.b_ref = bf16[256,1536]{1,0:T(8,128)(2,1)} collective-permute-done((bf16[256,1536]{1,0:T(8,128)(2,1)S(1)}, bf16[256,1536]{1,0:T(8,128)(2,1)}, u32[]{:S(2)}, u32[]{:S(2)}) %collective-permute-start.13) | collective-permute-done | bytes 786464 | tf_op jit(solution)/shard_map/ppermute | solution.py:1195
  489.4 6.4 shard_map.395
  495.8 9.5 %collective-permute-done.4 = bf16[256,1536]{1,0:T(8,128)(2,1)} collective-permute-done((bf16[256,1536]{1,0:T(8,128)(2,1)}, bf16[256,1536]{1,0:T(8,128)(2,1)}, u32[]{:S(2)}, u32[]{:S(2)}) %collective-permute-start.4) | collective-permute-done | bytes 786464 | tf_op jit(solution)/shard_map/ppermute | solution.py:1195
  505.3 2.9 multiply_reduce_fusion
  508.9 8.9 %shard_map.391 = (f32[512,384]{1,0:T(8,128)}, f32[512,384]{1,0:T(8,128)}, f32[512,384]{1,0:T(8,128)}) custom-call(bf16[256,1536]{1,0:T(8,128)(2,1)} %get-tuple-element.188.refs_0_.refs_11_, bf16[256,1536]{1,0:T(8,128)(2,1)} %collective-permute-done.7.refs_1_.refs_12_, bf16[512,384]{1,0:T(8,128)(2,1)} %get-tuple-element.189.refs_2_, ...), custom_call_target="tpu_custom_call" | custom-call | flops 1610612736 | bytes 9848832 | tf_op jit(solution)/shard_map/pallas_call | solution.py:39
  517.8 2.6 shard_map.392
  520.3 9.4 %shard_map.396 = (f32[512,384]{1,0:T(8,128)}, f32[512,384]{1,0:T(8,128)}, f32[512,384]{1,0:T(8,128)}) custom-call(bf16[256,1536]{1,0:T(8,128)(2,1)} %get-tuple-element.201.refs_0_.refs_13_, bf16[256,1536]{1,0:T(8,128)(2,1)} %collective-permute-done.14.refs_1_.refs_14_, bf16[512,384]{1,0:T(8,128)(2,1)} %get-tuple-element.202.refs_2_, ...), custom_call_target="tpu_custom_call" | custom-call | flops 1610612736 | bytes 11421696 | tf_op jit(solution)/shard_map/pallas_call | solution.py:39
  529.7 2.5 shard_map.397
  532.8 2.6 shard_map.407
  540.5 4.8 shard_map.393
  549.8 4.8 shard_map.398
  562.5 7.2 shard_map.408
  570.3 9.1 %collective-permute-done.11.b_ref = bf16[256,1536]{1,0:T(8,128)(2,1)S(1)} collective-permute-done((bf16[256,1536]{1,0:T(8,128)(2,1)S(1)}, bf16[256,1536]{1,0:T(8,128)(2,1)S(1)}, u32[]{:S(2)}, u32[]{:S(2)}) %collective-permute-start.11) | collective-permute-done | bytes 786464 | tf_op jit(solution)/shard_map/ppermute | solution.py:1195
  580.3 6.4 shard_map.394
  586.7 10.6 %shard_map.411 = (bf16[4,192,1536]{2,1,0:T(8,128)(2,1)}, bf16[4,192,1536]{2,1,0:T(8,128)(2,1)}) custom-call(bf16[256,1536]{1,0:T(8,128)(2,1)} %get-tuple-element.161.refs_3_.refs_0_, bf16[256,1536]{1,0:T(8,128)(2,1)} %get-tuple-element.162.refs_4_.refs_1_, bf16[256,1536]{1,0:T(8,128)(2,1)} %get-tuple-element.163.refs_5_.refs_2_, ...), custom_call_target="tpu_custom_call" | custom-call | flops 4831838208 | bytes 14942208 | tf_op jit(solution)/shard_map/pallas_call | solution.py:618
  599.9 6.5 shard_map.399
  608.1 11.4 %shard_map.400 = (f32[512,384]{1,0:T(8,128)}, f32[1024,384]{1,0:T(8,128)}, f32[1024,384]{1,0:T(8,128)}) custom-call(bf16[256,1536]{1,0:T(8,128)(2,1)} %get-tuple-element.213.refs_0_, bf16[256,1536]{1,0:T(8,128)(2,1)} %collective-permute-done.19.refs_1_, bf16[512,384]{1,0:T(8,128)(2,1)} %get-tuple-element.214.refs_2_, ...), custom_call_target="tpu_custom_call" | custom-call | flops 2617245696 | bytes 12206080 | tf_op jit(solution)/shard_map/pallas_call | solution.py:39
  620.5 13.0 %shard_map.401 = (f32[512,384]{1,0:T(8,128)}, f32[1024,384]{1,0:T(8,128)}, f32[1024,384]{1,0:T(8,128)}) custom-call(bf16[256,1536]{1,0:T(8,128)(2,1)} %get-tuple-element.222.refs_0_.refs_2_, bf16[256,1536]{1,0:T(8,128)(2,1)} %copy-done.27, bf16[512,384]{1,0:T(8,128)(2,1)} %get-tuple-element.223.refs_2_, bf16[512,384]{1,0:T(8,128)(2,1)} %get-tuple-element.215.refs_3_, ...), custom_call_target="tpu_custom_call" | custom-call | flops 2617245696 | bytes 15351808 | tf_op jit(solution)/shard_map/pallas_call | solution.py:39
  633.5 2.6 fusion.48
  636.2 5.3 shard_map.402
  641.5 5.3 shard_map.403
  653.9 7.8 shard_map.404
  661.8 8.0 shard_map.405
  670.4 3.0 multiply_reduce_fusion.1
  673.4 5.3 shard_map.410
  679.4 3.6 broadcast_select_fusion
  685.1 2.9 fusion.4
  688.8 3.0 collective-permute-start.48
  692.4 8.9 %shard_map.409 = (bf16[4,192,1152]{2,1,0:T(8,128)(2,1)}, bf16[4,192,1152]{2,1,0:T(8,128)(2,1)}) custom-call(bf16[256,1536]{1,0:T(8,128)(2,1)} %get-tuple-element.270.refs_0_, bf16[256,1536]{1,0:T(8,128)(2,1)} %get-tuple-element.271.refs_1_, bf16[256,1536]{1,0:T(8,128)(2,1)} %get-tuple-element.272.refs_2_, bf16[256,1536]{1,0:T(8,128)(2,1)} %get-tuple-element.273.refs_3_, ...), custom_call_target="tpu_custom_call" | custom-call | flops 3623878656 | bytes 9043968 | tf_op jit(solution)/shard_map/pallas_call | solution.py:618
  703.9 6.2 shard_map.406
  715.5 25.0 %collective-permute-start.43 = (bf16[192,384]{1,0:T(8,128)(2,1)}, bf16[192,384]{1,0:T(8,128)(2,1)}, u32[]{:S(2)}, u32[]{:S(2)}) collective-permute-start(bf16[192,384]{1,0:T(8,128)(2,1)} %get-tuple-element.334), channel_id=1, source_target_pairs={{0,16},{4,20},{8,24},{12,28},{16,0},{20,4},{24,8},{28,12},{1,17},{... | collective-permute-start | bytes 442376 | tf_op jit(solution)/shard_map/ppermute | solution.py:1214
  740.5 16.3 %collective-permute-done.47 = bf16[192,1536]{1,0:T(8,128)(2,1)} collective-permute-done((bf16[192,1536]{1,0:T(8,128)(2,1)}, bf16[192,1536]{1,0:T(8,128)(2,1)}, u32[]{:S(2)}, u32[]{:S(2)}) %collective-permute-start.47) | collective-permute-done | bytes 589856 | tf_op jit(solution)/shard_map/ppermute | solution.py:1214
  765.0 3.8 collective-permute-start.36
  780.5 8.3 collective-permute-done.40
  788.8 24.5 %collective-permute-done.39 = bf16[192,1152]{1,0:T(8,128)(2,1)S(1)} collective-permute-done((bf16[192,1152]{1,0:T(8,128)(2,1)S(1)}, bf16[192,1152]{1,0:T(8,128)(2,1)S(1)}, u32[]{:S(2)}, u32[]{:S(2)}) %collective-permute-start.39) | collective-permute-done | bytes 442400 | tf_op jit(solution)/shard_map/ppermute | solution.py:1214
  815.5 2.5 slice_convert_fusion
  (357 shorter events, 104.7 us)
Async XLA Ops:
  7.2 808.3 %reduce-scatter.3.cloned.1.call-start = ((), (), s32[]{:S(2)}) async-start(), calls=%async_computation.2 | async-start | bytes 7962624 | tf_op jit(solution)/shard_map/reduce_scatter | solution.py:1340
  215.5 147.1 %collective-permute-start = (bf16[256,1536]{1,0:T(8,128)(2,1)S(1)}, bf16[256,1536]{1,0:T(8,128)(2,1)}, u32[]{:S(2)}, u32[]{:S(2)}) collective-permute-start(bf16[256,1536]{1,0:T(8,128)(2,1)S(1)} %get-tuple-element.322.refs_0_), channel_id=1, source_target_pairs={{0,1},{1,0},{2,3},{3,2},{4,5},{5,4},{6,7},{7,6},{8,9},{9,8},{10,11... | collective-permute-start | bytes 2359304 | tf_op jit(solution)/shard_map/ppermute | solution.py:1192
  215.5 169.8 %collective-permute-start.2 = (bf16[256,1536]{1,0:T(8,128)(2,1)S(1)}, bf16[256,1536]{1,0:T(8,128)(2,1)}, u32[]{:S(2)}, u32[]{:S(2)}) collective-permute-start(bf16[256,1536]{1,0:T(8,128)(2,1)S(1)} %get-tuple-element.310.refs_0_.refs_2_), channel_id=1, source_target_pairs={{0,1},{1,0},{2,3},{3,2},{4,5},{5,4},{6,7},{7,6},{8,9},{9,8},{10,11... | collective-permute-start | bytes 2359304 | tf_op jit(solution)/shard_map/ppermute | solution.py:1192
  422.5 395.5 %reduce-scatter.5.cloned.1.call-start = ((), (), s32[]{:S(2)}) async-start(), calls=%async_computation.3 | async-start | bytes 7962624 | tf_op jit(solution)/shard_map/reduce_scatter | solution.py:1338
  424.3 24.8 %collective-permute-start.5 = (bf16[256,1536]{1,0:T(8,128)(2,1)}, bf16[256,1536]{1,0:T(8,128)(2,1)S(1)}, u32[]{:S(2)}, u32[]{:S(2)}) collective-permute-start(bf16[256,1536]{1,0:T(8,128)(2,1)} %get-tuple-element.186), channel_id=1, source_target_pairs={{0,1},{1,0},{2,3},{3,2},{4,5},{5,4},{6,7},{7,6},{8,9},{9,8},{10,11... | collective-permute-start | bytes 2359304 | tf_op jit(solution)/shard_map/ppermute | solution.py:1192
  438.5 18.1 %collective-permute-start.1 = (bf16[256,1536]{1,0:T(8,128)(2,1)}, bf16[256,1536]{1,0:T(8,128)(2,1)S(1)}, u32[]{:S(2)}, u32[]{:S(2)}) collective-permute-start(bf16[256,1536]{1,0:T(8,128)(2,1)} %get-tuple-element.179), channel_id=1, source_target_pairs={{0,1},{1,0},{2,3},{3,2},{4,5},{5,4},{6,7},{7,6},{8,9},{9,8},{10,11... | collective-permute-start | bytes 2359304 | tf_op jit(solution)/shard_map/ppermute | solution.py:1192
  438.9 13.9 %collective-permute-start.12 = (bf16[256,1536]{1,0:T(8,128)(2,1)}, bf16[256,1536]{1,0:T(8,128)(2,1)S(1)}, u32[]{:S(2)}, u32[]{:S(2)}) collective-permute-start(bf16[256,1536]{1,0:T(8,128)(2,1)} %get-tuple-element.199), channel_id=1, source_target_pairs={{0,1},{1,0},{2,3},{3,2},{4,5},{5,4},{6,7},{7,6},{8,9},{9,8},{10,11... | collective-permute-start | bytes 2359304 | tf_op jit(solution)/shard_map/ppermute | solution.py:1192
  448.6 8.0 collective-permute-start.3
  451.9 21.6 %collective-permute-start.6 = (bf16[256,1536]{1,0:T(8,128)(2,1)S(1)}, bf16[256,1536]{1,0:T(8,128)(2,1)}, u32[]{:S(2)}, u32[]{:S(2)}) collective-permute-start(bf16[256,1536]{1,0:T(8,128)(2,1)S(1)} %add_convert_fusion.5.a_ref), channel_id=1, source_target_pairs={{0,2},{1,3},{2,0},{3,1},{4,6},{5,7},{6,4},{7,5},{8,10},{9,11},{10,... | collective-permute-start | bytes 2359304 | tf_op jit(solution)/shard_map/ppermute | solution.py:1195
  455.3 34.0 %collective-permute-start.13 = (bf16[256,1536]{1,0:T(8,128)(2,1)S(1)}, bf16[256,1536]{1,0:T(8,128)(2,1)}, u32[]{:S(2)}, u32[]{:S(2)}) collective-permute-start(bf16[256,1536]{1,0:T(8,128)(2,1)S(1)} %add_convert_fusion.3.a_ref), channel_id=1, source_target_pairs={{0,2},{1,3},{2,0},{3,1},{4,6},{5,7},{6,4},{7,5},{8,10},{9,11},{10,... | collective-permute-start | bytes 2359304 | tf_op jit(solution)/shard_map/ppermute | solution.py:1195
  458.3 47.0 %collective-permute-start.4 = (bf16[256,1536]{1,0:T(8,128)(2,1)}, bf16[256,1536]{1,0:T(8,128)(2,1)}, u32[]{:S(2)}, u32[]{:S(2)}) collective-permute-start(bf16[256,1536]{1,0:T(8,128)(2,1)} %get-tuple-element.305), channel_id=1, source_target_pairs={{0,2},{1,3},{2,0},{3,1},{4,6},{5,7},{6,4},{7,5},{8,10},{9,11},{10,... | collective-permute-start | bytes 2359304 | tf_op jit(solution)/shard_map/ppermute | solution.py:1195
  480.3 28.5 %collective-permute-start.7 = (bf16[256,1536]{1,0:T(8,128)(2,1)}, bf16[256,1536]{1,0:T(8,128)(2,1)}, u32[]{:S(2)}, u32[]{:S(2)}) collective-permute-start(bf16[256,1536]{1,0:T(8,128)(2,1)} %get-tuple-element.188.refs_0_.refs_11_), channel_id=1, source_target_pairs={{0,1},{1,0},{2,3},{3,2},{4,5},{5,4},{6,7},{7,6},{8,9},{9,8},{10,11... | collective-permute-start | bytes 2359304 | tf_op jit(solution)/shard_map/ppermute | solution.py:1192
  495.7 24.6 %collective-permute-start.14 = (bf16[256,1536]{1,0:T(8,128)(2,1)}, bf16[256,1536]{1,0:T(8,128)(2,1)}, u32[]{:S(2)}, u32[]{:S(2)}) collective-permute-start(bf16[256,1536]{1,0:T(8,128)(2,1)} %get-tuple-element.201.refs_0_.refs_13_), channel_id=1, source_target_pairs={{0,1},{1,0},{2,3},{3,2},{4,5},{5,4},{6,7},{7,6},{8,9},{9,8},{10,11... | collective-permute-start | bytes 2359304 | tf_op jit(solution)/shard_map/ppermute | solution.py:1192
  520.3 15.7 %collective-permute-start.8 = (f32[8,512]{1,0:T(8,128)}, f32[8,512]{1,0:T(8,128)S(1)}, u32[]{:S(2)}, u32[]{:S(2)}) collective-permute-start(f32[8,512]{1,0:T(8,128)} %get-tuple-element.194), channel_id=1, source_target_pairs={{0,1},{1,0},{2,3},{3,2},{4,5},{5,4},{6,7},{7,6},{8,9},{9,8},{10,11... | collective-permute-start | bytes 49160 | tf_op jit(solution)/shard_map/ppermute | solution.py:1192
  532.3 5.3 collective-permute-start.15
  536.1 10.8 %collective-permute-start.26 = (f32[2,8,256]{2,1,0:T(8,128)S(1)}, f32[2,8,256]{2,1,0:T(8,128)S(1)}, u32[]{:S(2)}, u32[]{:S(2)}) collective-permute-start(f32[2,8,256]{2,1,0:T(8,128)S(1)} %pad_maximum_fusion.6), channel_id=1, source_target_pairs={{0,1},{1,0},{2,3},{3,2},{4,5},{5,4},{6,7},{7,6},{8,9},{9,8},{10,11... | collective-permute-start | bytes 49160 | tf_op jit(solution)/shard_map/ppermute | solution.py:1192
  536.1 3.8 collective-permute-start.9
  545.3 13.5 %collective-permute-start.10 = (bf16[256,1536]{1,0:T(8,128)(2,1)}, bf16[256,1536]{1,0:T(8,128)(2,1)S(1)}, u32[]{:S(2)}, u32[]{:S(2)}) collective-permute-start(bf16[256,1536]{1,0:T(8,128)(2,1)} %get-tuple-element.196), channel_id=1, source_target_pairs={{0,1},{1,0},{2,3},{3,2},{4,5},{5,4},{6,7},{7,6},{8,9},{9,8},{10,11... | collective-permute-start | bytes 2359304 | tf_op jit(solution)/shard_map/ppermute | solution.py:1192
  554.6 5.6 collective-permute-start.17
  554.7 4.1 collective-permute-start.27
  559.0 20.4 %collective-permute-start.11 = (bf16[256,1536]{1,0:T(8,128)(2,1)S(1)}, bf16[256,1536]{1,0:T(8,128)(2,1)S(1)}, u32[]{:S(2)}, u32[]{:S(2)}) collective-permute-start(bf16[256,1536]{1,0:T(8,128)(2,1)S(1)} %add_convert_fusion.4.a_ref), channel_id=1, source_target_pairs={{0,2},{1,3},{2,0},{3,1},{4,6},{5,7},{6,4},{7,5},{8,10},{9,11},{10,... | collective-permute-start | bytes 2359304 | tf_op jit(solution)/shard_map/ppermute | solution.py:1195
  560.7 38.3 %collective-permute-start.18 = (bf16[256,1536]{1,0:T(8,128)(2,1)S(1)}, bf16[256,1536]{1,0:T(8,128)(2,1)S(1)}, u32[]{:S(2)}, u32[]{:S(2)}) collective-permute-start(bf16[256,1536]{1,0:T(8,128)(2,1)S(1)} %add_convert_fusion.2.a_ref), channel_id=1, source_target_pairs={{0,2},{1,3},{2,0},{3,1},{4,6},{5,7},{6,4},{7,5},{8,10},{9,11},{10,... | collective-permute-start | bytes 2359304 | tf_op jit(solution)/shard_map/ppermute | solution.py:1195
  569.7 36.8 %collective-permute-start.28 = (bf16[128,1536]{1,0:T(8,128)(2,1)}, bf16[128,1536]{1,0:T(8,128)(2,1)S(1)}, u32[]{:S(2)}, u32[]{:S(2)}) collective-permute-start(bf16[128,1536]{1,0:T(8,128)(2,1)} %get-tuple-element.253), channel_id=1, source_target_pairs={{0,1},{1,0},{2,3},{3,2},{4,5},{5,4},{6,7},{7,6},{8,9},{9,8},{10,11... | collective-permute-start | bytes 1179656 | tf_op jit(solution)/shard_map/ppermute | solution.py:1192
  569.8 36.8 %collective-permute-start.29 = (bf16[128,1536]{1,0:T(8,128)(2,1)}, bf16[128,1536]{1,0:T(8,128)(2,1)S(1)}, u32[]{:S(2)}, u32[]{:S(2)}) collective-permute-start(bf16[128,1536]{1,0:T(8,128)(2,1)} %get-tuple-element.255), channel_id=1, source_target_pairs={{0,1},{1,0},{2,3},{3,2},{4,5},{5,4},{6,7},{7,6},{8,9},{9,8},{10,11... | collective-permute-start | bytes 1179656 | tf_op jit(solution)/shard_map/ppermute | solution.py:1192
  586.7 21.4 %collective-permute-start.19 = (bf16[256,1536]{1,0:T(8,128)(2,1)}, bf16[256,1536]{1,0:T(8,128)(2,1)}, u32[]{:S(2)}, u32[]{:S(2)}) collective-permute-start(bf16[256,1536]{1,0:T(8,128)(2,1)} %get-tuple-element.213.refs_0_), channel_id=1, source_target_pairs={{0,1},{1,0},{2,3},{3,2},{4,5},{5,4},{6,7},{7,6},{8,9},{9,8},{10,11... | collective-permute-start | bytes 2359304 | tf_op jit(solution)/shard_map/ppermute | solution.py:1192
  597.3 87.8 %collective-permute-start.45 = (bf16[4,192,1536]{2,1,0:T(8,128)(2,1)}, bf16[4,192,1536]{2,1,0:T(8,128)(2,1)}, u32[]{:S(2)}, u32[]{:S(2)}) collective-permute-start(bf16[4,192,1536]{2,1,0:T(8,128)(2,1)} %get-tuple-element.292), channel_id=1, source_target_pairs={{0,4},{4,0},{8,12},{12,8},{16,20},{20,16},{24,28},{28,24},{1,5},{5... | collective-permute-start | bytes 7077896 | tf_op jit(solution)/shard_map/ppermute | solution.py:1206
  606.3 13.3 %collective-permute-start.20 = (bf16[256,1536]{1,0:T(8,128)(2,1)}, bf16[256,1536]{1,0:T(8,128)(2,1)S(1)}, u32[]{:S(2)}, u32[]{:S(2)}) collective-permute-start(bf16[256,1536]{1,0:T(8,128)(2,1)} %get-tuple-element.222.refs_0_.refs_2_), channel_id=1, source_target_pairs={{0,1},{1,0},{2,3},{3,2},{4,5},{5,4},{6,7},{7,6},{8,9},{9,8},{10,11... | collective-permute-start | bytes 2359304 | tf_op jit(solution)/shard_map/ppermute | solution.py:1192
  606.8 40.9 %collective-permute-start.30 = (bf16[128,1536]{1,0:T(8,128)(2,1)S(1)}, bf16[128,1536]{1,0:T(8,128)(2,1)S(1)}, u32[]{:S(2)}, u32[]{:S(2)}) collective-permute-start(bf16[128,1536]{1,0:T(8,128)(2,1)S(1)} %broadcast_select_fusion.7), channel_id=1, source_target_pairs={{0,2},{1,3},{2,0},{3,1},{4,6},{5,7},{6,4},{7,5},{8,10},{9,11},{10,... | collective-permute-start | bytes 1179656 | tf_op jit(solution)/shard_map/ppermute | solution.py:1195
  648.9 4.3 collective-permute-start.22
  661.7 17.7 %collective-permute-start.23 = (bf16[256,1536]{1,0:T(8,128)(2,1)}, bf16[256,1536]{1,0:T(8,128)(2,1)}, u32[]{:S(2)}, u32[]{:S(2)}) collective-permute-start(bf16[256,1536]{1,0:T(8,128)(2,1)} %get-tuple-element.241), channel_id=1, source_target_pairs={{0,1},{1,0},{2,3},{3,2},{4,5},{5,4},{6,7},{7,6},{8,9},{9,8},{10,11... | collective-permute-start | bytes 2359304 | tf_op jit(solution)/shard_map/ppermute | solution.py:1192
  669.8 9.6 %collective-permute-start.24 = (bf16[256,1536]{1,0:T(8,128)(2,1)}, bf16[256,1536]{1,0:T(8,128)(2,1)}, u32[]{:S(2)}, u32[]{:S(2)}) collective-permute-start(bf16[256,1536]{1,0:T(8,128)(2,1)} %get-tuple-element.245), channel_id=1, source_target_pairs={{0,1},{1,0},{2,3},{3,2},{4,5},{5,4},{6,7},{7,6},{8,9},{9,8},{10,11... | collective-permute-start | bytes 2359304 | tf_op jit(solution)/shard_map/ppermute | solution.py:1192
  678.7 32.4 %collective-permute-start.41 = (bf16[4,192,384]{2,1,0:T(8,128)(2,1)}, bf16[4,192,384]{2,1,0:T(8,128)(2,1)}, u32[]{:S(2)}, u32[]{:S(2)}) collective-permute-start(bf16[4,192,384]{2,1,0:T(8,128)(2,1)} %get-tuple-element.281), channel_id=1, source_target_pairs={{0,4},{4,0},{8,12},{12,8},{16,20},{20,16},{24,28},{28,24},{1,5},{5... | collective-permute-start | bytes 1769480 | tf_op jit(solution)/shard_map/ppermute | solution.py:1206
  683.0 19.6 %collective-permute-start.25 = (bf16[256,1536]{1,0:T(8,128)(2,1)}, bf16[256,1536]{1,0:T(8,128)(2,1)S(1)}, u32[]{:S(2)}, u32[]{:S(2)}) collective-permute-start(bf16[256,1536]{1,0:T(8,128)(2,1)} %get-tuple-element.315), channel_id=1, source_target_pairs={{0,2},{1,3},{2,0},{3,1},{4,6},{5,7},{6,4},{7,5},{8,10},{9,11},{10,... | collective-permute-start | bytes 2359304 | tf_op jit(solution)/shard_map/ppermute | solution.py:1195
  688.8 26.7 %collective-permute-start.48 = (bf16[192,1536]{1,0:T(8,128)(2,1)}, bf16[192,1536]{1,0:T(8,128)(2,1)}, u32[]{:S(2)}, u32[]{:S(2)}) collective-permute-start(bf16[192,1536]{1,0:T(8,128)(2,1)} %get-tuple-element.313), channel_id=1, source_target_pairs={{0,24},{4,28},{8,0},{12,4},{16,8},{20,12},{24,16},{28,20},{1,25},{... | collective-permute-start | bytes 1769480 | tf_op jit(solution)/shard_map/ppermute | solution.py:1214
  691.8 64.9 %collective-permute-start.47 = (bf16[192,1536]{1,0:T(8,128)(2,1)}, bf16[192,1536]{1,0:T(8,128)(2,1)}, u32[]{:S(2)}, u32[]{:S(2)}) collective-permute-start(bf16[192,1536]{1,0:T(8,128)(2,1)} %get-tuple-element.314), channel_id=1, source_target_pairs={{0,16},{4,20},{8,24},{12,28},{16,0},{20,4},{24,8},{28,12},{1,17},{... | collective-permute-start | bytes 1769480 | tf_op jit(solution)/shard_map/ppermute | solution.py:1214
  691.8 64.9 %collective-permute-start.46 = (bf16[192,1536]{1,0:T(8,128)(2,1)}, bf16[192,1536]{1,0:T(8,128)(2,1)}, u32[]{:S(2)}, u32[]{:S(2)}) collective-permute-start(bf16[192,1536]{1,0:T(8,128)(2,1)} %get-tuple-element.312), channel_id=1, source_target_pairs={{0,8},{4,12},{8,16},{12,20},{16,24},{20,28},{24,0},{28,4},{1,9},{5... | collective-permute-start | bytes 1769480 | tf_op jit(solution)/shard_map/ppermute | solution.py:1214
  702.5 72.0 %collective-permute-start.37 = (bf16[4,192,1152]{2,1,0:T(8,128)(2,1)}, bf16[4,192,1152]{2,1,0:T(8,128)(2,1)}, u32[]{:S(2)}, u32[]{:S(2)}) collective-permute-start(bf16[4,192,1152]{2,1,0:T(8,128)(2,1)} %get-tuple-element.277), channel_id=1, source_target_pairs={{0,4},{4,0},{8,12},{12,8},{16,20},{20,16},{24,28},{28,24},{1,5},{5... | collective-permute-start | bytes 5308424 | tf_op jit(solution)/shard_map/ppermute | solution.py:1206
  713.2 55.6 %collective-permute-start.44 = (bf16[192,384]{1,0:T(8,128)(2,1)}, bf16[192,384]{1,0:T(8,128)(2,1)}, u32[]{:S(2)}, u32[]{:S(2)}) collective-permute-start(bf16[192,384]{1,0:T(8,128)(2,1)} %get-tuple-element.333), channel_id=1, source_target_pairs={{0,24},{4,28},{8,0},{12,4},{16,8},{20,12},{24,16},{28,20},{1,25},{... | collective-permute-start | bytes 442376 | tf_op jit(solution)/shard_map/ppermute | solution.py:1214
  715.5 53.3 %collective-permute-start.43 = (bf16[192,384]{1,0:T(8,128)(2,1)}, bf16[192,384]{1,0:T(8,128)(2,1)}, u32[]{:S(2)}, u32[]{:S(2)}) collective-permute-start(bf16[192,384]{1,0:T(8,128)(2,1)} %get-tuple-element.334), channel_id=1, source_target_pairs={{0,16},{4,20},{8,24},{12,28},{16,0},{20,4},{24,8},{28,12},{1,17},{... | collective-permute-start | bytes 442376 | tf_op jit(solution)/shard_map/ppermute | solution.py:1214
  756.7 12.7 %collective-permute-start.42 = (bf16[192,384]{1,0:T(8,128)(2,1)}, bf16[192,384]{1,0:T(8,128)(2,1)}, u32[]{:S(2)}, u32[]{:S(2)}) collective-permute-start(bf16[192,384]{1,0:T(8,128)(2,1)} %get-tuple-element.332), channel_id=1, source_target_pairs={{0,8},{4,12},{8,16},{12,20},{16,24},{20,28},{24,0},{28,4},{1,9},{5... | collective-permute-start | bytes 442376 | tf_op jit(solution)/shard_map/ppermute | solution.py:1214
  756.7 4.2 collective-permute-start.32
  761.2 3.8 collective-permute-start.33
  765.0 8.1 collective-permute-start.36
  768.8 4.5 collective-permute-start.35
  768.8 5.6 collective-permute-start.34
  776.2 12.6 %collective-permute-start.40 = (bf16[192,1152]{1,0:T(8,128)(2,1)S(1)}, bf16[192,1152]{1,0:T(8,128)(2,1)S(1)}, u32[]{:S(2)}, u32[]{:S(2)}) collective-permute-start(bf16[192,1152]{1,0:T(8,128)(2,1)S(1)} %get-tuple-element.318), channel_id=1, source_target_pairs={{0,24},{4,28},{8,0},{12,4},{16,8},{20,12},{24,16},{28,20},{1,25},{... | collective-permute-start | bytes 1327112 | tf_op jit(solution)/shard_map/ppermute | solution.py:1214
  778.2 35.1 %collective-permute-start.39 = (bf16[192,1152]{1,0:T(8,128)(2,1)S(1)}, bf16[192,1152]{1,0:T(8,128)(2,1)S(1)}, u32[]{:S(2)}, u32[]{:S(2)}) collective-permute-start(bf16[192,1152]{1,0:T(8,128)(2,1)S(1)} %get-tuple-element.319), channel_id=1, source_target_pairs={{0,16},{4,20},{8,24},{12,28},{16,0},{20,4},{24,8},{28,12},{1,17},{... | collective-permute-start | bytes 1327112 | tf_op jit(solution)/shard_map/ppermute | solution.py:1214
  779.2 34.1 %collective-permute-start.38 = (bf16[192,1152]{1,0:T(8,128)(2,1)S(1)}, bf16[192,1152]{1,0:T(8,128)(2,1)S(1)}, u32[]{:S(2)}, u32[]{:S(2)}) collective-permute-start(bf16[192,1152]{1,0:T(8,128)(2,1)S(1)} %get-tuple-element.317), channel_id=1, source_target_pairs={{0,8},{4,12},{8,16},{12,20},{16,24},{20,28},{24,0},{28,4},{1,9},{5... | collective-permute-start | bytes 1327112 | tf_op jit(solution)/shard_map/ppermute | solution.py:1214
  (64 other events, 716.8 us)
Sparse Core Ops, SparseCore 0:
  422.6 127.5 reduce-scatter.2
  554.3 156.3 reduce-scatter.4

commit v3 on v2

--- a/solution.py
+++ b/solution.py
@@ -643,7 +643,7 @@
         out_specs=(vmem,) * len(outs) + (hbm,) * len(far_outs),
         scratch_shapes=list(scratch),
         compiler_params=pltpu.CompilerParams(
-            vmem_limit_bytes=60 * 2**20, collective_id=cid, has_side_effects=True
+            vmem_limit_bytes=61 * 2**20, collective_id=cid, has_side_effects=True
         ),
         cost_estimate=pl.CostEstimate(flops=int(flops), bytes_accessed=moved, transcendentals=0),
     )(*blocks, *far)
@@ -679,60 +679,83 @@
         d = lax.axis_index("dp")
         self.z, self.y = d // 2, lax.rem(d, 2)
         self.ref, self.sems, self.n, self.r = ref, sems, n, ref.shape[0] // (2 * n)
-
-    def block(self, o, y):
-        return self.ref.at[pl.ds(pl.multiple_of((2 * o + y) * self.r, 16), self.r)]
-
-    def copy(self, o, kind, index, z, y, own=True):
-        block = self.block(o, self.y if own else 1 - self.y)
+        self.cols = (0, ref.shape[1])
+        self.near = (0, ref.shape[1] - 256)
+        self.last = (ref.shape[1] - 256, ref.shape[1])
+
+    def copy(self, o, kind, index, z, y, own, cols):
+        start = (2 * o + (self.y if own else 1 - self.y)) * self.r
+        block = self.ref.at[pl.ds(pl.multiple_of(start, 16), self.r), pl.ds(cols[0], cols[1] - cols[0])]
         sems = self.sems
-        return remote(
-            block, block, sems.at[2 * kind, index], sems.at[2 * kind + 1, index], dp=2 * z + y
-        )
-
-    def up(self, s):
-        return self.copy(self.z - s, 0, s, self.z + 1, self.y)
-
-    def down(self, s):
-        return self.copy(self.z + s, 1, s, self.z - 1, self.y)
-
-    def over(self, o):
-        return self.copy(o, 2, o, self.z, 1 - self.y)
+        return remote(block, block, sems.at[2 * kind, index], sems.at[2 * kind + 1, index], dp=2 * z + y)
+
+    def along(self, way, s, own=True):
+        kind = (0 if way > 0 else 1) + (0 if own else 3)
+        cols = self.cols if own else self.last
+        return self.copy(self.z - way * s, kind, s, self.z + way, self.y, own, cols)
+
+    def came(self, way, s, own=True):
+        kind = (0 if way > 0 else 1) + (0 if own else 3)
+        cols = self.cols if own else self.last
+        return self.copy(self.z - way * (s + 1), kind, s, self.z - way, self.y, own, cols)
+
+    def over(self, o, cols):
+        return self.copy(o, 2, o, self.z, 1 - self.y, True, cols)
+
+    def inside(self, o):
+        return (o >= 0) & (o <= self.n - 1)
 
     def start(self, own, sem):
-        copy = pltpu.make_async_copy(own, self.block(self.z, self.y), sem)
+        start = (2 * self.z + self.y) * self.r
+        copy = pltpu.make_async_copy(own, self.ref.at[pl.ds(pl.multiple_of(start, 16), self.r)], sem)
         copy.start()
         copy.wait()
-        pl.when(self.z < self.n - 1)(lambda: self.up(0).start())
-        pl.when(self.z > 0)(lambda: self.down(0).start())
-        self.over(self.z).start()
+        for way in (1, -1):
+            pl.when(self.inside(self.z + way))(lambda way=way: self.along(way, 0).start())
+        self.over(self.z, self.cols).start()
 
     def step(self, s):
-        z, n = self.z, self.n
-
-        @pl.when(z - 1 - s >= 0)
-        def _():
-            self.copy(z - 1 - s, 0, s, z - 1, self.y).wait_recv()
-            pl.when(z < n - 1)(lambda: self.up(s + 1).start())
-            self.over(z - 1 - s).start()
-
-        @pl.when(z + 1 + s <= n - 1)
-        def _():
-            self.copy(z + 1 + s, 1, s, z + 1, self.y).wait_recv()
-            pl.when(z > 0)(lambda: self.down(s + 1).start())
-            self.over(z + 1 + s).start()
+        for way in (1, -1):
+
+            @pl.when(self.inside(self.z - way * (s + 1)))
+            def _(way=way):
+                self.came(way, s).wait_recv()
+                pl.when(self.inside(self.z + way))(lambda: self.along(way, s + 1).start())
+                self.over(self.z - way * (s + 1), self.near).start()
+
+        self.rest(s)
+
+    def rest(self, s):
+        if s == 0:
+            self.copy(self.z, 2, self.z, self.z, 1 - self.y, False, self.cols).wait_recv()
+        for way in (1, -1):
+            if s == 0:
+                pl.when(self.inside(self.z + way))(lambda way=way: self.along(way, 0, False).start())
+            else:
+
+                @pl.when(self.inside(self.z - way * s))
+                def _(way=way):
+                    self.came(way, s - 1, False).wait_recv()
+                    if s < self.n - 1:
+                        pl.when(self.inside(self.z + way))(lambda: self.along(way, s, False).start())
 
     def finish(self):
+        self.rest(self.n - 1)
         for o in range(self.n):
-            self.copy(o, 2, o, self.z, 1 - self.y, own=False).wait_recv()
+            pl.when(self.z != o)(
+                lambda o=o: self.copy(o, 2, o, self.z, 1 - self.y, False, self.near).wait_recv()
+            )
 
     def drain(self):
-        z, n = self.z, self.n
-        for s in range(n - 1):
-            pl.when((z - s >= 0) & (z < n - 1))(lambda: self.up(s).wait_send())
-            pl.when((z + s <= n - 1) & (z > 0))(lambda: self.down(s).wait_send())
-        for o in range(n):
-            self.over(o).wait_send()
+        for own in (True, False):
+            for s in range(self.n - 1):
+                for way in (1, -1):
+                    pl.when(self.inside(self.z - way * s) & self.inside(self.z + way))(
+                        lambda s=s, way=way, own=own: self.along(way, s, own).wait_send()
+                    )
+        for o in range(self.n):
+            pl.when(self.z == o)(lambda: self.over(self.z, self.cols).wait_send())
+            pl.when(self.z != o)(lambda o=o: self.over(o, self.near).wait_send())
 
 
 class Swap:
@@ -870,8 +893,9 @@
         y0=rows, y1=rows, y2=rows, y3=rows,
         ck_raw=shape((4 * texts, wide), F32), cv=shape((4 * texts, wide), BF),
         ck_stat=shape((8, 4 * texts), F32), ck=shape((4 * texts, wide), BF),
-    )
-    far_outs = dict(f0=shape((D, own_first.shape[1]), BF), g_got=rows)
+        f0=shape((D, own_first.shape[1]), BF),
+    )
+    far_outs = dict(g_got=rows)
     blocks = [hidden, context, time_rows, tables[0], tables[1], small]
     far = [own_self, own_cross, own_first, cotangent]
     names = [*outs, *far_outs]
@@ -1034,7 +1058,7 @@
         pltpu.VMEM((2, quarter, D), BF),
         pltpu.VMEM((2, quarter, D), F32),
         pltpu.VMEM((4, 3, 8, half), F32),
-        pltpu.SemaphoreType.DMA((3, 6, n)),
+        pltpu.SemaphoreType.DMA((3, 10, n)),
         pltpu.SemaphoreType.DMA((2, 8)),
         pltpu.SemaphoreType.DMA((2, 8)),
         pltpu.SemaphoreType.DMA((2, 12)),
@@ -1047,7 +1071,7 @@
     return dict(zip(names, got))
 
 
-def cross_forward(state, bias, own_second, own_third, n_dp, heads):
+def cross_forward(state, cotangent, bias, own_second, own_third, n_dp, heads):
     quarter = state["y0"].shape[0]
     half, wide = 2 * quarter, heads * HEAD
     n = n_dp // 2
@@ -1059,20 +1083,22 @@
         cattn0=shape((half, wide), BF), cattn1=shape((half, wide), BF),
         clse0=shape((8, half), F32), clse1=shape((8, half), F32),
         after_c0=shape((quarter, D), F32), after_c1=shape((quarter, D), F32),
-        z0=rows, z1=rows, z2=rows, z3=rows,
-    )
-    far_outs = dict(f1=shape((D, own_second.shape[1]), BF), f2=shape((D, own_third.shape[1]), BF))
-    given = ("w_cross", "after0", "after1", "y0", "y1", "y2", "y3", "ck", "cv", "shifts", "gains")
-    blocks = [state[name] for name in given] + [bias]
-    far = [own_second, own_third]
+        z0=rows, z1=rows, z2=rows, z3=rows, d0=rows, d1=rows, d2=rows, d3=rows,
+        dact0=shape((2 * half, HC), BF), dact1=shape((2 * half, HC), BF),
+        f1=shape((D, own_second.shape[1]), BF), f2=shape((D, own_third.shape[1]), BF),
+    )
+    far_outs = {}
+    given = ("w_cross", "after0", "after1", "y0", "y1", "y2", "y3", "ck", "cv", "shifts", "gains", "g_got")
+    blocks = [state[name] for name in given] + [bias, cotangent]
+    far = [own_second, own_third, state["f0"]]
     names = [*outs, *far_outs]
 
     def kernel(*refs):
         i = dict(zip(given, refs))
-        bias_ref, own1, own2 = refs[len(given) : len(given) + 3]
-        refs = refs[len(given) + 3 :]
+        bias_ref, cot, own1, own2, f0 = refs[len(given) : len(given) + 5]
+        refs = refs[len(given) + 5 :]
         o = dict(zip(names, refs))
-        theirs, landed, mine, chips, fars, stats_in, ring, near, cross_x, near_sums, local = refs[len(names) :]
+        theirs, landed, mine, chips, fars, stats_in, w_down, ring, near, cross_x, near_sums, local = refs[len(names) :]
         t, core, across, diagonal = tensor_peers()
         cores, xs = Swap(near), Swap(cross_x)
         sums = Sums(stats_in, near_sums, (core, across, diagonal))
@@ -1080,6 +1106,18 @@
         g1 = Gather(o["f1"], ring.at[0], n)
         g2 = Gather(o["f2"], ring.at[1], n)
         g1.start(own1, local.at[0])
+        first_down = pltpu.make_async_copy(f0.at[:, pl.ds(HC, HC)], w_down, local.at[1])
+        first_down.start()
+        d_slots = [o["d0"], o["d1"], o["d2"], o["d3"]]
+        s_five = i["shifts"][5:6]
+        first = t < 2
+        sent_d = []
+
+        def act_grad(part):
+            down = o["f1"][:, HC:] if part else w_down[...]
+            for p, slot in enumerate(d_slots):
+                o[f"dact{part}"][p * quarter : (p + 1) * quarter] = dot_nn(slot[...], down).astype(BF)
+
         w = i["w_cross"]
         slots = [i["y0"], i["y1"], i["y2"], i["y3"]]
         raw, stat = [o["cq_raw0"], o["cq_raw1"]], [o["cq_stat0"], o["cq_stat1"]]
@@ -1090,6 +1128,14 @@
         for j in range(2):
             project_body(slots[2 * j : 2 * j + 2], w, 0, raw[j], None, stat[j], 1, 0, wide)
             shared.append(sums.start(stat[j]))
+
+            def scaled(rows, j=j):
+                own, other = cot[rows].astype(F32), i["g_got"][rows].astype(F32)
+                g = jnp.where(first, own, other) if j == 0 else jnp.where(first, other, own)
+                d_slots[2 * j][rows] = (g * s_five).astype(BF)
+
+            over_rows(quarter, scaled)
+            sent_d.append(cores.start(d_slots[2 * j], d_slots[2 * j + 1], core))
         sent = []
         for j in range(2):
             shared[j]()
@@ -1106,8 +1152,13 @@
             sent[j].wait_recv()
             join_body(mine.at[j], landed.at[j], chips.at[j])
             crossed.append(xs.start(chips.at[j], fars.at[j], across))
-        for s in range(1, n - 1):
+        for s in range(1, n - 2):
             g1.step(s)
+        for copy in sent_d:
+            copy.wait_recv()
+        first_down.wait()
+        act_grad(0)
+        g1.step(n - 2)
         g2.start(own2, local.at[0])
         base = [i["after0"], i["after1"]]
         after = [o["after_c0"], o["after_c1"]]
@@ -1120,12 +1171,16 @@
                 lambda rows, j=j: base[j][rows], chips.at[j], fars.at[j], 1.0, m_row, t_row, after[j], z_slots[2 * j]
             )
             passed.append(cores.start(z_slots[2 * j], z_slots[2 * j + 1], core))
-        for s in range(n - 1):
+        g2.step(0)
+        g1.finish()
+        if n > 2:
+            g2.step(1)
+        act_grad(1)
+        for s in range(2, n - 1):
             g2.step(s)
         for copy in passed:
             copy.wait_recv()
-        for g in (g1, g2):
-            g.finish()
+        g2.finish()
         for g in (g1, g2):
             g.drain()
         cores.settle()
@@ -1138,14 +1193,708 @@
         pltpu.VMEM((2, quarter, D), BF),
         pltpu.VMEM((2, quarter, D), BF),
         pltpu.VMEM((2, 3, 8, half), F32),
-        pltpu.SemaphoreType.DMA((2, 6, n)),
+        pltpu.VMEM((D, HC), BF),
+        pltpu.SemaphoreType.DMA((2, 10, n)),
         pltpu.SemaphoreType.DMA((2, 8)),
         pltpu.SemaphoreType.DMA((2, 8)),
         pltpu.SemaphoreType.DMA((2, 6)),
-        pltpu.SemaphoreType.DMA((1,)),
+        pltpu.SemaphoreType.DMA((3,)),
     ]
     got = run_remote(
         kernel, list(outs.values()), list(far_outs.values()), blocks, far, scratch, 2, 1e10
+    )
+    return dict(zip(names, got))
+
+
+def back_body(g, v, chip, far, m, s, out_ref, rows_ref, sum_ref):
+    sum_ref[...] = jnp.zeros_like(sum_ref)
+
+    def body(i):
+        da = chip[i].astype(F32) + far[i].astype(F32)
+        n, r = norm_of(v[i].astype(F32))
+        dn = da * m
+        mean = jnp.mean(dn, axis=-1, keepdims=True)
+        along = jnp.mean(dn * n, axis=-1, keepdims=True)
+        out = g(i) + r * (dn - mean - n * along)
+        out_ref[i] = out
+        rows_ref[i] = (out * s).astype(BF)
+        dan = da * n
+        for k in range(STEP // 8):
+            sum_ref[:8] += da[k * 8 : k * 8 + 8]
+            sum_ref[8:] += dan[k * 8 : k * 8 + 8]
+
+    over_rows(v.shape[0], body)
+
+
+def feed_forward(state, cotangent, n_dp):
+    quarter = state["z0"].shape[0]
+    half = 2 * quarter
+    rows = shape((quarter, D), BF)
+    whole = shape((quarter, D), F32)
+    outs = dict(
+        gc0=whole, gc1=whole, e0=rows, e1=rows, e2=rows, e3=rows,
+        sf0=shape((16, D), F32), sf1=shape((16, D), F32), branch=whole,
+    )
+    far_outs = {f"t{j}": shape((D, 2 * HC), BF) for j in range(3)}
+    given = ("z0", "z1", "z2", "z3", "d0", "d1", "d2", "d3", "after_c0", "after_c1", "shifts", "g_got")
+    blocks = [state[name] for name in given] + [cotangent]
+    far = [state["f0"], state["f1"], state["f2"], state["dact0"], state["dact1"]]
+    names = [*outs, *far_outs]
+
+    def kernel(*refs):
+        i = dict(zip(given, refs))
+        cot, f, dact, refs = refs[len(given)], refs[len(given) + 1 :][:3], refs[len(given) + 4 :][:2], refs[len(given) + 6 :]
+        o = dict(zip(names, refs))
+        (
+            w, act, dpre, theirs, landed, mine, chips, fars, turned, near, cross_x, local,
+        ) = refs[len(names) :]
+        t, core, across, diagonal = tensor_peers()
+        first = t < 2
+        cores, xs = Swap(near), Swap(cross_x)
+        loads = [pltpu.make_async_copy(f[j], w.at[j], local.at[j]) for j in range(3)]
+        loads += [pltpu.make_async_copy(dact[j], dpre.at[j], local.at[3 + j]) for j in range(2)]
+        for copy in loads:
+            copy.start()
+        greet(n_dp)
+        z = [i["z0"], i["z1"], i["z2"], i["z3"]]
+        ds = [i["d0"], i["d1"], i["d2"], i["d3"]]
+        loads[2].wait()
+        for p in range(4):
+            dpre[2, p * quarter : (p + 1) * quarter] = dot_nn(ds[p][...], w[2, :, HC:]).astype(BF)
+
+        def pre_part(h, j):
+            for p in (2 * h, 2 * h + 1):
+                own = slice(p * quarter, (p + 1) * quarter)
+                u = dot_nn(z[p][...], w[j, :, :HC])
+                sq = u * u
+                th = jnp.tanh(u * (GELU + GELU * CUBE * sq))
+                near_half = 0.5 + 0.5 * th
+                act[j, own] = (u * near_half).astype(BF)
+                slope = near_half + u * near_half * (1.0 - th) * (GELU + 3 * GELU * CUBE * sq)
+                dpre[j, own] = (dpre[j, own].astype(F32) * slope).astype(BF)
+
+        def contracted(a, p, side):
+            own = slice(p * quarter, (p + 1) * quarter)
+            total = None
+            for j in range(3):
+                term = dot_nt(a[j, own], w[j, :, side * HC : (side + 1) * HC])
+                total = term if total is None else total + term
+            return total
+
+        def back_half(h):
+            theirs[h] = contracted(dpre, 2 * h + 1, 0).astype(BF)
+            copy = cores.start(theirs.at[h], landed.at[h], core)
+            mine[h] = contracted(dpre, 2 * h, 0)
+            return copy
+
+        def forward_half(h):
+            theirs[2 + h] = contracted(act, 2 * h + 1, 1).astype(BF)
+            copy = cores.start(theirs.at[2 + h], landed.at[2 + h], core)
+            mine[h] = contracted(act, 2 * h, 1)
+            return copy
+
+        def join(k, copy):
+            copy.wait_recv()
+            join_body(mine.at[k % 2], landed.at[k], chips.at[k])
+
+        loads[0].wait()
+        loads[3].wait()
+        pre_part(0, 0)
+        loads[1].wait()
+        loads[4].wait()
+        pre_part(0, 1)
+        pre_part(0, 2)
+        sent = back_half(0)
+        pre_part(1, 0)
+        join(0, sent)
+        crossed = [xs.start(chips.at[0], fars.at[0], across)]
+        pre_part(1, 1)
+        pre_part(1, 2)
+        sent = back_half(1)
+        sent_f = forward_half(0)
+        join(1, sent)
+        crossed.append(xs.start(chips.at[1], fars.at[1], across))
+        join(2, sent_f)
+        sent_f = forward_half(1)
+        join(3, sent_f)
+        own_half = jnp.where(first, 0, 1)
+        last = xs.start(chips.at[3 - own_half], fars.at[2], across)
+
+        def turn_rows(slots):
+            for p in range(4):
+                turned[:, p * quarter : (p + 1) * quarter] = jnp.transpose(slots[p][...])
+
+        def weight_grad(j, side, right):
+            for k in range(0, D, 512):
+                w[j, k : k + 512, side * HC : (side + 1) * HC] = dot_nn(turned[k : k + 512], right[j]).astype(BF)
+
+        def g_of(h):
+            def rows_of(r):
+                own, other = cot[r].astype(F32), i["g_got"][r].astype(F32)
+                return jnp.where(first, own, other) if h == 0 else jnp.where(first, other, own)
+
+            return rows_of
+
+        e = [o["e0"], o["e1"], o["e2"], o["e3"]]
+        passed = []
+
+        def norm_half(h):
+            crossed[h].wait_recv()
+            back_body(
+                g_of(h), i[f"after_c{h}"], chips.at[h], fars.at[h], 1.0 + i["shifts"][4:5], 1.0,
+                o[f"gc{h}"], e[2 * h], o[f"sf{h}"],
+            )
+            passed.append(cores.start(e[2 * h], e[2 * h + 1], core))
+
+        turn_rows(z)
+        weight_grad(0, 0, dpre)
+        norm_half(0)
+        weight_grad(1, 0, dpre)
+        weight_grad(2, 0, dpre)
+        turn_rows(ds)
+        stores = []
+        for j in range(3):
+            weight_grad(j, 1, act)
+            store = pltpu.make_async_copy(w.at[j], o[f"t{j}"], local.at[j])
+            store.start()
+            stores.append(store)
+            if j == 0:
+                norm_half(1)
+        last.wait_recv()
+        o["branch"][...] = chips[2 + own_half].astype(F32) + fars[2].astype(F32)
+        for copy in passed:
+            copy.wait_recv()
+        for store in stores:
+            store.wait()
+        cores.settle()
+        xs.settle()
+
+    scratch = [
+        pltpu.VMEM((3, D, 2 * HC), BF),
+        pltpu.VMEM((3, 2 * half, HC), BF),
+        pltpu.VMEM((3, 2 * half, HC), BF),
+        pltpu.VMEM((4, quarter, D), BF),
+        pltpu.VMEM((4, quarter, D), BF),
+        pltpu.VMEM((2, quarter, D), F32),
+        pltpu.VMEM((4, quarter, D), BF),
+        pltpu.VMEM((3, quarter, D), BF),
+        pltpu.VMEM((D, 2 * half), BF),
+        pltpu.SemaphoreType.DMA((2, 8)),
+        pltpu.SemaphoreType.DMA((2, 4)),
+        pltpu.SemaphoreType.DMA((5,)),
+    ]
+    got = run_remote(
+        kernel, list(outs.values()), list(far_outs.values()), blocks, far, scratch, 3, 6e10
+    )
+    return dict(zip(names, got))
+
+
+class Scatter:
+    def __init__(self, got, arrived, over, along, n):
+        d = lax.axis_index("dp")
+        self.z, self.y = d // 2, lax.rem(d, 2)
+        self.got, self.arrived, self.sems_y, self.sems_z, self.n = got, arrived, over, along, n
+        self.r = arrived.shape[1]
+
+    def block(self, full, o, own):
+        start = (2 * o + (self.y if own else 1 - self.y)) * self.r
+        return full.at[pl.ds(pl.multiple_of(start, 16), self.r)]
+
+    def begin(self, full):
+        self.full = full
+        self.sent = []
+        for o in range(self.n):
+            copy = remote(
+                self.block(full, o, False), self.got.at[o], self.sems_y.at[0, o], self.sems_y.at[1, o],
+                dp=2 * self.z + 1 - self.y,
+            )
+            copy.start()
+            self.sent.append(copy)
+
+    def pair(self, a, b, local):
+        loads = []
+        for o in range(self.n):
+            copy = pltpu.make_async_copy(self.block(self.full, o, True), a.at[o], local.at[0, o])
+            copy.start()
+            loads.append(copy)
+        for o in range(self.n):
+            self.sent[o].wait()
+            copy = pltpu.make_async_copy(self.got.at[o], b.at[o], local.at[1, o])
+            copy.start()
+            loads.append(copy)
+        for o in range(self.n):
+            loads[o].wait()
+            loads[self.n + o].wait()
+            a[o] = (a[o].astype(F32) + b[o].astype(F32)).astype(BF)
+
+    def spread(self, a):
+        self.out = []
+        for k in range(1, self.n):
+            at = lax.rem(self.z + k, self.n)
+            copy = remote(
+                a.at[at], self.arrived.at[k - 1], self.sems_z.at[0, k], self.sems_z.at[1, k], dp=2 * at + self.y
+            )
+            copy.start()
+            self.out.append(copy)
+
+    def total(self, a, stage, result, sem):
+        for copy in self.out:
+            copy.wait()
+        total = a[self.z].astype(F32)
+        for k in range(self.n - 1):
+            total = total + self.arrived[k].astype(F32)
+        stage[...] = total
+        copy = pltpu.make_async_copy(stage, result, sem)
+        copy.start()
+        copy.wait()
+
+
+def attend_back_body(do_ref, q_ref, k_refs, v_refs, lse_ref, bias_ref, dq_ref, dk_ref, dv_ref, fresh):
+    rows, wide = q_ref.shape
+    for h in range(wide // HEAD):
+        lanes = slice(h * HEAD, (h + 1) * HEAD)
+        k = jnp.concatenate([r[:, lanes] for r in k_refs]) if len(k_refs) > 1 else k_refs[0][:, lanes]
+        v = jnp.concatenate([r[:, lanes] for r in v_refs]) if len(v_refs) > 1 else v_refs[0][:, lanes]
+        for b in range(rows // QB):
+            block = slice(b * QB, (b + 1) * QB)
+            qb = q_ref[block, lanes]
+            do = do_ref[block, lanes]
+            s = dot_nt(k, qb) * FACTOR
+            if bias_ref is not None:
+                s = s + bias_ref[...]
+            p = jnp.exp(s - lse_ref[h : h + 1, block])
+            dp = dot_nt(v, do)
+            center = jnp.sum(p * dp, axis=0, keepdims=True)
+            ds = (p * (dp - center)).astype(BF)
+            dq_ref[block, lanes] = dot_tn(ds, k) * FACTOR
+            dk = dot_nn(ds, qb) * FACTOR
+            dv = dot_nn(p.astype(BF), do)
+            if b == 0 and fresh:
+                dk_ref[:, lanes] = dk
+                dv_ref[:, lanes] = dv
+            else:
+                dk_ref[:, lanes] += dk
+                dv_ref[:, lanes] += dv
+
+
+def dots_body(dy_ref, raw_ref, col, stat_ref, row, gain, tables, grad_ref, grad_row, wide):
+    scale = lax.rsqrt(to_columns(stat_ref[...]) / D + EPS)[:, row : row + 1]
+    dots = jnp.zeros((dy_ref.shape[0], 1), F32)
+    for h in range(wide // HEAD):
+        own = slice(h * HEAD, (h + 1) * HEAD)
+        dy = dy_ref[:, own]
+        if tables is not None:
+            dy = turn(dy, tables[0], -tables[1])
+            dy_ref[:, own] = dy
+        both = raw_ref[:, col + h * HEAD : col + (h + 1) * HEAD] * dy
+        dots = dots + jnp.sum(both * gain[h], axis=1, keepdims=True)
+        grad_ref[grad_row : grad_row + 1, own] += jnp.sum(both * scale, axis=0, keepdims=True)
+    return dots
+
+
+def root_back_body(dy_ref, raw_ref, col, stat_ref, row, dots_ref, dots_row, gain, low_ref, at, wide):
+    scale = lax.rsqrt(to_columns(stat_ref[...]) / D + EPS)[:, row : row + 1]
+    along = scale * scale * scale * to_columns(dots_ref[...])[:, dots_row : dots_row + 1] / D
+    for h in range(wide // HEAD):
+        own = slice(h * HEAD, (h + 1) * HEAD)
+        raw = raw_ref[:, col + h * HEAD : col + (h + 1) * HEAD]
+        dx = scale * gain[h] * dy_ref[:, own] - raw * along
+        low_ref[:, at + h * HEAD : at + (h + 1) * HEAD] = dx.astype(BF)
+
+
+class Grads:
+    def __init__(self, turned, stage, sems):
+        self.turned, self.stage, self.sems = turned, stage, sems
+        self.stores = [None, None]
+        self.used = 0
+
+    def turn(self, slots):
+        at = 0
+        for slot in slots:
+            m = slot.shape[0]
+            self.turned[:, at : at + m] = jnp.transpose(slot[...])
+            at += m
+
+    def put(self, ys, full, col):
+        i = self.used % 2
+        self.used += 1
+        if self.stores[i] is not None:
+            self.stores[i].wait()
+        for k in range(0, D, 512):
+            total, at = None, 0
+            for y in ys:
+                m = y.shape[0]
+                term = dot_nn(self.turned[k : k + 512, at : at + m], y)
+                total = term if total is None else total + term
+                at += m
+            self.stage[i, k : k + 512] = total.astype(BF)
+        store = pltpu.make_async_copy(self.stage.at[i], full.at[:, pl.ds(col, GC)], self.sems.at[i])
+        store.start()
+        self.stores[i] = store
+
+    def finish(self):
+        for i in range(2):
+            if self.stores[i] is not None:
+                self.stores[i].wait()
+                self.stores[i] = None
+
+
+def cross_backward(state, bias, n_dp, heads):
+    quarter, texts = state["e0"].shape[0], state["c0"].shape[0]
+    half, wide = 2 * quarter, heads * HEAD
+    n, r = n_dp // 2, D // n_dp
+    W = state["t0"].shape[1]
+    rows = shape((quarter, D), BF)
+    whole = shape((quarter, D), F32)
+    sums_shape = shape((16, D), F32)
+    outs = dict(
+        gs0=whole, gs1=whole, h0=rows, h1=rows, h2=rows, h3=rows, sc0=sums_shape, sc1=sums_shape,
+        cross_gain=shape((8, wide), F32), ctx_grad=shape((texts, D), BF),
+    )
+    far_outs = dict(
+        tc=shape((D, 4 * wide), BF), p1=shape((n, r, W), BF), s0=shape((r, W), F32),
+        got0=shape((n, r, W), BF), got1=shape((n, r, W), BF),
+    )
+    given = (
+        "e0", "e1", "e2", "e3", "cq0", "cq1", "ck", "cv", "clse0", "clse1", "cq_raw0", "cq_raw1", "ck_raw",
+        "cq_stat0", "cq_stat1", "ck_stat", "gains", "shifts", "gc0", "gc1", "after0", "after1", "w_cross",
+        "cattn0", "cattn1", "y0", "y1", "y2", "y3", "c0", "c1", "c2", "c3",
+    )
+    blocks = [state[name] for name in given] + [bias]
+    far = [state["t0"], state["t1"]]
+    names = [*outs, *far_outs]
+
+    def kernel(*refs):
+        i = dict(zip(given, refs))
+        bias_ref, t0, t1 = refs[len(given) : len(given) + 3]
+        refs = refs[len(given) + 3 :]
+        o = dict(zip(names, refs))
+        (
+            do, dq, dk, dv, low, dckv, theirs, landed, mine, chips, fars, c_theirs, c_landed, c_chips, c_far,
+            dots, ck_dots, stats_in, turned, stage, a, b, arrived, result,
+            near, cross_x, near_sums, over, along, local, stores,
+        ) = refs[len(names) :]
+        t, core, across, diagonal = tensor_peers()
+        first = t < 2
+        cores, xs = Swap(near), Swap(cross_x)
+        sums = Sums(stats_in, near_sums, (core, across, diagonal))
+        greet(n_dp)
+        f0 = Scatter(o["got0"], arrived, over.at[0], along.at[0], n)
+        f1 = Scatter(o["got1"], arrived, over.at[1], along.at[0], n)
+        f0.begin(t0)
+        w = i["w_cross"]
+        e = [i["e0"], i["e1"], i["e2"], i["e3"]]
+        gain_q = [i["gains"][2 * heads + h : 2 * heads + h + 1] for h in range(heads)]
+        gain_k = [i["gains"][3 * heads + h : 3 * heads + h + 1] for h in range(heads)]
+        o["cross_gain"][...] = jnp.zeros_like(o["cross_gain"])
+
+        def back(h):
+            for p in range(2):
+                do[p * quarter : (p + 1) * quarter] = dot_nn(e[2 * h + p][...], w[:, 3 * wide :]).astype(BF)
+            attend_back_body(
+                do, i[f"cq{h}"], [i["ck"]], [i["cv"]], i[f"clse{h}"], bias_ref, dq, dk, dv, h == 0
+            )
+            column = dots_body(
+                dq, i[f"cq_raw{h}"], 0, i[f"cq_stat{h}"], 0, gain_q, None, o["cross_gain"], 0, wide
+            )
+            dots[h] = to_rows([column], half)
+            return sums.start(dots.at[h])
+
+        def send(h):
+            root_back_body(
+                dq, i[f"cq_raw{h}"], 0, i[f"cq_stat{h}"], 0, dots.at[h], 0, gain_q, low.at[h], 0, wide
+            )
+            theirs[h] = dot_nt(low[h, quarter:], w[:, :wide]).astype(BF)
+            copy = cores.start(theirs.at[h], landed.at[h], core)
+            mine[...] = dot_nt(low[h, :quarter], w[:, :wide])
+            return copy
+
+        def join(h, copy):
+            copy.wait_recv()
+            join_body(mine, landed.at[h], chips.at[h])
+            return xs.start(chips.at[h], fars.at[h], across)
+
+        collect = back(0)
+        collect()
+        sent0 = send(0)
+        collect = back(1)
+        crossed = [join(0, sent0)]
+        column = dots_body(dk, i["ck_raw"], 0, i["ck_stat"], 0, gain_k, None, o["cross_gain"], 1, wide)
+        ck_dots[...] = to_rows([column], 4 * texts)
+        collect_k = [sums.start(ck_dots.at[:, pl.ds(j * 2 * texts, 2 * texts)]) for j in range(2)]
+        collect()
+        sent1 = send(1)
+        crossed.append(join(1, sent1))
+        f1.begin(t1)
+        for part in collect_k:
+            part()
+        f0.pair(a, b, local)
+        f0.spread(a)
+
+        root_back_body(dk, i["ck_raw"], 0, i["ck_stat"], 0, ck_dots, 0, gain_k, dckv, 0, wide)
+        dckv[:, wide:] = dv[...].astype(BF)
+        c_sent = []
+        for j in range(2):
+            at = 2 * texts * j
+            c_theirs[j] = dot_nt(dckv[at + texts : at + 2 * texts], w[:, wide : 3 * wide]).astype(BF)
+            c_sent.append(cores.start(c_theirs.at[j], c_landed.at[j], core))
+        for j in range(2):
+            at = 2 * texts * j
+            part = dot_nt(dckv[at : at + texts], w[:, wide : 3 * wide])
+            c_sent[j].wait_recv()
+            c_chips[j] = (part + c_landed[j].astype(F32)).astype(BF)
+        own_half = jnp.where(first, 0, 1)
+        c_last = xs.start(c_chips.at[1 - own_half], c_far, across)
+
+        h_slots = [o["h0"], o["h1"], o["h2"], o["h3"]]
+        passed = []
+
+        def norm_half(h):
+            crossed[h].wait_recv()
+            back_body(
+                lambda rows: i[f"gc{h}"][rows], i[f"after{h}"], chips.at[h], fars.at[h], i["shifts"][6:7],
+                i["shifts"][2:3], o[f"gs{h}"], h_slots[2 * h], o[f"sc{h}"],
+            )
+            passed.append(cores.start(h_slots[2 * h], h_slots[2 * h + 1], core))
+
+        norm_half(0)
+        grads = Grads(turned, stage, stores)
+        grads.turn([i["y0"], i["y1"], i["y2"], i["y3"]])
+        grads.put([low[0], low[1]], o["tc"], 0)
+        norm_half(1)
+        grads.turn([i["c0"], i["c1"], i["c2"], i["c3"]])
+        for c in range(2):
+            grads.put([dckv[:, c * wide : (c + 1) * wide]], o["tc"], (1 + c) * wide)
+        grads.turn(e)
+        grads.put([i["cattn0"][...], i["cattn1"][...]], o["tc"], 3 * wide)
+        c_last.wait_recv()
+        o["ctx_grad"][...] = (c_chips[own_half].astype(F32) + c_far[...].astype(F32)).astype(BF)
+        grads.finish()
+        f0.total(a, result, o["s0"], stores.at[0])
+        f1.pair(a, b, local)
+        copy = pltpu.make_async_copy(a, o["p1"], stores.at[0])
+        copy.start()
+        copy.wait()
+        for copy in passed:
+            copy.wait_recv()
+        cores.settle()
+        xs.settle()
+
+    scratch = [
+        pltpu.VMEM((half, wide), BF),
+        pltpu.VMEM((half, wide), F32),
+        pltpu.VMEM((4 * texts, wide), F32),
+        pltpu.VMEM((4 * texts, wide), F32),
+        pltpu.VMEM((2, half, wide), BF),
+        pltpu.VMEM((4 * texts, 2 * wide), BF),
+        pltpu.VMEM((2, quarter, D), BF),
+        pltpu.VMEM((2, quarter, D), BF),
+        pltpu.VMEM((quarter, D), F32),
+        pltpu.VMEM((2, quarter, D), BF),
+        pltpu.VMEM((2, quarter, D), BF),
+        pltpu.VMEM((2, texts, D), BF),
+        pltpu.VMEM((2, texts, D), BF),
+        pltpu.VMEM((2, texts, D), BF),
+        pltpu.VMEM((texts, D), BF),
+        pltpu.VMEM((2, 8, half), F32),
+        pltpu.VMEM((8, 4 * texts), F32),
+        pltpu.VMEM((4, 3, 8, half), F32),
+        pltpu.VMEM((D, 2 * half), BF),
+        pltpu.VMEM((2, D, GC), BF),
+        pltpu.VMEM((n, r, W), BF),
+        pltpu.VMEM((n, r, W), BF),
+        pltpu.VMEM((n - 1, r, W), BF),
+        pltpu.VMEM((r, W), F32),
+        pltpu.SemaphoreType.DMA((2, 8)),
+        pltpu.SemaphoreType.DMA((2, 4)),
+        pltpu.SemaphoreType.DMA((2, 12)),
+        pltpu.SemaphoreType.DMA((2, 2, n)),
+        pltpu.SemaphoreType.DMA((1, 2, n)),
+        pltpu.SemaphoreType.DMA((2, n)),
+        pltpu.SemaphoreType.DMA((2,)),
+    ]
+    got = run_remote(
+        kernel, list(outs.values()), list(far_outs.values()), blocks, far, scratch, 4, 4e10
+    )
+    return dict(zip(names, got))
+
+
+def self_backward(state, hidden, tables, n_dp, heads):
+    quarter = hidden.shape[0]
+    half, wide = 2 * quarter, heads * HEAD
+    n, r = n_dp // 2, D // n_dp
+    W, V = state["t2"].shape[1], 2 * wide
+    outs = dict(hidden_grad=shape((quarter, D), BF), ss=shape((16, D), F32), self_gain=shape((8, wide), F32))
+    far_outs = dict(
+        s1=shape((r, W), F32), s2=shape((r, W), F32), s3=shape((r, W), F32), s4=shape((r, V), F32), s5=shape((r, V), F32),
+        tv=shape((D, V), BF), tq=shape((D, V), BF),
+        got2=shape((n, r, W), BF), got3=shape((n, r, W), BF), got4=shape((n, r, V), BF), got5=shape((n, r, V), BF),
+    )
+    given = (
+        "h0", "h1", "h2", "h3", "q0", "q1", "k0", "k1", "v0", "v1", "lse0", "lse1", "qk0", "qk1", "stat0", "stat1",
+        "gains", "shifts", "gs0", "gs1", "attn0", "attn1", "w_self",
+    )
+    blocks = [state[name] for name in given] + [hidden, *tables]
+    far = [state["p1"], state["t2"], state["tc"], *(state[f"x{p}"] for p in range(4))]
+    names = [*outs, *far_outs]
+
+    def kernel(*refs):
+        i = dict(zip(given, refs))
+        hid, cos, sin, p1, t2, tc = refs[len(given) : len(given) + 6]
+        xs_far = refs[len(given) + 6 : len(given) + 10]
+        refs = refs[len(given) + 10 :]
+        o = dict(zip(names, refs))
+        (
+            do, dq, dk, dv, low, theirs, landed, mine, chips, far_chip,
+            dots, stats_in, turned, stage, a, b, arrived, arrived_v, result,
+            near, cross_x, near_sums, over, along, local, stores, slots,
+        ) = refs[len(names) :]
+        t, core, across, diagonal = tensor_peers()
+        first = t < 2
+        cores, xs = Swap(near), Swap(cross_x)
+        sums = Sums(stats_in, near_sums, (core, across, diagonal))
+        held = pltpu.make_async_copy(p1, a.at[0], stores.at[0])
+        held.start()
+        x_copies = [pltpu.make_async_copy(xs_far[p], theirs.at[p % 2], slots.at[p]) for p in range(4)]
+        for p in range(2):
+            x_copies[p].start()
+        greet(n_dp)
+        f1 = Scatter(None, arrived.at[0], None, along.at[0], n)
+        f2 = Scatter(o["got2"], arrived.at[1], over.at[0], along.at[1], n)
+        fc = Scatter(o["got3"], arrived.at[2], over.at[1], along.at[2], n)
+        fv = Scatter(o["got4"], arrived_v.at[0], over.at[2], along.at[3], n)
+        fq = Scatter(o["got5"], arrived_v.at[1], over.at[3], along.at[4], n)
+        f2.begin(t2)
+        held.wait()
+        f1.spread(a.at[0])
+        w = i["w_self"]
+        hs = [i["h0"], i["h1"], i["h2"], i["h3"]]
+        ks, vs = [i["k0"], i["k1"]], [i["v0"], i["v1"]]
+        gain = [[i["gains"][g * heads + h : g * heads + h + 1] for h in range(heads)] for g in range(2)]
+        o["self_gain"][...] = jnp.zeros_like(o["self_gain"])
+        for h in range(2):
+            for p in range(2):
+                do[p * quarter : (p + 1) * quarter] = dot_nn(hs[2 * h + p][...], w[:, 3 * wide :]).astype(BF)
+            attend_back_body(do, i[f"q{h}"], ks, vs, i[f"lse{h}"], None, dq.at[h], dk, dv, h == 0)
+        collects = []
+        for h in range(2):
+            own = slice(h * half, (h + 1) * half)
+            turns = (cos[own], sin[own])
+            dk_half = dk.at[pl.ds(h * half, half)]
+            columns = [
+                dots_body(dq.at[h], i[f"qk{h}"], 0, i[f"stat{h}"], 0, gain[0], turns, o["self_gain"], 0, wide),
+                dots_body(dk_half, i[f"qk{h}"], wide, i[f"stat{h}"], 1, gain[1], turns, o["self_gain"], 1, wide),
+            ]
+            dots[h] = to_rows(columns, half)
+            collects.append(sums.start(dots.at[h]))
+            low[h, :, 2 * wide :] = dv[own].astype(BF)
+
+        grads = Grads(turned, stage, stores)
+        for p in range(4):
+            x_copies[p].wait()
+            turned[:, p * quarter : (p + 1) * quarter] = jnp.transpose(theirs[p % 2])
+            if p < 2:
+                x_copies[p + 2].start()
+        grads.put([low[0, :, 2 * wide :], low[1, :, 2 * wide :]], o["tv"], 0)
+        fc.begin(tc)
+        f2.pair(a.at[1], b, local)
+        f2.spread(a.at[1])
+        sent = []
+
+        def join(h):
+            sent[h].wait_recv()
+            join_body(mine, landed.at[h], chips.at[h])
+
+        for h in range(2):
+            collects[h]()
+            dk_half = dk.at[pl.ds(h * half, half)]
+            root_back_body(dq.at[h], i[f"qk{h}"], 0, i[f"stat{h}"], 0, dots.at[h], 0, gain[0], low.at[h], 0, wide)
+            root_back_body(
+                dk_half, i[f"qk{h}"], wide, i[f"stat{h}"], 1, dots.at[h], 1, gain[1], low.at[h], wide, wide
+            )
+            theirs[h] = dot_nt(low[h, quarter:], w[:, : 3 * wide]).astype(BF)
+            sent.append(cores.start(theirs.at[h], landed.at[h], core))
+            if h == 1:
+                join(0)
+            mine[...] = dot_nt(low[h, :quarter], w[:, : 3 * wide])
+        join(1)
+        own_half = jnp.where(first, 0, 1)
+        last = xs.start(chips.at[1 - own_half], far_chip, across)
+        for c in range(2):
+            lanes = slice(c * wide, (c + 1) * wide)
+            grads.put([low[0, :, lanes], low[1, :, lanes]], o["tq"], c * wide)
+        grads.turn(hs)
+        grads.put([i["attn0"][...], i["attn1"][...]], o["tv"], wide)
+        grads.finish()
+        f1.total(a.at[0], result, o["s1"], stores.at[0])
+        fv.begin(o["tv"])
+
+        last.wait_recv()
+        m_row = 1.0 + i["shifts"][1:2]
+        sum_ref = o["ss"]
+        sum_ref[...] = jnp.zeros_like(sum_ref)
+
+        def body(rows):
+            da = chips[own_half, rows].astype(F32) + far_chip[rows].astype(F32)
+            nv, rv = norm_of(hid[rows].astype(F32))
+            dn = da * m_row
+            mean = jnp.mean(dn, axis=-1, keepdims=True)
+            proj = jnp.mean(dn * nv, axis=-1, keepdims=True)
+            g = jnp.where(first, i["gs0"][rows], i["gs1"][rows])
+            o["hidden_grad"][rows] = (g + rv * (dn - mean - nv * proj)).astype(BF)
+            dan = da * nv
+            for k in range(STEP // 8):
+                sum_ref[:8] += da[k * 8 : k * 8 + 8]
+                sum_ref[8:] += dan[k * 8 : k * 8 + 8]
+
+        over_rows(quarter, body)
+        fc.pair(a.at[0], b, local)
+        fc.spread(a.at[0])
+        fq.begin(o["tq"])
+        f2.total(a.at[1], result, o["s2"], stores.at[0])
+        a_v, b_v = a.at[1, :, :, pl.ds(0, V)], b.at[:, :, pl.ds(0, V)]
+        fv.pair(a_v, b_v, local)
+        fv.spread(a_v)
+        fc.total(a.at[0], result, o["s3"], stores.at[0])
+        a_q = a.at[0, :, :, pl.ds(0, V)]
+        fq.pair(a_q, b_v, local)
+        fq.spread(a_q)
+        fv.total(a_v, result.at[:, pl.ds(0, V)], o["s4"], stores.at[0])
+        fq.total(a_q, result.at[:, pl.ds(0, V)], o["s5"], stores.at[0])
+        cores.settle()
+        xs.settle()
+
+    scratch = [
+        pltpu.VMEM((half, wide), BF),
+        pltpu.VMEM((2, half, wide), F32),
+        pltpu.VMEM((2 * half, wide), F32),
+        pltpu.VMEM((2 * half, wide), F32),
+        pltpu.VMEM((2, half, 3 * wide), BF),
+        pltpu.VMEM((2, quarter, D), BF),
+        pltpu.VMEM((2, quarter, D), BF),
+        pltpu.VMEM((quarter, D), F32),
+        pltpu.VMEM((2, quarter, D), BF),
+        pltpu.VMEM((quarter, D), BF),
+        pltpu.VMEM((2, 8, half), F32),
+        pltpu.VMEM((2, 3, 8, half), F32),
+        pltpu.VMEM((D, 2 * half), BF),
+        pltpu.VMEM((2, D, GC), BF),
+        pltpu.VMEM((2, n, r, W), BF),
+        pltpu.VMEM((n, r, W), BF),
+        pltpu.VMEM((3, n - 1, r, W), BF),
+        pltpu.VMEM((2, n - 1, r, V), BF),
+        pltpu.VMEM((r, W), F32),
+        pltpu.SemaphoreType.DMA((2, 4)),
+        pltpu.SemaphoreType.DMA((2, 4)),
+        pltpu.SemaphoreType.DMA((2, 6)),
+        pltpu.SemaphoreType.DMA((4, 2, n)),
+        pltpu.SemaphoreType.DMA((5, 2, n)),
+        pltpu.SemaphoreType.DMA((2, n)),
+        pltpu.SemaphoreType.DMA((2,)),
+        pltpu.SemaphoreType.DMA((4,)),
+    ]
+    got = run_remote(
+        kernel, list(outs.values()), list(far_outs.values()), blocks, far, scratch, 5, 5e10
     )
     return dict(zip(names, got))
 
@@ -1295,7 +2044,7 @@
             hidden_in, context[0], out_cotangent, time_emb[0], tables, small,
             own_self, own_cross, own_ffn[0], n_dp, heads,
         )
-        st |= cross_forward(st, text_bias, own_ffn[1], own_ffn[2], n_dp, heads)
+        st |= cross_forward(st, out_cotangent, text_bias, own_ffn[1], own_ffn[2], n_dp, heads)
         d = lax.axis_index("dp")
         cosine, sine = ((t[:half], t[half:]) for t in tables)
         s0, s1, s2, s3, s4, s5, norm_gain, norm_shift = (st["shifts"][i : i + 1] for i in range(8))
@@ -1326,97 +2075,21 @@
         def with_peer(rows):
             return [rows, core_swap(rows)]
 
-        dffn = [with_peer((a.astype(F32) * s5).astype(BF)) for a in g]
-        dact = [expand(a, w_ffn, HC, hid_low) for a in dffn]
-        act, dpre, mine, theirs = zip(*(feed(ffn_rows[i], dact[i], w_ffn, 0) for i in range(2)))
-        ffn_chip = [join(a, b) for a, b in zip(mine, theirs)]
-        ffn_far = [x_swap(a) for a in ffn_chip]
-        g_c, rows, sums_f = zip(
-            *(norm_backward(g[i], after_cross[i], ffn_chip[i], ffn_far[i], 1.0 + s4, ones) for i in range(2))
-        )
-        down_grad = full_grads(dffn[0] + dffn[1], act)
-        down_grad = lax.psum_scatter(down_grad, "dp", scatter_dimension=0, tiled=True).astype(F32)
-        up_grad = full_grads(ffn_rows[0] + ffn_rows[1], dpre)
-        up_grad = lax.psum_scatter(up_grad, "dp", scatter_dimension=0, tiled=True).astype(F32)
-
-        dcross = [with_peer(a) for a in rows]
-        sofar = ()
-        dcq = []
-        for i in range(2):
-            a, *sofar = attend_back(dcross[i], w_cross, at_co, cq[i], [ck], [cv], text_bias, clse[i], sofar)
-            dcq.append(a)
-        dck, dcv = sofar
-        dcq_low, mine, theirs, cq_gain_grad = [], [], [], 0.0
-        for i in range(2):
-            raws = [(cq_raw[i], 0, 0)]
-            dots, grad = root_dots([dcq[i]], raws, [cq_stat[i]], [cq_gain], None, wide)
-            cq_gain_grad = cq_gain_grad + grad[0]
-            low, a, b = root_back(
-                [dcq[i]], raws, [cq_stat[i]], [sum_vectors(dots)], [cq_gain], None, w_cross, at_cq, wide, 1
-            )
-            dcq_low.append(low)
-            mine.append(a)
-            theirs.append(b)
-        cross_in_chip = [join(a, b) for a, b in zip(mine, theirs)]
-        cross_in_far = [x_swap(a) for a in cross_in_chip]
-        g_s, rows, sums_c = zip(
-            *(norm_backward(g_c[i], after_self[i], cross_in_chip[i], cross_in_far[i], norm_gain, s2) for i in range(2))
-        )
-        raws = [(ck_raw, 0, 0)]
-        dots, grad = root_dots([dck], raws, [ck_stat], [ck_gain], None, wide)
-        ck_gain_grad = grad[0]
-        dots = jnp.concatenate(sum_halves((dots[:, : 2 * texts], dots[:, 2 * texts :])), -1)
-        dckv, mine0, mine1, theirs0, theirs1 = root_back(
-            [dck], raws, [ck_stat], [dots], [ck_gain], dcv, w_cross, at_ck, wide, 2
-        )
-        chip = [join(mine0, theirs0), join(mine1, theirs1)]
-        context_grad = (own_half(chip).astype(F32) + x_swap(other_half(chip)).astype(F32)).astype(BF)
-        cross_grad = scatter_dp(
-            *weight_grads(
-                [(cross_rows[0] + cross_rows[1], dcq_low), (ctx, [dckv]), (dcross[0] + dcross[1], cattn)], n_dp
-            )
-        )
-
-        dself = [with_peer(a) for a in rows]
-        oT_grad = scatter_dp(*weight_grads([(dself[0] + dself[1], attn)], n_dp))
-        sofar = ()
-        dq = []
-        for i in range(2):
-            a, *sofar = attend_back(dself[i], w_self, at_o, q[i], k, v, None, lse[i], sofar)
-            dq.append(a)
-        dk, dv = sofar
-        dk, dv = (dk[:half], dk[half:]), (dv[:half], dv[half:])
-        dqkv, mine, theirs = [], [], []
-        turned, dots, self_gain_grad = [], [], 0.0
-        for i in range(2):
-            raws = [(qk[i], 0, 0), (qk[i], wide, 1)]
-            tq, tk, dot_q, dot_k, grad = root_dots(
-                [dq[i], dk[i]], raws, [stat[i]] * 2, [sq_gain, sk_gain], (cosine[i], sine[i]), wide
-            )
-            self_gain_grad = self_gain_grad + grad[:2]
-            turned.append((tq, tk))
-            dots.append(jnp.stack([dot_q, dot_k]))
-        dots = sum_halves(dots)
-        for i in range(2):
-            raws = [(qk[i], 0, 0), (qk[i], wide, 1)]
-            low, a, b = root_back(
-                list(turned[i]), raws, [stat[i]] * 2, [dots[i][0], dots[i][1]],
-                [sq_gain, sk_gain], dv[i], w_self, 0, wide, 1,
-            )
-            dqkv.append(low)
-            mine.append(a)
-            theirs.append(b)
-        qkv_grad = scatter_dp(*weight_grads([(self_rows[0] + self_rows[1], dqkv)], n_dp))
-        chip = [join(a, b) for a, b in zip(mine, theirs)]
-        ones_row = jnp.ones((1, D), F32)
-        hidden_grad, _, sums_s = norm_backward(
-            own_half(g_s), hidden_in, own_half(chip), x_swap(other_half(chip)), 1.0 + s1, ones_row
-        )
-        hidden_grad = hidden_grad.astype(BF)
-
-        mine, theirs = zip(*(contract(a, w_ffn, HC) for a in act))
-        chip = [join(a, b) for a, b in zip(mine, theirs)]
-        ffn_branch = own_half(chip).astype(F32) + x_swap(other_half(chip)).astype(F32)
+        st |= feed_forward(st, out_cotangent, n_dp)
+        g_c, sums_f = both("gc"), both("sf")
+
+        st |= cross_backward(st, text_bias, n_dp, heads)
+        st |= self_backward(st, hidden_in, tables, n_dp, heads)
+        hid_grads = [st["s0"], st["s1"], st["s2"]]
+        up_grad = jnp.concatenate([a[:, :HC] for a in hid_grads], axis=1)
+        down_grad = jnp.concatenate([a[:, HC:] for a in hid_grads], axis=1)
+        cross_grad = st["s3"]
+        qkv_grad = [st["s5"][:, :wide], st["s5"][:, wide:], st["s4"][:, :wide]]
+        oT_grad = st["s4"][:, wide:]
+        g_s, sums_c, sums_s = both("gs"), both("sc"), st["ss"]
+        hidden_grad, context_grad = st["hidden_grad"], st["ctx_grad"]
+
+        ffn_branch = st["branch"]
         block_out = (own_half(after_cross) + ffn_branch * s5).astype(BF)
 
         self_branch = own_half(self_chip).astype(F32) + own_half(self_far).astype(F32)
@@ -1437,7 +2110,7 @@
         sums_clip = sum_all(sums_own)
         time_grad = sums_clip[:6]
         low_sums = sums_clip.reshape(8, n_dp, r_dp).transpose(1, 0, 2).reshape(n_dp, -1)
-        gain_grads = jnp.stack([self_gain_grad[0], self_gain_grad[1], cq_gain_grad, ck_gain_grad])
+        gain_grads = jnp.concatenate([st["self_gain"][:2], st["cross_gain"][:2]])
         low_gains = gain_grads.reshape(4 * heads, n_dp, g_cols).transpose(1, 0, 2).reshape(n_dp, -1)
         packed = jnp.concatenate([low_sums, low_gains], axis=1).astype(BF)
         packed = jnp.pad(packed, ((0, 0), (0, -packed.shape[1] % 1024))).reshape(n_major, 2, 8, -1)
@@ -1455,9 +2128,9 @@
             context_grad[None],
             time_grad[None],
             eight[:6],
-            qkv_grad[:, :wide],
-            qkv_grad[:, wide : 2 * wide],
-            qkv_grad[:, 2 * wide :],
+            qkv_grad[0],
+            qkv_grad[1],
+            qkv_grad[2],
             oT_grad.T,
             gains_out[0],
             gains_out[1],

time: 833 us -> 784 us (0.941)
  Pallas kernels: 578 us -> 720 us
  waiting for transfers between devices: 88.8 us -> 6.89 us
  starting transfers between devices: 62.1 us -> 10.5 us
  other arithmetic: 50.2 us -> 15.8 us
  between operations: 16.4 us -> 2.33 us
  local copies, waits for them, and re-layouts: 32.4 us -> 20.9 us
    pallas_call x2 -> x5, Pallas kernels: 335 us -> 720 us  [run_remote(): pl.pallas_call(kernel, out_shape=(*outs, *far_outs), in_specs=[vmem] * le...]
    pallas_call x30 -> x0, Pallas kernels: 243 us -> none  [the longest x27 218 us: run(): pl.pallas_call(kernel, out_shape=tuple(outs), in_specs=[pl.BlockSpec(memo...]
    ppermute x12 -> x3, waiting for transfers between devices: 50.3 us -> 2.11 us  [scatter_dp(): lax.ppermute(block(t).astype(BF), 'dp', back_perm[t])]
    ppermute x12 -> x1, waiting for transfers between devices: 36.4 us -> 3.52 us  [x_swap(): return lax.ppermute(v, 'tensor', x_perm)]
    ppermute x12 -> x3, starting transfers between devices: 38.4 us -> 8.38 us  [scatter_dp(): lax.ppermute(block(t).astype(BF), 'dp', back_perm[t])]
    ppermute x12 -> x1, starting transfers between devices: 15 us -> 0.4 us  [x_swap(): return lax.ppermute(v, 'tensor', x_perm)]
  transfers between devices with their start and end apart: 51 -> 6, of which waited for: 15 -> 4; matrix products, arithmetic and copies ran while one was open for 7% -> 1% of each run, Pallas kernels for 42% -> 0%
where the time goes in v3:
time: 784 us; the launch traced here: 777 us
  Pallas kernels  720 us (92%)
  local copies, waits for them, and re-layouts  20.9 us (3%)
  other arithmetic  15.8 us (2%)
  starting transfers between devices  10.5 us (1%)
    pallas_call x5, Pallas kernels, run_remote(): pl.pallas_call(kernel, out_shape=(*outs, *far_outs), in_specs=[vmem] * le...  720 us
  transfers between devices with their start and end apart: 6, of which 4 were waited for; matrix products, arithmetic and copies ran while one was open for 1% of the time, Pallas kernels for 0%

profile of v3, /device:TPU:0, one launch (start us, length us, event | category | flops | bytes accessed | tf_op | source)
XLA Modules:
  0.0 776.9 jit_solution(4801874835801673711)
XLA Ops:
  0.8 0.7 constant_dynamic-slice_fusion.3
  1.5 1.0 fusion.1
  2.7 0.4 sin.8
  3.5 0.4 cos.6
  3.9 1.0 copy.79.refs_3_.refs_24_
  5.1 1.4 copy-done.1
  6.7 0.8 copy-done.14
  7.9 0.7 copy-done.19
  9.1 0.6 pad_bitcast_fusion.refs_5_
  9.7 1.4 copy.89
  12.0 0.2 copy.80
  12.2 0.7 broadcast_select_fusion.refs_12_.refs_33_
  12.9 0.8 broadcast_multiply_fusion.refs_4_.refs_25_
  13.8 1.1 pad_maximum_fusion.6
  14.9 1.1 pad_maximum_fusion.4
  16.0 195.3 %shard_map.382 = (bf16[1536,1536]{1,0:T(8,128)(2,1)}, bf16[1536,1536]{1,0:T(8,128)(2,1)}, bf16[256,1536]{1,0:T(8,128)(2,1)}, bf16[128,1536]{1,0:T(8,128)(2,1)}, ...) custom-call(bf16[256,1536]{1,0:T(8,128)(2,1)} %refs_23_.1, ...), custom_call_target="tpu_custom_call" | custom-call | flops 20000000000 | bytes 39415808 | tf_op jit(solution)/shard_map/pallas_call | solution.py:639
  211.3 1.4 slice_reduce_fusion.6
  212.7 0.9 pad_maximum_fusion.8.refs_15_
  213.5 114.9 %shard_map.383 = (f32[512,384]{1,0:T(8,128)}, f32[512,384]{1,0:T(8,128)}, f32[8,512]{1,0:T(8,128)}, f32[8,512]{1,0:T(8,128)}, bf16[512,384]{1,0:T(8,128)(2,1)}, ...) custom-call(bf16[1536,1536]{1,0:T(8,128)(2,1)} %get-tuple-element.12, ...), custom_call_target="tpu_custom_call" | custom-call | flops 10000000000 | bytes 38660096 | tf_op jit(solution)/shard_map/pallas_call | solution.py:639
  328.4 77.9 %shard_map.384 = (f32[256,1536]{1,0:T(8,128)}, f32[256,1536]{1,0:T(8,128)}, bf16[256,1536]{1,0:T(8,128)(2,1)}, bf16[256,1536]{1,0:T(8,128)(2,1)}, bf16[256,1536]...) custom-call(bf16[256,1536]{1,0:T(8,128)(2,1)} %get-tuple-element.135, ...), custom_call_target="tpu_custom_call" | custom-call | flops 60000002048 | bytes 19120128 | tf_op jit(solution)/shard_map/pallas_call | solution.py:639
  406.4 119.1 %shard_map.385 = (f32[256,1536]{1,0:T(8,128)}, f32[256,1536]{1,0:T(8,128)}, bf16[256,1536]{1,0:T(8,128)(2,1)}, bf16[256,1536]{1,0:T(8,128)(2,1)}, bf16[256,1536]...) custom-call(bf16[256,1536]{1,0:T(8,128)(2,1)} %get-tuple-element.148, ...), custom_call_target="tpu_custom_call" | custom-call | flops 40000000000 | bytes 30627840 | tf_op jit(solution)/shard_map/pallas_call | solution.py:639
  525.5 0.9 broadcast_select_fusion.1
  526.6 2.0 multiply_reduce_fusion.1
  528.7 213.2 %shard_map.386 = (bf16[256,1536]{1,0:T(8,128)(2,1)}, f32[16,1536]{1,0:T(8,128)}, f32[8,384]{1,0:T(8,128)}, f32[192,1536]{1,0:T(8,128)}, f32[192,1536]{1,0:T(8,12...) custom-call(bf16[256,1536]{1,0:T(8,128)(2,1)} %get-tuple-element.172, ...), custom_call_target="tpu_custom_call" | custom-call | flops 49999998976 | bytes 20156416 | tf_op jit(solution)/shard_map/pallas_call | solution.py:639
  741.9 0.9 slice_reduce_fusion.4
  742.8 3.2 multiply_reduce_fusion
  746.3 1.0 copy-done.5
  747.4 0.3 copy-done.3
  747.8 1.3 fusion
  749.1 1.3 pad_maximum_fusion.2
  750.4 0.5 copy-done.4
  750.9 1.0 slice_bitcast_fusion
  752.0 0.8 slice.232
  752.7 0.7 slice.231
  753.5 0.4 collective-permute-start.1
  754.1 3.5 collective-permute-done.1
  757.9 1.7 collective-permute-start.2
  759.6 0.8 fusion.26
  760.4 1.3 collective-permute-done.2
  761.7 5.0 collective-permute-start.3
  766.7 3.4 collective-permute-start.4
  770.1 0.8 slice_bitcast_fusion.1
  771.0 0.6 broadcast_in_dim.107
  771.7 2.0 collective-permute-done.5
  773.8 0.6 fusion.27
  774.5 0.6 fusion.28
  775.0 0.9 copy.95
  775.9 0.7 copy.96
  (134 shorter events, 3.1 us)
Async XLA Ops:
  3.3 1.6 copy-start
  5.0 1.5 copy-start.1
  6.6 1.0 copy-start.14
  6.6 1.0 copy-start.15
  6.6 1.1 copy-start.16
  6.6 1.2 copy-start.17
  6.6 1.3 copy-start.18
  7.5 1.0 copy-start.19
  7.5 1.1 copy-start.20
  7.5 1.2 copy-start.21
  7.6 1.2 copy-start.27
  7.6 1.2 copy-start.28
  7.6 1.2 copy-start.29
  7.6 1.2 copy-start.30
  7.6 1.2 copy-start.26
  7.6 1.2 copy-start.31
  7.7 1.3 copy-start.32
  406.3 120.2 %copy-start.22 = (f32[16,1536]{1,0:T(8,128)S(1)}, f32[16,1536]{1,0:T(8,128)}, u32[]{:S(2)}) copy-start(f32[16,1536]{1,0:T(8,128)} %get-tuple-element.207) | copy-start | bytes 294916
  406.3 120.2 %copy-start.23 = (f32[16,1536]{1,0:T(8,128)S(1)}, f32[16,1536]{1,0:T(8,128)}, u32[]{:S(2)}) copy-start(f32[16,1536]{1,0:T(8,128)} %get-tuple-element.208) | copy-start | bytes 294916
  406.4 120.3 %copy-start.7 = (bf16[256,1536]{1,0:T(8,128)(2,1)S(1)}, bf16[256,1536]{1,0:T(8,128)(2,1)}, u32[]{:S(2)}) copy-start(bf16[256,1536]{1,0:T(8,128)(2,1)} %get-tuple-element.203) | copy-start | bytes 2359300
  406.4 120.3 %copy-start.8 = (bf16[256,1536]{1,0:T(8,128)(2,1)S(1)}, bf16[256,1536]{1,0:T(8,128)(2,1)}, u32[]{:S(2)}) copy-start(bf16[256,1536]{1,0:T(8,128)(2,1)} %get-tuple-element.204) | copy-start | bytes 2359300
  406.4 120.3 %copy-start.9 = (bf16[256,1536]{1,0:T(8,128)(2,1)S(1)}, bf16[256,1536]{1,0:T(8,128)(2,1)}, u32[]{:S(2)}) copy-start(bf16[256,1536]{1,0:T(8,128)(2,1)} %get-tuple-element.205) | copy-start | bytes 2359300
  528.7 214.1 %copy-start.2 = (f32[256,1536]{1,0:T(8,128)S(1)}, f32[256,1536]{1,0:T(8,128)}, u32[]{:S(2)}) copy-start(f32[256,1536]{1,0:T(8,128)} %get-tuple-element.133.refs_8_) | copy-start | bytes 4718596
  528.7 214.1 %copy-start.24 = (f32[1536]{0:T(1024)S(1)}, f32[1536]{0:T(1024)}, u32[]{:S(2)}) copy-start(f32[1536]{0:T(1024)} %slice_reduce_fusion.6) | copy-start | bytes 18436
  742.8 3.4 copy-start.6
  746.0 1.3 copy-start.5
  746.1 7.3 collective-permute-start
  746.3 1.4 copy-start.3
  749.1 1.8 copy-start.4
  750.9 8.7 %copy-start.12 = (f32[192,768]{1,0:T(8,128)S(1)}, f32[192,768]{1,0:T(8,128)}, u32[]{:S(2)}) copy-start(f32[192,768]{1,0:T(8,128)} %get-tuple-element.213) | copy-start | bytes 1769476
  752.0 18.1 %copy-start.11 = (f32[192,768]{1,0:T(8,128)S(1)}, f32[192,768]{1,0:T(8,128)}, u32[]{:S(2)}) copy-start(f32[192,768]{1,0:T(8,128)} %get-tuple-element.214) | copy-start | bytes 1769476
  753.5 4.2 collective-permute-start.1
  757.7 17.3 %copy-start.10 = (bf16[256,1536]{1,0:T(8,128)(2,1)S(1)}, bf16[256,1536]{1,0:T(8,128)(2,1)}, u32[]{:S(2)}) copy-start(bf16[256,1536]{1,0:T(8,128)(2,1)} %get-tuple-element.299) | copy-start | bytes 2359300
  757.9 3.8 collective-permute-start.2
  760.4 15.5 %copy-start.13 = (bf16[128,1536]{1,0:T(8,128)(2,1)S(1)}, bf16[128,1536]{1,0:T(8,128)(2,1)}, u32[]{:S(2)}) copy-start(bf16[128,1536]{1,0:T(8,128)(2,1)} %get-tuple-element.201) | copy-start | bytes 1179652
  761.7 9.9 %collective-permute-start.3 = (bf16[8,256]{1,0:T(8,128)(2,1)S(1)}, bf16[8,256]{1,0:T(8,128)(2,1)S(1)}, u32[]{:S(2)}, u32[]{:S(2)}) collective-permute-start(bf16[8,256]{1,0:T(8,128)(2,1)S(1)} %get-tuple-element.253), channel_id=1, source_target_pairs={{0,8},{4,12},{8,16},{12,20},{16,24},{20,28},{24,0},{28,4},{1,9},{5... | collective-permute-start | bytes 12296 | tf_op jit(solution)/shard_map/ppermute | solution.py:1963
  766.7 5.0 collective-permute-start.4
  770.1 3.6 collective-permute-start.5
  774.5 2.2 copy-start.25

commit v4 on v3

--- a/solution.py
+++ b/solution.py
@@ -633,20 +633,54 @@
     )(*flat, *after)
 
 
+class Flush:
+    def __init__(self, names, held, outs, sems):
+        self.copies = {
+            name: pltpu.make_async_copy(held[j], outs[j], sems.at[j]) for j, name in enumerate(names)
+        }
+        self.gone = []
+
+    def __call__(self, *names):
+        for name in names:
+            self.copies[name].start()
+            self.gone.append(name)
+
+    def finish(self):
+        self(*[name for name in self.copies if name not in self.gone])
+        for copy in self.copies.values():
+            copy.wait()
+
+
 def run_remote(kernel, outs, far_outs, blocks, far, scratch, cid, flops):
-    moved = sum(math.prod(v.shape) * v.dtype.itemsize for v in (*blocks, *outs))
+    moved = sum(math.prod(v.shape) * v.dtype.itemsize for v in (*blocks, *outs.values()))
     vmem, hbm = pl.BlockSpec(memory_space=pltpu.VMEM), pl.BlockSpec(memory_space=pl.ANY)
-    return pl.pallas_call(
-        kernel,
-        out_shape=(*outs, *far_outs),
+    n_in, n_out, n_far = len(blocks) + len(far), len(outs), len(far_outs)
+
+    def body(*refs):
+        given, refs = refs[:n_in], refs[n_in:]
+        results, refs = refs[:n_out], refs[n_out:]
+        beyond, refs = refs[:n_far], refs[n_far:]
+        held, sems, rest = refs[:n_out], refs[n_out], refs[n_out + 1 :]
+        flush = Flush(list(outs), held, results, sems)
+        kernel(*given, *held, *beyond, *rest, flush=flush)
+        flush.finish()
+
+    got = pl.pallas_call(
+        body,
+        out_shape=(*outs.values(), *far_outs.values()),
         in_specs=[vmem] * len(blocks) + [hbm] * len(far),
-        out_specs=(vmem,) * len(outs) + (hbm,) * len(far_outs),
-        scratch_shapes=list(scratch),
+        out_specs=(hbm,) * (n_out + n_far),
+        scratch_shapes=[
+            *(pltpu.VMEM(v.shape, v.dtype) for v in outs.values()),
+            pltpu.SemaphoreType.DMA((n_out,)),
+            *scratch,
+        ],
         compiler_params=pltpu.CompilerParams(
             vmem_limit_bytes=61 * 2**20, collective_id=cid, has_side_effects=True
         ),
         cost_estimate=pl.CostEstimate(flops=int(flops), bytes_accessed=moved, transcendentals=0),
     )(*blocks, *far)
+    return dict(zip([*outs, *far_outs], got))
 
 
 def tensor_peers():
@@ -900,7 +934,7 @@
     far = [own_self, own_cross, own_first, cotangent]
     names = [*outs, *far_outs]
 
-    def kernel(*refs):
+    def kernel(*refs, flush):
         hid, ctx, times, cos, sin, small_ref = refs[:6]
         own1, own2, own3, cot = refs[6:10]
         o = dict(zip(names, refs[10 : 10 + len(names)]))
@@ -988,6 +1022,7 @@
             shared.append(sums.start(stat[j]))
             if j == 0 and n > 2:
                 g2.step(1)
+        flush("shifts", "gains", "got", "x0", "x1", "x2", "x3", "qk0", "qk1", "v0", "v1")
         q, k = [o["q0"], o["q1"]], [o["k0"], o["k1"]]
         gain = [[o["gains"][i * heads + h : i * heads + h + 1] for h in range(heads)] for i in range(4)]
         for s in range(2, n - 1):
@@ -997,6 +1032,8 @@
             shared[j]()
             own = slice(j * half, (j + 1) * half)
             normalize_body(qk[j], stat[j], gain[:2], cos[own], sin[own], [q[j], k[j]], wide)
+
+        flush("stat0", "stat1", "q0", "q1", "k0", "k1")
 
         attn, lse = [o["attn0"], o["attn1"]], [o["lse0"], o["lse1"]]
         sent = []
@@ -1014,6 +1051,7 @@
             sent[j].wait_recv()
             join_body(mine.at[j], landed.at[j], chip[j])
             crossed.append(xs.start(chip[j], far_refs[j], across))
+        flush("attn0", "attn1", "lse0", "lse1", "w_self", "chip0", "chip1")
         if n > 2:
             g3.step(1)
 
@@ -1026,6 +1064,8 @@
             part = o["ck_stat"].at[:, pl.ds(j * halves, halves)]
             sums.start(part)()
         normalize_body(o["ck_raw"], o["ck_stat"], gain[3:], None, None, [o["ck"]], wide)
+
+        flush("w_cross", "c0", "c1", "c2", "c3", "ck_raw", "cv", "ck_stat", "ck")
 
         after = [o["after0"], o["after1"]]
         y_slots = [o["y0"], o["y1"], o["y2"], o["y3"]]
@@ -1037,11 +1077,13 @@
                 base(j), chip[j], far_refs[j], shifts[2:3], shifts[6:7], shifts[7:8], after[j], y_slots[2 * j]
             )
             passed.append(cores.start(y_slots[2 * j], y_slots[2 * j + 1], core))
+            flush(f"far{j}", f"after{j}", f"y{2 * j}")
             if j == 0:
                 for s in range(2, n - 1):
                     g3.step(s)
         for copy in passed:
             copy.wait_recv()
+        flush("y1", "y3")
         g_copy.wait_recv()
         g3.finish()
         for g in (g1, g2, g3):
@@ -1065,10 +1107,7 @@
         pltpu.SemaphoreType.DMA((2, n_dp)),
         pltpu.SemaphoreType.DMA((1,)),
     ]
-    got = run_remote(
-        kernel, list(outs.values()), list(far_outs.values()), blocks, far, scratch, 1, 2e10
-    )
-    return dict(zip(names, got))
+    return run_remote(kernel, outs, far_outs, blocks, far, scratch, 1, 2e10)
 
 
 def cross_forward(state, cotangent, bias, own_second, own_third, n_dp, heads):
@@ -1093,7 +1132,7 @@
     far = [own_second, own_third, state["f0"]]
     names = [*outs, *far_outs]
 
-    def kernel(*refs):
+    def kernel(*refs, flush):
         i = dict(zip(given, refs))
         bias_ref, cot, own1, own2, f0 = refs[len(given) : len(given) + 5]
         refs = refs[len(given) + 5 :]
@@ -1156,8 +1195,10 @@
             g1.step(s)
         for copy in sent_d:
             copy.wait_recv()
+        flush("cq_raw0", "cq_raw1", "cq_stat0", "cq_stat1", "cq0", "cq1", "cattn0", "cattn1", "clse0", "clse1")
         first_down.wait()
         act_grad(0)
+        flush("d0", "d1", "d2", "d3", "dact0")
         g1.step(n - 2)
         g2.start(own2, local.at[0])
         base = [i["after0"], i["after1"]]
@@ -1171,15 +1212,18 @@
                 lambda rows, j=j: base[j][rows], chips.at[j], fars.at[j], 1.0, m_row, t_row, after[j], z_slots[2 * j]
             )
             passed.append(cores.start(z_slots[2 * j], z_slots[2 * j + 1], core))
+            flush(f"after_c{j}", f"z{2 * j}")
         g2.step(0)
         g1.finish()
         if n > 2:
             g2.step(1)
         act_grad(1)
+        flush("dact1", "f1")
         for s in range(2, n - 1):
             g2.step(s)
         for copy in passed:
             copy.wait_recv()
+        flush("z1", "z3")
         g2.finish()
         for g in (g1, g2):
             g.drain()
@@ -1200,10 +1244,7 @@
         pltpu.SemaphoreType.DMA((2, 6)),
         pltpu.SemaphoreType.DMA((3,)),
     ]
-    got = run_remote(
-        kernel, list(outs.values()), list(far_outs.values()), blocks, far, scratch, 2, 1e10
-    )
-    return dict(zip(names, got))
+    return run_remote(kernel, outs, far_outs, blocks, far, scratch, 2, 1e10)
 
 
 def back_body(g, v, chip, far, m, s, out_ref, rows_ref, sum_ref):
@@ -1241,7 +1282,7 @@
     far = [state["f0"], state["f1"], state["f2"], state["dact0"], state["dact1"]]
     names = [*outs, *far_outs]
 
-    def kernel(*refs):
+    def kernel(*refs, flush):
         i = dict(zip(given, refs))
         cot, f, dact, refs = refs[len(given)], refs[len(given) + 1 :][:3], refs[len(given) + 4 :][:2], refs[len(given) + 6 :]
         o = dict(zip(names, refs))
@@ -1345,6 +1386,7 @@
                 o[f"gc{h}"], e[2 * h], o[f"sf{h}"],
             )
             passed.append(cores.start(e[2 * h], e[2 * h + 1], core))
+            flush(f"gc{h}", f"sf{h}", f"e{2 * h}")
 
         turn_rows(z)
         weight_grad(0, 0, dpre)
@@ -1383,10 +1425,7 @@
         pltpu.SemaphoreType.DMA((2, 4)),
         pltpu.SemaphoreType.DMA((5,)),
     ]
-    got = run_remote(
-        kernel, list(outs.values()), list(far_outs.values()), blocks, far, scratch, 3, 6e10
-    )
-    return dict(zip(names, got))
+    return run_remote(kernel, outs, far_outs, blocks, far, scratch, 3, 6e10)
 
 
 class Scatter:
@@ -1394,7 +1433,7 @@
         d = lax.axis_index("dp")
         self.z, self.y = d // 2, lax.rem(d, 2)
         self.got, self.arrived, self.sems_y, self.sems_z, self.n = got, arrived, over, along, n
-        self.r = arrived.shape[1]
+        self.r = D // (2 * n)
 
     def block(self, full, o, own):
         start = (2 * o + (self.y if own else 1 - self.y)) * self.r
@@ -1427,22 +1466,74 @@
             loads[self.n + o].wait()
             a[o] = (a[o].astype(F32) + b[o].astype(F32)).astype(BF)
 
-    def spread(self, a):
-        self.out = []
-        for k in range(1, self.n):
-            at = lax.rem(self.z + k, self.n)
-            copy = remote(
-                a.at[at], self.arrived.at[k - 1], self.sems_z.at[0, k], self.sems_z.at[1, k], dp=2 * at + self.y
-            )
-            copy.start()
-            self.out.append(copy)
-
-    def total(self, a, stage, result, sem):
-        for copy in self.out:
-            copy.wait()
+    def spread(self, a, relay=None):
+        self.a, self.relay = a, relay if self.n == 4 else None
+        if self.relay is None:
+            self.out = []
+            for k in range(1, self.n):
+                at = lax.rem(self.z + k, self.n)
+                copy = self.send(at, at, self.arrived.at[k - 1], k, k)
+                copy.start()
+                self.out.append(copy)
+            return
+        z = self.z
+        self.end = (z == 0) | (z == 3)
+        self.inner = jnp.where(z < 2, 1, 2)
+        self.edge = jnp.where(z < 2, 0, 3)
+
+        @pl.when(self.end)
+        def _():
+            self.send(3 - z, self.inner, relay.at[0], 1, 1).start()
+            self.send(3 - self.inner, self.inner, relay.at[1], 2, 2).start()
+            self.send(self.inner, self.inner, self.arrived.at[0], 0, 0).start()
+
+        @pl.when(jnp.logical_not(self.end))
+        def _():
+            self.send(self.edge, self.edge, self.arrived.at[0], 0, 0).start()
+
+    def send(self, block, to, place, k, j):
+        return remote(
+            self.a.at[block], place, self.sems_z.at[0, k], self.sems_z.at[1, j], dp=2 * to + self.y
+        )
+
+    def forward(self, b, local):
+        if self.relay is None:
+            return
+
+        @pl.when(jnp.logical_not(self.end))
+        def _():
+            loads = []
+            for k in range(2):
+                self.send(self.edge, self.edge, self.relay.at[k], 1 + k, 1 + k).wait_recv()
+                copy = pltpu.make_async_copy(self.relay.at[k], b.at[k], local.at[0, k])
+                copy.start()
+                loads.append(copy)
+            for k, to in enumerate((3 - self.edge, 3 - self.inner)):
+                loads[k].wait()
+                self.a[to] = (self.a[to].astype(F32) + b[k].astype(F32)).astype(BF)
+                self.send(to, to, self.arrived.at[1], 1 + k, 3).start()
+
+    def total(self, a, stage, result, sem, b, local):
+        count = self.n - 1
+        if self.relay is None:
+            for copy in self.out:
+                copy.wait()
+        else:
+            count = 2
+            for slot, j in ((0, 0), (1, 3)):
+                self.send(self.edge, self.edge, self.arrived.at[slot], j, j).wait_recv()
+            for k in range(3):
+                self.send(self.edge, self.edge, self.arrived.at[0], k, k).wait_send()
+        arrived = self.arrived
+        if self.n != 4:
+            loads = [pltpu.make_async_copy(arrived.at[k], b.at[k], local.at[0, k]) for k in range(count)]
+            for copy in loads:
+                copy.start()
+            wait(loads)
+            arrived = b
         total = a[self.z].astype(F32)
-        for k in range(self.n - 1):
-            total = total + self.arrived[k].astype(F32)
+        for k in range(count):
+            total = total + arrived[k].astype(F32)
         stage[...] = total
         copy = pltpu.make_async_copy(stage, result, sem)
         copy.start()
@@ -1552,9 +1643,11 @@
         cross_gain=shape((8, wide), F32), ctx_grad=shape((texts, D), BF),
     )
     far_outs = dict(
-        tc=shape((D, 4 * wide), BF), p1=shape((n, r, W), BF), s0=shape((r, W), F32),
+        tc=shape((D, 4 * wide), BF), p1=shape((n, r, W), BF), s0=shape((r, W), F32), relay0=shape((2, r, W), BF),
         got0=shape((n, r, W), BF), got1=shape((n, r, W), BF),
     )
+    if n != 4:
+        far_outs["arrived"] = shape((n - 1, r, W), BF)
     given = (
         "e0", "e1", "e2", "e3", "cq0", "cq1", "ck", "cv", "clse0", "clse1", "cq_raw0", "cq_raw1", "ck_raw",
         "cq_stat0", "cq_stat1", "ck_stat", "gains", "shifts", "gc0", "gc1", "after0", "after1", "w_cross",
@@ -1564,7 +1657,7 @@
     far = [state["t0"], state["t1"]]
     names = [*outs, *far_outs]
 
-    def kernel(*refs):
+    def kernel(*refs, flush):
         i = dict(zip(given, refs))
         bias_ref, t0, t1 = refs[len(given) : len(given) + 3]
         refs = refs[len(given) + 3 :]
@@ -1579,6 +1672,7 @@
         cores, xs = Swap(near), Swap(cross_x)
         sums = Sums(stats_in, near_sums, (core, across, diagonal))
         greet(n_dp)
+        arrived = o.get("arrived", arrived)
         f0 = Scatter(o["got0"], arrived, over.at[0], along.at[0], n)
         f1 = Scatter(o["got1"], arrived, over.at[1], along.at[0], n)
         f0.begin(t0)
@@ -1629,7 +1723,7 @@
         for part in collect_k:
             part()
         f0.pair(a, b, local)
-        f0.spread(a)
+        f0.spread(a, o["relay0"])
 
         root_back_body(dk, i["ck_raw"], 0, i["ck_stat"], 0, ck_dots, 0, gain_k, dckv, 0, wide)
         dckv[:, wide:] = dv[...].astype(BF)
@@ -1656,12 +1750,14 @@
                 i["shifts"][2:3], o[f"gs{h}"], h_slots[2 * h], o[f"sc{h}"],
             )
             passed.append(cores.start(h_slots[2 * h], h_slots[2 * h + 1], core))
+            flush(f"gs{h}", f"sc{h}", f"h{2 * h}")
 
         norm_half(0)
         grads = Grads(turned, stage, stores)
         grads.turn([i["y0"], i["y1"], i["y2"], i["y3"]])
         grads.put([low[0], low[1]], o["tc"], 0)
         norm_half(1)
+        f0.forward(b, local)
         grads.turn([i["c0"], i["c1"], i["c2"], i["c3"]])
         for c in range(2):
             grads.put([dckv[:, c * wide : (c + 1) * wide]], o["tc"], (1 + c) * wide)
@@ -1670,7 +1766,7 @@
         c_last.wait_recv()
         o["ctx_grad"][...] = (c_chips[own_half].astype(F32) + c_far[...].astype(F32)).astype(BF)
         grads.finish()
-        f0.total(a, result, o["s0"], stores.at[0])
+        f0.total(a, result, o["s0"], stores.at[0], b, local)
         f1.pair(a, b, local)
         copy = pltpu.make_async_copy(a, o["p1"], stores.at[0])
         copy.start()
@@ -1703,7 +1799,7 @@
         pltpu.VMEM((2, D, GC), BF),
         pltpu.VMEM((n, r, W), BF),
         pltpu.VMEM((n, r, W), BF),
-        pltpu.VMEM((n - 1, r, W), BF),
+        pltpu.VMEM((n - 1, r, W) if n == 4 else (8, HEAD), BF),
         pltpu.VMEM((r, W), F32),
         pltpu.SemaphoreType.DMA((2, 8)),
         pltpu.SemaphoreType.DMA((2, 4)),
@@ -1713,41 +1809,46 @@
         pltpu.SemaphoreType.DMA((2, n)),
         pltpu.SemaphoreType.DMA((2,)),
     ]
-    got = run_remote(
-        kernel, list(outs.values()), list(far_outs.values()), blocks, far, scratch, 4, 4e10
-    )
-    return dict(zip(names, got))
-
-
-def self_backward(state, hidden, tables, n_dp, heads):
+    return run_remote(kernel, outs, far_outs, blocks, far, scratch, 4, 4e10)
+
+
+def self_backward(state, hidden, tables, sums_two, sums_five, n_dp, heads):
     quarter = hidden.shape[0]
     half, wide = 2 * quarter, heads * HEAD
     n, r = n_dp // 2, D // n_dp
     W, V = state["t2"].shape[1], 2 * wide
-    outs = dict(hidden_grad=shape((quarter, D), BF), ss=shape((16, D), F32), self_gain=shape((8, wide), F32))
+    g_cols = HEAD // n_dp
+    outs = dict(
+        hidden_grad=shape((quarter, D), BF), ss=shape((16, D), F32), self_gain=shape((8, wide), F32),
+        time=shape((8, D), F32), tiny=shape((r, HEAD), F32),
+    )
     far_outs = dict(
         s1=shape((r, W), F32), s2=shape((r, W), F32), s3=shape((r, W), F32), s4=shape((r, V), F32), s5=shape((r, V), F32),
         tv=shape((D, V), BF), tq=shape((D, V), BF),
+        relay1=shape((2, r, W), BF), relay2=shape((2, r, W), BF), relay3=shape((2, r, W), BF), relay4=shape((2, r, V), BF),
         got2=shape((n, r, W), BF), got3=shape((n, r, W), BF), got4=shape((n, r, V), BF), got5=shape((n, r, V), BF),
     )
+    if n != 4:
+        far_outs["arrived"] = shape((3, n - 1, r, W), BF)
+        far_outs["arrived_v"] = shape((2, n - 1, r, V), BF)
     given = (
         "h0", "h1", "h2", "h3", "q0", "q1", "k0", "k1", "v0", "v1", "lse0", "lse1", "qk0", "qk1", "stat0", "stat1",
-        "gains", "shifts", "gs0", "gs1", "attn0", "attn1", "w_self",
+        "gains", "shifts", "gs0", "gs1", "attn0", "attn1", "w_self", "sf0", "sf1", "sc0", "sc1", "cross_gain",
     )
-    blocks = [state[name] for name in given] + [hidden, *tables]
+    blocks = [state[name] for name in given] + [hidden, *tables, sums_two, sums_five]
     far = [state["p1"], state["t2"], state["tc"], *(state[f"x{p}"] for p in range(4))]
     names = [*outs, *far_outs]
 
-    def kernel(*refs):
+    def kernel(*refs, flush):
         i = dict(zip(given, refs))
-        hid, cos, sin, p1, t2, tc = refs[len(given) : len(given) + 6]
-        xs_far = refs[len(given) + 6 : len(given) + 10]
-        refs = refs[len(given) + 10 :]
+        hid, cos, sin, two, five, p1, t2, tc = refs[len(given) : len(given) + 8]
+        xs_far = refs[len(given) + 8 : len(given) + 12]
+        refs = refs[len(given) + 12 :]
         o = dict(zip(names, refs))
         (
             do, dq, dk, dv, low, theirs, landed, mine, chips, far_chip,
-            dots, stats_in, turned, stage, a, b, arrived, arrived_v, result,
-            near, cross_x, near_sums, over, along, local, stores, slots,
+            dots, stats_in, turned, stage, a, b, arrived, arrived_v, result, four_sums, side, side_in,
+            near, cross_x, near_sums, over, along, local, stores, slots, side_sems,
         ) = refs[len(names) :]
         t, core, across, diagonal = tensor_peers()
         first = t < 2
@@ -1759,6 +1860,7 @@
         for p in range(2):
             x_copies[p].start()
         greet(n_dp)
+        arrived, arrived_v = o.get("arrived", arrived), o.get("arrived_v", arrived_v)
         f1 = Scatter(None, arrived.at[0], None, along.at[0], n)
         f2 = Scatter(o["got2"], arrived.at[1], over.at[0], along.at[1], n)
         fc = Scatter(o["got3"], arrived.at[2], over.at[1], along.at[2], n)
@@ -1766,7 +1868,7 @@
         fq = Scatter(o["got5"], arrived_v.at[1], over.at[3], along.at[4], n)
         f2.begin(t2)
         held.wait()
-        f1.spread(a.at[0])
+        f1.spread(a.at[0], o["relay1"])
         w = i["w_self"]
         hs = [i["h0"], i["h1"], i["h2"], i["h3"]]
         ks, vs = [i["k0"], i["k1"]], [i["v0"], i["v1"]]
@@ -1797,8 +1899,9 @@
                 x_copies[p + 2].start()
         grads.put([low[0, :, 2 * wide :], low[1, :, 2 * wide :]], o["tv"], 0)
         fc.begin(tc)
+        f1.forward(b, local)
         f2.pair(a.at[1], b, local)
-        f2.spread(a.at[1])
+        f2.spread(a.at[1], o["relay2"])
         sent = []
 
         def join(h):
@@ -1826,7 +1929,7 @@
         grads.turn(hs)
         grads.put([i["attn0"][...], i["attn1"][...]], o["tv"], wide)
         grads.finish()
-        f1.total(a.at[0], result, o["s1"], stores.at[0])
+        f1.total(a.at[0], result, o["s1"], stores.at[0], b, local)
         fv.begin(o["tv"])
 
         last.wait_recv()
@@ -1848,19 +1951,72 @@
                 sum_ref[8:] += dan[k * 8 : k * 8 + 8]
 
         over_rows(quarter, body)
+        flush("hidden_grad")
+
+        def summed(ref, at):
+            return jnp.sum(ref[at : at + 8], axis=0, keepdims=True)
+
+        def own(name, at):
+            return jnp.where(first, summed(i[name + "0"], at), summed(i[name + "1"], at))
+
+        four_sums[0] = jnp.concatenate(
+            [
+                summed(sum_ref, 0), summed(sum_ref, 8), two[...], own("sf", 0), own("sf", 8), five[...],
+                own("sc", 8), own("sc", 0),
+            ]
+        )
+        cores.start(four_sums.at[0], four_sums.at[1], core).wait_recv()
+        four_sums[2] = four_sums[0] + four_sums[1]
+        xs.start(four_sums.at[2], four_sums.at[3], across).wait_recv()
+        o["time"][...] = four_sums[2] + four_sums[3]
+        flush("time", "ss", "self_gain")
+        head_rows = [
+            ref[g : g + 1, h * HEAD : (h + 1) * HEAD]
+            for ref in (o["self_gain"], i["cross_gain"])
+            for g in range(2)
+            for h in range(heads)
+        ]
+        head_rows = jnp.concatenate([*head_rows, jnp.zeros((16 - 4 * heads, HEAD), F32)])
+        at = lax.broadcasted_iota(jnp.int32, (D, HEAD), 0)
+        to = lax.broadcasted_iota(jnp.int32, (D, HEAD), 1)
+        pick = (at == (to // g_cols) * r + lax.rem(to, g_cols)).astype(F32)
+        spread = dot_nt(head_rows.astype(BF), pick.astype(BF))
+        both = jnp.concatenate([o["time"][...], spread, jnp.zeros((HEAD - 24, D), F32)])
+        side[...] = jnp.transpose(both).astype(BF)
+        d = lax.axis_index("dp")
+
+        def side_block(k):
+            return side.at[pl.ds(pl.multiple_of(lax.rem(d + k, n_dp) * r, 16), r)]
+
+        side_copies = []
+        for k in range(1, n_dp):
+            copy = remote(
+                side_block(k), side_in.at[k - 1], side_sems.at[0, k], side_sems.at[1, k], dp=lax.rem(d + k, n_dp)
+            )
+            copy.start()
+            side_copies.append(copy)
+        f2.forward(b, local)
+        fq.begin(o["tq"])
         fc.pair(a.at[0], b, local)
-        fc.spread(a.at[0])
-        fq.begin(o["tq"])
-        f2.total(a.at[1], result, o["s2"], stores.at[0])
-        a_v, b_v = a.at[1, :, :, pl.ds(0, V)], b.at[:, :, pl.ds(0, V)]
+        fc.spread(a.at[0], o["relay3"])
+        f2.total(a.at[1], result, o["s2"], stores.at[0], b, local)
+        a_v, a_q = (a.at[1, :, :, pl.ds(c * V, V)] for c in range(2))
+        b_v = b.at[:, :, pl.ds(0, V)]
         fv.pair(a_v, b_v, local)
-        fv.spread(a_v)
-        fc.total(a.at[0], result, o["s3"], stores.at[0])
-        a_q = a.at[0, :, :, pl.ds(0, V)]
+        fv.spread(a_v, o["relay4"])
+        fc.forward(b, local)
+        fv.forward(b_v, local)
         fq.pair(a_q, b_v, local)
         fq.spread(a_q)
-        fv.total(a_v, result.at[:, pl.ds(0, V)], o["s4"], stores.at[0])
-        fq.total(a_q, result.at[:, pl.ds(0, V)], o["s5"], stores.at[0])
+        fc.total(a.at[0], result, o["s3"], stores.at[0], b, local)
+        fv.total(a_v, result.at[:, pl.ds(0, V)], o["s4"], stores.at[0], b_v, local)
+        small = side_block(0)[...].astype(F32)
+        for k in range(1, n_dp):
+            side_copies[k - 1].wait()
+            small = small + side_in[k - 1].astype(F32)
+        o["tiny"][...] = small
+        flush("tiny")
+        fq.total(a_q, result.at[:, pl.ds(0, V)], o["s5"], stores.at[0], b_v, local)
         cores.settle()
         xs.settle()
 
@@ -1881,9 +2037,12 @@
         pltpu.VMEM((2, D, GC), BF),
         pltpu.VMEM((2, n, r, W), BF),
         pltpu.VMEM((n, r, W), BF),
-        pltpu.VMEM((3, n - 1, r, W), BF),
-        pltpu.VMEM((2, n - 1, r, V), BF),
+        pltpu.VMEM((3, n - 1, r, W) if n == 4 else (8, HEAD), BF),
+        pltpu.VMEM((2, n - 1, r, V) if n == 4 else (8, HEAD), BF),
         pltpu.VMEM((r, W), F32),
+        pltpu.VMEM((4, 8, D), F32),
+        pltpu.VMEM((D, HEAD), BF),
+        pltpu.VMEM((n_dp - 1, r, HEAD), BF),
         pltpu.SemaphoreType.DMA((2, 4)),
         pltpu.SemaphoreType.DMA((2, 4)),
         pltpu.SemaphoreType.DMA((2, 6)),
@@ -1892,11 +2051,9 @@
         pltpu.SemaphoreType.DMA((2, n)),
         pltpu.SemaphoreType.DMA((2,)),
         pltpu.SemaphoreType.DMA((4,)),
+        pltpu.SemaphoreType.DMA((2, n_dp)),
     ]
-    got = run_remote(
-        kernel, list(outs.values()), list(far_outs.values()), blocks, far, scratch, 5, 5e10
-    )
-    return dict(zip(names, got))
+    return run_remote(kernel, outs, far_outs, blocks, far, scratch, 5, 5e10)
 
 
 def rotary_tables(positions, head_dim):
@@ -2079,48 +2236,25 @@
         g_c, sums_f = both("gc"), both("sf")
 
         st |= cross_backward(st, text_bias, n_dp, heads)
-        st |= self_backward(st, hidden_in, tables, n_dp, heads)
+        g_own = own_half(both("gs"))
+        self_branch = own_half(self_chip).astype(F32) + own_half(self_far).astype(F32)
+        ffn_branch = st["branch"]
+        sums_two = jnp.sum(g_own * self_branch, 0, keepdims=True)
+        sums_five = jnp.sum(out_cotangent.astype(F32) * ffn_branch, 0, keepdims=True)
+        st |= self_backward(st, hidden_in, tables, sums_two, sums_five, n_dp, heads)
         hid_grads = [st["s0"], st["s1"], st["s2"]]
         up_grad = jnp.concatenate([a[:, :HC] for a in hid_grads], axis=1)
         down_grad = jnp.concatenate([a[:, HC:] for a in hid_grads], axis=1)
         cross_grad = st["s3"]
         qkv_grad = [st["s5"][:, :wide], st["s5"][:, wide:], st["s4"][:, :wide]]
         oT_grad = st["s4"][:, wide:]
-        g_s, sums_c, sums_s = both("gs"), both("sc"), st["ss"]
         hidden_grad, context_grad = st["hidden_grad"], st["ctx_grad"]
 
-        ffn_branch = st["branch"]
         block_out = (own_half(after_cross) + ffn_branch * s5).astype(BF)
 
-        self_branch = own_half(self_chip).astype(F32) + own_half(self_far).astype(F32)
-        sums_f = own_half(sums_f)
-        sums_c = own_half(sums_c)
-        sums_own = jnp.stack(
-            [
-                jnp.sum(sums_s[:8], 0),
-                jnp.sum(sums_s[8:], 0),
-                jnp.sum(own_half(g_s) * self_branch, 0),
-                jnp.sum(sums_f[:8], 0),
-                jnp.sum(sums_f[8:], 0),
-                jnp.sum(out_cotangent.astype(F32) * ffn_branch, 0),
-                jnp.sum(sums_c[8:], 0),
-                jnp.sum(sums_c[:8], 0),
-            ]
-        )
-        sums_clip = sum_all(sums_own)
-        time_grad = sums_clip[:6]
-        low_sums = sums_clip.reshape(8, n_dp, r_dp).transpose(1, 0, 2).reshape(n_dp, -1)
-        gain_grads = jnp.concatenate([st["self_gain"][:2], st["cross_gain"][:2]])
-        low_gains = gain_grads.reshape(4 * heads, n_dp, g_cols).transpose(1, 0, 2).reshape(n_dp, -1)
-        packed = jnp.concatenate([low_sums, low_gains], axis=1).astype(BF)
-        packed = jnp.pad(packed, ((0, 0), (0, -packed.shape[1] % 1024))).reshape(n_major, 2, 8, -1)
-        minor = d % 2
-        tiny = scatter_dp(
-            lax.dynamic_slice_in_dim(packed, 1 - minor, 1, 1)[:, 0],
-            lax.dynamic_slice_in_dim(packed, minor, 1, 1)[:, 0],
-        ).reshape(-1)
-        eight = tiny[: 8 * r_dp].reshape(8, r_dp)
-        gains_out = tiny[8 * r_dp : 8 * r_dp + 4 * heads * g_cols].reshape(4, heads, g_cols)
+        time_grad = st["time"][:6]
+        eight = st["tiny"][:, :8].T
+        gains_out = st["tiny"][:g_cols, 8 : 8 + 4 * heads].T.reshape(4, heads, g_cols)
 
         return (
             block_out,

time: 784 us -> 742 us (0.946)
  Pallas kernels: 720 us -> 697 us
  starting transfers between devices: 10.5 us -> 0 us
    pallas_call x5, Pallas kernels: 720 us -> 697 us  [run_remote(): pl.pallas_call(body, out_shape=(*outs.values(), *far_outs.values()), in_s...]
    ppermute x6 -> x0, starting transfers between devices: 10.5 us -> none  [the longest x3 8.38 us: scatter_dp(): lax.ppermute(block(t).astype(BF), 'dp', back_perm[t])]
  transfers between devices with their start and end apart: 6 -> 0, of which waited for: 4 -> 0; matrix products, arithmetic and copies ran while one was open for 1% -> 0% of each run, Pallas kernels for 0% -> 0%
where the time goes in v4:
time: 742 us; the launch traced here: 734 us
  Pallas kernels  697 us (94%)
  local copies, waits for them, and re-layouts  22 us (3%)
  other arithmetic  12.4 us (2%)
    pallas_call x5, Pallas kernels, run_remote(): pl.pallas_call(body, out_shape=(*outs.values(), *far_outs.values()), in_s...  697 us

profile of v4, /device:TPU:0, one launch (start us, length us, event | category | flops | bytes accessed | tf_op | source)
XLA Modules:
  0.0 733.8 jit_solution(14394449878387964755)
XLA Ops:
  0.7 0.7 constant_dynamic-slice_fusion.3
  1.5 1.0 fusion.1
  2.5 0.2 broadcast_in_dim.105
  2.7 0.4 sin.8
  3.1 0.2 copy.91
  3.3 0.8 broadcast_multiply_fusion.refs_4_.refs_30_
  4.1 0.2 broadcast_in_dim.104
  4.3 0.4 cos.6
  4.7 1.0 copy.93.refs_3_.refs_29_
  5.9 1.4 copy-done.1
  7.5 1.1 pad_maximum_fusion.6
  8.6 0.2 copy-done.18
  8.8 0.2 copy-done.19
  9.2 0.4 copy-done.21
  9.8 1.1 pad_maximum_fusion.4
  11.2 0.6 pad_bitcast_fusion.refs_5_
  11.9 0.6 copy.104
  12.5 186.0 %shard_map.382 = (bf16[1536,1536]{1,0:T(8,128)(2,1)}, bf16[1536,1536]{1,0:T(8,128)(2,1)}, bf16[256,1536]{1,0:T(8,128)(2,1)}, bf16[128,1536]{1,0:T(8,128)(2,1)}, ...) custom-call(bf16[256,1536]{1,0:T(8,128)(2,1)} %refs_28_.1, ...), custom_call_target="tpu_custom_call" | custom-call | flops 20000000000 | bytes 39415808 | tf_op jit(solution)/shard_map/pallas_call | solution.py:668
  199.4 0.2 copy.94
  199.6 0.7 broadcast_select_fusion.refs_12_.refs_33_
  200.3 0.9 pad_maximum_fusion.8.refs_15_
  201.2 108.8 %shard_map.383 = (f32[512,384]{1,0:T(8,128)}, f32[512,384]{1,0:T(8,128)}, f32[8,512]{1,0:T(8,128)}, f32[8,512]{1,0:T(8,128)}, bf16[512,384]{1,0:T(8,128)(2,1)}, ...) custom-call(bf16[1536,1536]{1,0:T(8,128)(2,1)} %get-tuple-element.12, ...), custom_call_target="tpu_custom_call" | custom-call | flops 10000000000 | bytes 38660096 | tf_op jit(solution)/shard_map/pallas_call | solution.py:668
  309.9 76.2 %shard_map.384 = (f32[256,1536]{1,0:T(8,128)}, f32[256,1536]{1,0:T(8,128)}, bf16[256,1536]{1,0:T(8,128)(2,1)}, bf16[256,1536]{1,0:T(8,128)(2,1)}, bf16[256,1536]...) custom-call(bf16[256,1536]{1,0:T(8,128)(2,1)} %get-tuple-element.135, ...), custom_call_target="tpu_custom_call" | custom-call | flops 60000002048 | bytes 19120128 | tf_op jit(solution)/shard_map/pallas_call | solution.py:668
  386.2 117.4 %shard_map.385 = (f32[256,1536]{1,0:T(8,128)}, f32[256,1536]{1,0:T(8,128)}, bf16[256,1536]{1,0:T(8,128)(2,1)}, bf16[256,1536]{1,0:T(8,128)(2,1)}, bf16[256,1536]...) custom-call(bf16[256,1536]{1,0:T(8,128)(2,1)} %get-tuple-element.148, ...), custom_call_target="tpu_custom_call" | custom-call | flops 40000000000 | bytes 30627840 | tf_op jit(solution)/shard_map/pallas_call | solution.py:668
  503.6 2.2 multiply_reduce_fusion.1
  505.8 0.6 broadcast_in_dim.112.refs_31_
  506.4 0.8 slice_reduce_fusion.2
  507.3 1.5 multiply_reduce_fusion
  508.7 0.6 broadcast_in_dim.113.refs_32_
  509.3 208.9 %shard_map.386 = (bf16[256,1536]{1,0:T(8,128)(2,1)}, f32[16,1536]{1,0:T(8,128)}, f32[8,384]{1,0:T(8,128)}, f32[8,1536]{1,0:T(8,128)}, f32[192,128]{1,0:T(8,128)}...) custom-call(bf16[256,1536]{1,0:T(8,128)(2,1)} %get-tuple-element.172, ...), custom_call_target="tpu_custom_call" | custom-call | flops 49999998976 | bytes 20721664 | tf_op jit(solution)/shard_map/pallas_call | solution.py:668
  718.3 1.4 fusion.14
  719.7 0.2 copy-done.7
  720.0 1.0 copy-done.5
  721.1 1.3 fusion
  722.4 1.3 pad_maximum_fusion.2
  723.7 0.5 copy-done.6
  724.2 1.0 slice_bitcast_fusion
  725.3 0.9 fusion.16
  726.1 0.8 slice_bitcast_fusion.1
  727.0 0.7 copy.97
  727.7 0.8 slice_reduce_fusion
  728.5 0.7 copy.96
  729.3 0.7 copy.100
  730.0 0.7 copy.101
  730.6 0.7 copy.98
  731.3 0.7 copy.99
  731.9 0.9 copy.108
  732.8 0.7 copy.109
  (102 shorter events, 1.5 us)
Async XLA Ops:
  4.1 1.6 copy-start
  5.8 1.5 copy-start.1
  7.4 1.2 copy-start.16
  7.4 1.2 copy-start.17
  7.4 1.4 copy-start.18
  7.5 1.6 copy-start.19
  7.5 1.7 copy-start.20
  8.6 1.0 copy-start.21
  8.6 1.1 copy-start.22
  8.6 1.2 copy-start.23
  9.7 1.2 copy-start.28
  9.7 1.2 copy-start.29
  9.7 1.3 copy-start.30
  9.7 1.3 copy-start.31
  9.7 1.3 copy-start.27
  9.7 1.3 copy-start.32
  9.7 1.3 copy-start.33
  9.8 2.1 copy-start.26
  386.1 117.4 %copy-start.9 = (bf16[256,1536]{1,0:T(8,128)(2,1)S(1)}, bf16[256,1536]{1,0:T(8,128)(2,1)}, u32[]{:S(2)}) copy-start(bf16[256,1536]{1,0:T(8,128)(2,1)} %get-tuple-element.198) | copy-start | bytes 2359300
  386.1 117.4 %copy-start.10 = (bf16[256,1536]{1,0:T(8,128)(2,1)S(1)}, bf16[256,1536]{1,0:T(8,128)(2,1)}, u32[]{:S(2)}) copy-start(bf16[256,1536]{1,0:T(8,128)(2,1)} %get-tuple-element.199) | copy-start | bytes 2359300
  386.1 117.4 %copy-start.11 = (bf16[256,1536]{1,0:T(8,128)(2,1)S(1)}, bf16[256,1536]{1,0:T(8,128)(2,1)}, u32[]{:S(2)}) copy-start(bf16[256,1536]{1,0:T(8,128)(2,1)} %get-tuple-element.200) | copy-start | bytes 2359300
  503.6 3.7 copy-start.2
  503.6 3.7 copy-start.3
  503.6 3.7 copy-start.4
  503.6 3.7 copy-start.8
  718.3 1.6 copy-start.7
  719.7 1.3 copy-start.5
  722.4 1.8 copy-start.6
  723.7 1.5 copy-start.14
  724.2 1.9 copy-start.13
  725.3 1.7 copy-start.24
  725.3 3.2 copy-start.25
  725.3 6.6 copy-start.12
  726.1 6.7 copy-start.15

commit v5 on v4

--- a/solution.py
+++ b/solution.py
@@ -1123,7 +1123,8 @@
         clse0=shape((8, half), F32), clse1=shape((8, half), F32),
         after_c0=shape((quarter, D), F32), after_c1=shape((quarter, D), F32),
         z0=rows, z1=rows, z2=rows, z3=rows, d0=rows, d1=rows, d2=rows, d3=rows,
-        dact0=shape((2 * half, HC), BF), dact1=shape((2 * half, HC), BF),
+        dpre0=shape((2 * half, HC), BF), dpre1=shape((2 * half, HC), BF),
+        act0=shape((2 * half, HC), BF), act1=shape((2 * half, HC), BF),
         f1=shape((D, own_second.shape[1]), BF), f2=shape((D, own_third.shape[1]), BF),
     )
     far_outs = {}
@@ -1155,7 +1156,16 @@
         def act_grad(part):
             down = o["f1"][:, HC:] if part else w_down[...]
             for p, slot in enumerate(d_slots):
-                o[f"dact{part}"][p * quarter : (p + 1) * quarter] = dot_nn(slot[...], down).astype(BF)
+                o[f"dpre{part}"][p * quarter : (p + 1) * quarter] = dot_nn(slot[...], down).astype(BF)
+
+        def activate(part, h):
+            up = o["f1"][:, :HC] if part else w_down[...]
+            act_ref, dpre_ref = o[f"act{part}"], o[f"dpre{part}"]
+            for p in (2 * h, 2 * h + 1):
+                own = slice(p * quarter, (p + 1) * quarter)
+                u = dot_nn(z_slots[p][...], up)
+                act_ref[own], slope = gelu_of(u)
+                dpre_ref[own] = (dpre_ref[own].astype(F32) * slope).astype(BF)
 
         w = i["w_cross"]
         slots = [i["y0"], i["y1"], i["y2"], i["y3"]]
@@ -1198,7 +1208,9 @@
         flush("cq_raw0", "cq_raw1", "cq_stat0", "cq_stat1", "cq0", "cq1", "cattn0", "cattn1", "clse0", "clse1")
         first_down.wait()
         act_grad(0)
-        flush("d0", "d1", "d2", "d3", "dact0")
+        first_up = pltpu.make_async_copy(f0.at[:, pl.ds(0, HC)], w_down, local.at[2])
+        first_up.start()
+        flush("d0", "d1", "d2", "d3")
         g1.step(n - 2)
         g2.start(own2, local.at[0])
         base = [i["after0"], i["after1"]]
@@ -1213,17 +1225,23 @@
             )
             passed.append(cores.start(z_slots[2 * j], z_slots[2 * j + 1], core))
             flush(f"after_c{j}", f"z{2 * j}")
-        g2.step(0)
+            if j == 0:
+                g2.step(0)
         g1.finish()
+        act_grad(1)
+        flush("f1")
         if n > 2:
             g2.step(1)
-        act_grad(1)
-        flush("dact1", "f1")
+        first_up.wait()
+        for j in range(2):
+            passed[j].wait_recv()
+            activate(0, j)
+        flush("z1", "z3", "act0", "dpre0")
+        activate(1, 0)
         for s in range(2, n - 1):
             g2.step(s)
-        for copy in passed:
-            copy.wait_recv()
-        flush("z1", "z3")
+        activate(1, 1)
+        flush("act1", "dpre1")
         g2.finish()
         for g in (g1, g2):
             g.drain()
@@ -1247,6 +1265,14 @@
     return run_remote(kernel, outs, far_outs, blocks, far, scratch, 2, 1e10)
 
 
+def gelu_of(u):
+    sq = u * u
+    th = jnp.tanh(u * (GELU + GELU * CUBE * sq))
+    near = 0.5 + 0.5 * th
+    slope = near + u * near * (1.0 - th) * (GELU + 3 * GELU * CUBE * sq)
+    return (u * near).astype(BF), slope
+
+
 def back_body(g, v, chip, far, m, s, out_ref, rows_ref, sum_ref):
     sum_ref[...] = jnp.zeros_like(sum_ref)
 
@@ -1279,12 +1305,12 @@
     far_outs = {f"t{j}": shape((D, 2 * HC), BF) for j in range(3)}
     given = ("z0", "z1", "z2", "z3", "d0", "d1", "d2", "d3", "after_c0", "after_c1", "shifts", "g_got")
     blocks = [state[name] for name in given] + [cotangent]
-    far = [state["f0"], state["f1"], state["f2"], state["dact0"], state["dact1"]]
+    far = [state[name] for name in ("f0", "f1", "f2", "dpre0", "dpre1", "act0", "act1")]
     names = [*outs, *far_outs]
 
     def kernel(*refs, flush):
         i = dict(zip(given, refs))
-        cot, f, dact, refs = refs[len(given)], refs[len(given) + 1 :][:3], refs[len(given) + 4 :][:2], refs[len(given) + 6 :]
+        cot, f, early, refs = refs[len(given)], refs[len(given) + 1 :][:3], refs[len(given) + 4 :][:4], refs[len(given) + 8 :]
         o = dict(zip(names, refs))
         (
             w, act, dpre, theirs, landed, mine, chips, fars, turned, near, cross_x, local,
@@ -1293,7 +1319,8 @@
         first = t < 2
         cores, xs = Swap(near), Swap(cross_x)
         loads = [pltpu.make_async_copy(f[j], w.at[j], local.at[j]) for j in range(3)]
-        loads += [pltpu.make_async_copy(dact[j], dpre.at[j], local.at[3 + j]) for j in range(2)]
+        places = (dpre.at[0], dpre.at[1], act.at[0], act.at[1])
+        loads += [pltpu.make_async_copy(early[j], places[j], local.at[3 + j]) for j in range(4)]
         for copy in loads:
             copy.start()
         greet(n_dp)
@@ -1307,11 +1334,7 @@
             for p in (2 * h, 2 * h + 1):
                 own = slice(p * quarter, (p + 1) * quarter)
                 u = dot_nn(z[p][...], w[j, :, :HC])
-                sq = u * u
-                th = jnp.tanh(u * (GELU + GELU * CUBE * sq))
-                near_half = 0.5 + 0.5 * th
-                act[j, own] = (u * near_half).astype(BF)
-                slope = near_half + u * near_half * (1.0 - th) * (GELU + 3 * GELU * CUBE * sq)
+                act[j, own], slope = gelu_of(u)
                 dpre[j, own] = (dpre[j, own].astype(F32) * slope).astype(BF)
 
         def contracted(a, p, side):
@@ -1338,19 +1361,13 @@
             copy.wait_recv()
             join_body(mine.at[k % 2], landed.at[k], chips.at[k])
 
-        loads[0].wait()
-        loads[3].wait()
-        pre_part(0, 0)
-        loads[1].wait()
-        loads[4].wait()
-        pre_part(0, 1)
         pre_part(0, 2)
+        for copy in (*loads[:2], *loads[3:]):
+            copy.wait()
         sent = back_half(0)
-        pre_part(1, 0)
+        pre_part(1, 2)
         join(0, sent)
         crossed = [xs.start(chips.at[0], fars.at[0], across)]
-        pre_part(1, 1)
-        pre_part(1, 2)
         sent = back_half(1)
         sent_f = forward_half(0)
         join(1, sent)
@@ -1423,7 +1440,7 @@
         pltpu.VMEM((D, 2 * half), BF),
         pltpu.SemaphoreType.DMA((2, 8)),
         pltpu.SemaphoreType.DMA((2, 4)),
-        pltpu.SemaphoreType.DMA((5,)),
+        pltpu.SemaphoreType.DMA((7,)),
     ]
     return run_remote(kernel, outs, far_outs, blocks, far, scratch, 3, 6e10)
 

time: 742 us -> 739 us (level)
  no operation moved by 1% of the time
where the time goes in v5:
time: 739 us; the launch traced here: 730 us
  Pallas kernels  694 us (94%)
  local copies, waits for them, and re-layouts  22 us (3%)
  other arithmetic  12.4 us (2%)
    pallas_call x5, Pallas kernels, run_remote(): pl.pallas_call(body, out_shape=(*outs.values(), *far_outs.values()), in_s...  694 us

profile of v5, /device:TPU:0, one launch (start us, length us, event | category | flops | bytes accessed | tf_op | source)
XLA Modules:
  0.0 730.1 jit_solution(47303916243540712)
XLA Ops:
  0.7 0.7 constant_dynamic-slice_fusion.3
  1.5 1.0 fusion.1
  2.5 0.2 broadcast_in_dim.105
  2.7 0.4 sin.8
  3.1 0.2 copy.91
  3.3 0.8 broadcast_multiply_fusion.refs_4_.refs_30_
  4.1 0.2 broadcast_in_dim.104
  4.3 0.4 cos.6
  4.7 1.0 copy.93.refs_3_.refs_29_
  5.9 1.4 copy-done.1
  7.5 1.1 pad_maximum_fusion.6
  8.7 0.2 copy-done.18
  8.9 0.2 copy-done.19
  9.2 0.4 copy-done.21
  9.8 1.1 pad_maximum_fusion.4
  11.2 0.6 pad_bitcast_fusion.refs_5_
  11.9 0.6 copy.104
  12.5 186.0 %shard_map.382 = (bf16[1536,1536]{1,0:T(8,128)(2,1)}, bf16[1536,1536]{1,0:T(8,128)(2,1)}, bf16[256,1536]{1,0:T(8,128)(2,1)}, bf16[128,1536]{1,0:T(8,128)(2,1)}, ...) custom-call(bf16[256,1536]{1,0:T(8,128)(2,1)} %refs_28_.1, ...), custom_call_target="tpu_custom_call" | custom-call | flops 20000000000 | bytes 39415808 | tf_op jit(solution)/shard_map/pallas_call | solution.py:668
  199.4 0.2 copy.94
  199.6 0.7 broadcast_select_fusion.refs_12_.refs_33_
  200.3 0.9 pad_maximum_fusion.8.refs_15_
  201.2 108.8 %shard_map.383 = (f32[512,384]{1,0:T(8,128)}, f32[512,384]{1,0:T(8,128)}, f32[8,512]{1,0:T(8,128)}, f32[8,512]{1,0:T(8,128)}, bf16[512,384]{1,0:T(8,128)(2,1)}, ...) custom-call(bf16[1536,1536]{1,0:T(8,128)(2,1)} %get-tuple-element.12, ...), custom_call_target="tpu_custom_call" | custom-call | flops 10000000000 | bytes 41805824 | tf_op jit(solution)/shard_map/pallas_call | solution.py:668
  310.0 72.7 %shard_map.384 = (f32[256,1536]{1,0:T(8,128)}, f32[256,1536]{1,0:T(8,128)}, bf16[256,1536]{1,0:T(8,128)(2,1)}, bf16[256,1536]{1,0:T(8,128)(2,1)}, bf16[256,1536]...) custom-call(bf16[256,1536]{1,0:T(8,128)(2,1)} %get-tuple-element.137, ...), custom_call_target="tpu_custom_call" | custom-call | flops 60000002048 | bytes 19120128 | tf_op jit(solution)/shard_map/pallas_call | solution.py:668
  382.7 117.4 %shard_map.385 = (f32[256,1536]{1,0:T(8,128)}, f32[256,1536]{1,0:T(8,128)}, bf16[256,1536]{1,0:T(8,128)(2,1)}, bf16[256,1536]{1,0:T(8,128)(2,1)}, bf16[256,1536]...) custom-call(bf16[256,1536]{1,0:T(8,128)(2,1)} %get-tuple-element.152, ...), custom_call_target="tpu_custom_call" | custom-call | flops 40000000000 | bytes 30627840 | tf_op jit(solution)/shard_map/pallas_call | solution.py:668
  500.1 2.2 multiply_reduce_fusion.1
  502.4 0.6 broadcast_in_dim.112.refs_31_
  503.0 0.8 slice_reduce_fusion.2
  503.8 1.5 multiply_reduce_fusion
  505.3 0.6 broadcast_in_dim.113.refs_32_
  505.9 208.7 %shard_map.386 = (bf16[256,1536]{1,0:T(8,128)(2,1)}, f32[16,1536]{1,0:T(8,128)}, f32[8,384]{1,0:T(8,128)}, f32[8,1536]{1,0:T(8,128)}, f32[192,128]{1,0:T(8,128)}...) custom-call(bf16[256,1536]{1,0:T(8,128)(2,1)} %get-tuple-element.176, ...), custom_call_target="tpu_custom_call" | custom-call | flops 49999998976 | bytes 20721664 | tf_op jit(solution)/shard_map/pallas_call | solution.py:668
  714.6 1.4 fusion.14
  716.0 0.2 copy-done.7
  716.3 1.0 copy-done.5
  717.4 1.3 fusion
  718.7 1.3 pad_maximum_fusion.2
  720.1 0.5 copy-done.6
  720.6 1.0 slice_bitcast_fusion
  721.6 0.9 fusion.16
  722.5 0.8 slice_bitcast_fusion.1
  723.3 0.7 copy.97
  724.0 0.8 slice_reduce_fusion
  724.8 0.7 copy.96
  725.6 0.7 copy.100
  726.3 0.7 copy.101
  726.9 0.7 copy.98
  727.6 0.7 copy.99
  728.2 0.9 copy.108
  729.1 0.7 copy.109
  (102 shorter events, 1.5 us)
Async XLA Ops:
  4.1 1.6 copy-start
  5.8 1.5 copy-start.1
  7.4 1.2 copy-start.16
  7.4 1.2 copy-start.17
  7.4 1.4 copy-start.18
  7.5 1.6 copy-start.19
  7.5 1.7 copy-start.20
  8.6 1.0 copy-start.21
  8.6 1.1 copy-start.22
  8.6 1.2 copy-start.23
  9.7 1.2 copy-start.28
  9.7 1.2 copy-start.29
  9.7 1.3 copy-start.30
  9.7 1.3 copy-start.31
  9.7 1.3 copy-start.27
  9.7 1.3 copy-start.32
  9.7 1.3 copy-start.33
  9.8 2.1 copy-start.26
  382.6 117.4 %copy-start.9 = (bf16[256,1536]{1,0:T(8,128)(2,1)S(1)}, bf16[256,1536]{1,0:T(8,128)(2,1)}, u32[]{:S(2)}) copy-start(bf16[256,1536]{1,0:T(8,128)(2,1)} %get-tuple-element.202) | copy-start | bytes 2359300
  382.7 117.4 %copy-start.10 = (bf16[256,1536]{1,0:T(8,128)(2,1)S(1)}, bf16[256,1536]{1,0:T(8,128)(2,1)}, u32[]{:S(2)}) copy-start(bf16[256,1536]{1,0:T(8,128)(2,1)} %get-tuple-element.203) | copy-start | bytes 2359300
  382.7 117.4 %copy-start.11 = (bf16[256,1536]{1,0:T(8,128)(2,1)S(1)}, bf16[256,1536]{1,0:T(8,128)(2,1)}, u32[]{:S(2)}) copy-start(bf16[256,1536]{1,0:T(8,128)(2,1)} %get-tuple-element.204) | copy-start | bytes 2359300
  500.1 3.7 copy-start.2
  500.1 3.7 copy-start.3
  500.1 3.7 copy-start.4
  500.1 3.7 copy-start.8
  714.6 1.6 copy-start.7
  716.0 1.3 copy-start.5
  718.7 1.8 copy-start.6
  720.1 1.5 copy-start.14
  720.6 1.9 copy-start.13
  721.6 1.7 copy-start.24
  721.6 3.2 copy-start.25
  721.6 6.6 copy-start.12
  722.5 6.7 copy-start.15

commit v6 on v5

--- a/solution.py
+++ b/solution.py
@@ -1321,12 +1321,13 @@
         loads = [pltpu.make_async_copy(f[j], w.at[j], local.at[j]) for j in range(3)]
         places = (dpre.at[0], dpre.at[1], act.at[0], act.at[1])
         loads += [pltpu.make_async_copy(early[j], places[j], local.at[3 + j]) for j in range(4)]
-        for copy in loads:
-            copy.start()
+        loads[2].start()
         greet(n_dp)
         z = [i["z0"], i["z1"], i["z2"], i["z3"]]
         ds = [i["d0"], i["d1"], i["d2"], i["d3"]]
         loads[2].wait()
+        for copy in (*loads[:2], *loads[3:]):
+            copy.start()
         for p in range(4):
             dpre[2, p * quarter : (p + 1) * quarter] = dot_nn(ds[p][...], w[2, :, HC:]).astype(BF)
 

time: 739 us -> 737 us (level)
  no operation moved by 1% of the time
where the time goes in v6:
time: 737 us; the launch traced here: 729 us
  Pallas kernels  693 us (94%)
  local copies, waits for them, and re-layouts  22 us (3%)
  other arithmetic  12.4 us (2%)
    pallas_call x5, Pallas kernels, run_remote(): pl.pallas_call(body, out_shape=(*outs.values(), *far_outs.values()), in_s...  693 us

profile of v6, /device:TPU:0, one launch (start us, length us, event | category | flops | bytes accessed | tf_op | source)
XLA Modules:
  0.0 729.2 jit_solution(17792118570007330930)
XLA Ops:
  0.7 0.7 constant_dynamic-slice_fusion.3
  1.5 1.0 fusion.1
  2.5 0.2 broadcast_in_dim.105
  2.7 0.4 sin.8
  3.1 0.2 copy.91
  3.3 0.8 broadcast_multiply_fusion.refs_4_.refs_30_
  4.1 0.2 broadcast_in_dim.104
  4.3 0.4 cos.6
  4.7 1.0 copy.93.refs_3_.refs_29_
  5.9 1.4 copy-done.1
  7.5 1.1 pad_maximum_fusion.6
  8.7 0.2 copy-done.18
  8.9 0.2 copy-done.19
  9.2 0.4 copy-done.21
  9.8 1.1 pad_maximum_fusion.4
  11.2 0.6 pad_bitcast_fusion.refs_5_
  11.9 0.6 copy.104
  12.5 186.0 %shard_map.382 = (bf16[1536,1536]{1,0:T(8,128)(2,1)}, bf16[1536,1536]{1,0:T(8,128)(2,1)}, bf16[256,1536]{1,0:T(8,128)(2,1)}, bf16[128,1536]{1,0:T(8,128)(2,1)}, ...) custom-call(bf16[256,1536]{1,0:T(8,128)(2,1)} %refs_28_.1, ...), custom_call_target="tpu_custom_call" | custom-call | flops 20000000000 | bytes 39415808 | tf_op jit(solution)/shard_map/pallas_call | solution.py:668
  199.4 0.2 copy.94
  199.6 0.7 broadcast_select_fusion.refs_12_.refs_33_
  200.3 0.9 pad_maximum_fusion.8.refs_15_
  201.2 108.8 %shard_map.383 = (f32[512,384]{1,0:T(8,128)}, f32[512,384]{1,0:T(8,128)}, f32[8,512]{1,0:T(8,128)}, f32[8,512]{1,0:T(8,128)}, bf16[512,384]{1,0:T(8,128)(2,1)}, ...) custom-call(bf16[1536,1536]{1,0:T(8,128)(2,1)} %get-tuple-element.12, ...), custom_call_target="tpu_custom_call" | custom-call | flops 10000000000 | bytes 41805824 | tf_op jit(solution)/shard_map/pallas_call | solution.py:668
  310.0 71.8 %shard_map.384 = (f32[256,1536]{1,0:T(8,128)}, f32[256,1536]{1,0:T(8,128)}, bf16[256,1536]{1,0:T(8,128)(2,1)}, bf16[256,1536]{1,0:T(8,128)(2,1)}, bf16[256,1536]...) custom-call(bf16[256,1536]{1,0:T(8,128)(2,1)} %get-tuple-element.137, ...), custom_call_target="tpu_custom_call" | custom-call | flops 60000002048 | bytes 19120128 | tf_op jit(solution)/shard_map/pallas_call | solution.py:668
  381.8 116.9 %shard_map.385 = (f32[256,1536]{1,0:T(8,128)}, f32[256,1536]{1,0:T(8,128)}, bf16[256,1536]{1,0:T(8,128)(2,1)}, bf16[256,1536]{1,0:T(8,128)(2,1)}, bf16[256,1536]...) custom-call(bf16[256,1536]{1,0:T(8,128)(2,1)} %get-tuple-element.152, ...), custom_call_target="tpu_custom_call" | custom-call | flops 40000000000 | bytes 30627840 | tf_op jit(solution)/shard_map/pallas_call | solution.py:668
  498.7 2.2 multiply_reduce_fusion.1
  500.9 0.6 broadcast_in_dim.112.refs_31_
  501.5 0.8 slice_reduce_fusion.2
  502.4 1.5 multiply_reduce_fusion
  503.8 0.6 broadcast_in_dim.113.refs_32_
  504.4 209.2 %shard_map.386 = (bf16[256,1536]{1,0:T(8,128)(2,1)}, f32[16,1536]{1,0:T(8,128)}, f32[8,384]{1,0:T(8,128)}, f32[8,1536]{1,0:T(8,128)}, f32[192,128]{1,0:T(8,128)}...) custom-call(bf16[256,1536]{1,0:T(8,128)(2,1)} %get-tuple-element.176, ...), custom_call_target="tpu_custom_call" | custom-call | flops 49999998976 | bytes 20721664 | tf_op jit(solution)/shard_map/pallas_call | solution.py:668
  713.7 1.4 fusion.14
  715.1 0.2 copy-done.7
  715.4 1.0 copy-done.5
  716.5 1.3 fusion
  717.8 1.3 pad_maximum_fusion.2
  719.1 0.5 copy-done.6
  719.6 1.0 slice_bitcast_fusion
  720.7 0.9 fusion.16
  721.5 0.8 slice_bitcast_fusion.1
  722.4 0.7 copy.97
  723.1 0.8 slice_reduce_fusion
  723.9 0.7 copy.96
  724.7 0.7 copy.100
  725.3 0.7 copy.101
  726.0 0.7 copy.98
  726.6 0.7 copy.99
  727.3 0.9 copy.108
  728.2 0.7 copy.109
  (102 shorter events, 1.5 us)
Async XLA Ops:
  4.1 1.6 copy-start
  5.8 1.5 copy-start.1
  7.4 1.2 copy-start.16
  7.4 1.2 copy-start.17
  7.4 1.4 copy-start.18
  7.5 1.6 copy-start.19
  7.5 1.7 copy-start.20
  8.6 1.0 copy-start.21
  8.6 1.1 copy-start.22
  8.6 1.2 copy-start.23
  9.7 1.2 copy-start.28
  9.7 1.2 copy-start.29
  9.7 1.3 copy-start.30
  9.7 1.3 copy-start.31
  9.7 1.3 copy-start.27
  9.7 1.3 copy-start.32
  9.7 1.3 copy-start.33
  9.8 2.1 copy-start.26
  381.7 116.9 %copy-start.9 = (bf16[256,1536]{1,0:T(8,128)(2,1)S(1)}, bf16[256,1536]{1,0:T(8,128)(2,1)}, u32[]{:S(2)}) copy-start(bf16[256,1536]{1,0:T(8,128)(2,1)} %get-tuple-element.202) | copy-start | bytes 2359300
  381.7 116.9 %copy-start.10 = (bf16[256,1536]{1,0:T(8,128)(2,1)S(1)}, bf16[256,1536]{1,0:T(8,128)(2,1)}, u32[]{:S(2)}) copy-start(bf16[256,1536]{1,0:T(8,128)(2,1)} %get-tuple-element.203) | copy-start | bytes 2359300
  381.7 116.9 %copy-start.11 = (bf16[256,1536]{1,0:T(8,128)(2,1)S(1)}, bf16[256,1536]{1,0:T(8,128)(2,1)}, u32[]{:S(2)}) copy-start(bf16[256,1536]{1,0:T(8,128)(2,1)} %get-tuple-element.204) | copy-start | bytes 2359300
  498.7 3.7 copy-start.2
  498.7 3.7 copy-start.3
  498.7 3.7 copy-start.4
  498.7 3.7 copy-start.8
  713.6 1.6 copy-start.7
  715.1 1.3 copy-start.5
  717.8 1.8 copy-start.6
  719.1 1.5 copy-start.14
  719.6 1.9 copy-start.13
  720.6 1.7 copy-start.24
  720.7 3.2 copy-start.25
  720.7 6.6 copy-start.12
  721.5 6.7 copy-start.15
